TPU v7x, 32 devices: a whole 2x2x4 slice. The times are simulated.
32 devices in a mesh: branch: 2 (over core), group: 2 (over y), seq: 8 (over z, x).
Axes of the slice: x: 2, y: 2, z: 4, core: 2. Of those that a mesh axis runs over, the one named last changes fastest.
Arguments:
- query_rows: bfloat16 [2, 2560, 4096], P('branch', ('group', 'seq')), parts along dimension 1, may hold values from -10 to 10
- key_rows: bfloat16 [2, 2560, 4096], P('branch', ('group', 'seq')), parts along dimension 1, may hold values from -9 to 9
- value_rows: bfloat16 [2, 2560, 4096], P('branch', ('group', 'seq')), parts along dimension 1, may hold values from -80 to 80
- residual: bfloat16 [2560, 2560], P(('group', 'seq')), parts along dimension 0, may hold values from -6 to 6
- control_mask: int32 [2560], P(('group', 'seq')), parts along dimension 0, may hold values 0 or 1
- step_index: int32 [2], P('group'), parts along dimension 0, may hold values from 0 to 49
- step_gates: float32 [50, 2560], replicated, may hold values from 0.1 to 1.9
- out_weight: bfloat16 [2, 4096, 2560], P('branch', None, 'seq'), may hold values from -0.109375 to 0.109375
Outputs:
- block_out: bfloat16 [2, 2560, 2560], P('branch', ('group', 'seq')), parts along dimension 1
There are 2 independent parts, one for each index of `group`. A program takes and returns all parts, laid end to end along the dimension named above; an argument that names none is the same for every part. Nothing has to cross between parts.
All inputs are finite; a program needn't handle non-finite values. No bound on the sum of `control_mask` on one device may be relied on, other than what follows from the above.
Results may differ from a plain program's by a relative error of at most 0.007.
Values may be sent and summed in bfloat16 or wider, within the bound.
No kernel may reach another device: no remote copies, remote signals or barrier semaphores. Data moves between devices by JAX's collectives and lax.ppermute only.
A program may use at most 128 MiB of HBM per device.

v0:
```python
import math

import jax
import jax.numpy as jnp
from jax import lax
from jax.sharding import PartitionSpec as P

HEADS = 32


def shifted(value, axis, steps):
    count = lax.axis_size(axis)
    leading, last = (max(0, -steps), min(count, count - steps))
    return lax.ppermute(value, axis, [(source, source + steps) for source in range(leading, last)])


def attend(exchanged):
    query_all, key_all, value_all = exchanged
    query_local = query_all[:, 0]
    key_local = key_all[:, 0]
    value_local = value_all[:, 0]
    total_rows = query_local.shape[0]
    count_heads = query_local.shape[1]
    head_size = query_local.shape[2]
    score_scale = float(head_size) ** (-0.5)
    block_rows = math.gcd(total_rows, 512)
    query_blocks = query_local.reshape(total_rows // block_rows, block_rows, count_heads, head_size)

    def one_block(query_block):
        scores = (
            jnp.einsum("qhd,khd->hqk", query_block, key_local, preferred_element_type=jnp.float32)
            * score_scale
        )
        peak = jnp.max(scores, axis=2, keepdims=True)
        expo = jnp.exp(scores - peak)
        total_sum = jnp.sum(expo, axis=2, keepdims=True)
        probs = expo.astype(jnp.bfloat16)
        attended = jnp.einsum(
            "hqk,khd->qhd", probs, value_local, preferred_element_type=jnp.float32
        )
        attended = attended / jnp.swapaxes(total_sum, 0, 1)
        return attended.astype(jnp.bfloat16)

    result = lax.map(one_block, query_blocks)
    return result.reshape(total_rows, count_heads, head_size)[:, None]


def per_device(
    query_rows, key_rows, value_rows, residual, control_mask, step_index, step_gates, out_weight
):
    tok_rows = query_rows.shape[1]
    groups = lax.axis_size("seq")
    per_group = HEADS // groups
    head_size = query_rows.shape[2] // HEADS
    query_split = query_rows[0].reshape(tok_rows, groups, per_group, head_size)
    key_split = key_rows[0].reshape(tok_rows, groups, per_group, head_size)
    value_split = value_rows[0].reshape(tok_rows, groups, per_group, head_size)
    head_major = attend(
        (
            lax.all_to_all(query_split, "seq", split_axis=1, concat_axis=0, tiled=True),
            lax.all_to_all(key_split, "seq", split_axis=1, concat_axis=0, tiled=True),
            lax.all_to_all(value_split, "seq", split_axis=1, concat_axis=0, tiled=True),
        )
    )
    weight_local = out_weight[0]
    token_major = lax.all_to_all(head_major, "seq", split_axis=0, concat_axis=1, tiled=True)
    token_flat = token_major.reshape(tok_rows, groups * per_group * head_size)
    projected = jnp.dot(
        token_flat,
        lax.all_gather(weight_local, "seq", axis=1, tiled=True),
        preferred_element_type=jnp.float32,
    )
    hint_local = jnp.where(control_mask[:, None] == 1, projected, jnp.zeros_like(projected)).astype(
        jnp.bfloat16
    )
    hint_moved = shifted(hint_local, "branch", 1)
    step_ids = lax.broadcasted_iota(jnp.int32, (step_gates.shape[0], 1), 0)
    gate_row = jnp.sum(
        jnp.where(step_ids == step_index[0], step_gates, jnp.zeros_like(step_gates)), axis=0
    )
    mixed_out = (
        residual.astype(jnp.float32)
        + gate_row[None, :] * projected
        + hint_moved.astype(jnp.float32)
    )
    is_main = lax.axis_index("branch") == 1
    chosen_out = jnp.where(is_main, mixed_out.astype(jnp.bfloat16), hint_local)
    return chosen_out[None]


def solution(mesh):
    placed = (
        P("branch", ("group", "seq"), None),
        P("branch", ("group", "seq"), None),
        P("branch", ("group", "seq"), None),
        P(("group", "seq"), None),
        P(("group", "seq")),
        P("group"),
        P(),
        P("branch", None, "seq"),
    )
    return jax.shard_map(
        per_device,
        mesh=mesh,
        in_specs=placed,
        out_specs=P("branch", ("group", "seq"), None),
        check_vma=False,
    )
```

profile of v0, /device:TPU:0, one launch (start us, length us, event | category | flops | bytes accessed | tf_op | source)
XLA Modules:
  0.0 494.0 jit_solution(9320915909612465745)
XLA Ops:
  8.8 1.6 copy.30
  10.4 7.3 %all-to-all-start.1 = ((bf16[160,8,4,128]{3,0,2,1:T(8,128)(2,1)}), bf16[160,8,4,128]{3,0,2,1:T(8,128)(2,1)S(1)}, u32[]{:S(2)}, u32[]{:S(2)}) async-start(bf16[160,8,4,128]{3,0,2,1:T(8,128)(2,1)} %copy.30), calls=%async_computation.1 | async-start | bytes 2621440 | tf_op jit(solution)/shard_map/all_to_all | solution.py:61
  17.6 3.3 reshape_squeeze.15
  20.9 1.6 copy.32
  22.6 40.9 %all-to-all-done.1 = bf16[160,8,4,128]{3,0,2,1:T(8,128)(2,1)S(1)} async-done(((bf16[160,8,4,128]{3,0,2,1:T(8,128)(2,1)}), bf16[160,8,4,128]{3,0,2,1:T(8,128)(2,1)S(1)}, u32[]{:S(2)}, u32[]{:S(2)}) %all-to-all-start.1) | async-done | bytes 1310752 | tf_op jit(solution)/shard_map/all_to_all | solution.py:61
  63.5 23.5 %all-to-all-start.2 = ((bf16[160,8,4,128]{3,0,2,1:T(8,128)(2,1)}), bf16[160,8,4,128]{3,0,2,1:T(8,128)(2,1)S(1)}, u32[]{:S(2)}, u32[]{:S(2)}) async-start(bf16[160,8,4,128]{3,0,2,1:T(8,128)(2,1)} %copy.32), calls=%async_computation.2 | async-start | bytes 2621440 | tf_op jit(solution)/shard_map/all_to_all | solution.py:62
  86.9 4.1 reshape_squeeze.12
  91.1 2.8 copy.28
  93.9 28.7 %all-to-all-done.2 = bf16[160,8,4,128]{3,0,2,1:T(8,128)(2,1)S(1)} async-done(((bf16[160,8,4,128]{3,0,2,1:T(8,128)(2,1)}), bf16[160,8,4,128]{3,0,2,1:T(8,128)(2,1)S(1)}, u32[]{:S(2)}, u32[]{:S(2)}) %all-to-all-start.2) | async-done | bytes 1310752 | tf_op jit(solution)/shard_map/all_to_all | solution.py:62
  123.7 16.4 %all-to-all-start = ((bf16[160,8,4,128]{3,2,0,1:T(4,128)(2,1)}), bf16[160,8,4,128]{3,2,0,1:T(4,128)(2,1)}, u32[]{:S(2)}, u32[]{:S(2)}) async-start(bf16[160,8,4,128]{3,2,0,1:T(4,128)(2,1)} %copy.28), calls=%async_computation | async-start | bytes 2621440 | tf_op jit(solution)/shard_map/all_to_all | solution.py:60
  142.7 43.6 %all-to-all-done = bf16[160,8,4,128]{3,2,0,1:T(4,128)(2,1)} async-done(((bf16[160,8,4,128]{3,2,0,1:T(4,128)(2,1)}), bf16[160,8,4,128]{3,2,0,1:T(4,128)(2,1)}, u32[]{:S(2)}, u32[]{:S(2)}) %all-to-all-start) | async-done | bytes 1310752 | tf_op jit(solution)/shard_map/all_to_all | solution.py:60
  187.8 20.9 %while.10 = (s32[]{:T(128)}, bf16[5,256,4,128]{3,1,0,2:T(8,128)(2,1)}, bf16[5,256,4,128]{3,1,0,2:T(8,128)(2,1)S(1)}, bf16[1280,4,128]{2,0,1:T(8,128)(2,1)S(1)}, bf16[1280,4,128]{2,0,1:T(8,128)(2,1)}, /*index=5*/s32[]{:T(128)}) while((s32[]{:T(128)}, bf16[5,256,4,128]{3,1,0,2:T(8,128)(2,1)}, bf16[5,256,4,128]{3,1,0,2:T(8,128)(2,1)S(1)}, ...), condition=%wide.region_4.5_spmd, body=%wide.region_1.4_spmd.sunk | while | flops 681834496 | bytes 24138340 | solution.py:44
  190.0 1.9 fusion.42
  194.2 1.9 fusion.42
  198.4 1.9 fusion.42
  202.6 1.9 fusion.42
  206.8 1.9 fusion.42
  208.7 7.4 %copy.36 = bf16[1280,1,4,128]{3,2,1,0:T(4,128)(2,1)} copy(bf16[1280,1,4,128]{3,0,2,1:T(8,128)(2,1)} %bitcast.16) | data formatting | bytes 2621440 | tf_op jit(solution)/shard_map/broadcast_in_dim;reshape | solution.py:45
  216.1 3.9 all-to-all-start.3
  220.0 36.2 %all-to-all-done.3 = bf16[1280,1,4,128]{3,2,1,0:T(4,128)(2,1)S(1)} async-done(((bf16[1280,1,4,128]{3,2,1,0:T(4,128)(2,1)}), bf16[1280,1,4,128]{3,2,1,0:T(4,128)(2,1)S(1)}, u32[]{:S(2)}, u32[]{:S(2)}) %all-to-all-start.3) | async-done | bytes 1310752 | tf_op jit(solution)/shard_map/all_to_all | solution.py:66
  256.6 1.8 reshape.16
  258.4 211.2 %all-gather.3.cloned.1.call-done = bf16[1,4096,2560]{1,2,0:T(8,128)(2,1)} async-done(((bf16[1,4096,320]{1,2,0:T(8,128)(2,1)}), bf16[1,4096,2560]{1,2,0:T(8,128)(2,1)}) %all-gather.3.cloned.1.call-update) | async-done | bytes 20971536 | tf_op jit(solution)/shard_map/all_gather | solution.py:70
  469.6 12.3 %select_convert_fusion = (bf16[160,2560]{1,0:T(8,128)(2,1)}, f32[160,2560]{1,0:T(8,128)S(1)}) fusion(pred[160]{0:T(512)(128)(4,1)S(1)} %broadcast_compare_fusion, bf16[160,4096]{1,0:T(8,128)(2,1)} %reshape.16, bf16[1,4096,2560]{1,2,0:T(8,128)(2,1)} %all-gather.3.cloned.1.call-done), kind=kOutput, calls=%fused_computation.20 | convolution fusion | flops 3355852800 | bytes 24740000 | tf_op jit(solution)/shard_map/dot_general | solution.py:68
  481.9 1.8 collective-permute-start
  (43 shorter events, 21.8 us)
Async XLA Ops:
  6.5 1.3 copy-start.2
  6.5 463.0 %all-gather.3.cloned.1.call-start = ((), (), s32[]{:S(2)}) async-start(), calls=%async_computation.4 | async-start | bytes 23592960 | tf_op jit(solution)/shard_map/all_gather | solution.py:70
  10.4 53.1 %all-to-all-start.1 = ((bf16[160,8,4,128]{3,0,2,1:T(8,128)(2,1)}), bf16[160,8,4,128]{3,0,2,1:T(8,128)(2,1)S(1)}, u32[]{:S(2)}, u32[]{:S(2)}) async-start(bf16[160,8,4,128]{3,0,2,1:T(8,128)(2,1)} %copy.30), calls=%async_computation.1 | async-start | bytes 2621440 | tf_op jit(solution)/shard_map/all_to_all | solution.py:61
  63.5 59.2 %all-to-all-start.2 = ((bf16[160,8,4,128]{3,0,2,1:T(8,128)(2,1)}), bf16[160,8,4,128]{3,0,2,1:T(8,128)(2,1)S(1)}, u32[]{:S(2)}, u32[]{:S(2)}) async-start(bf16[160,8,4,128]{3,0,2,1:T(8,128)(2,1)} %copy.32), calls=%async_computation.2 | async-start | bytes 2621440 | tf_op jit(solution)/shard_map/all_to_all | solution.py:62
  122.6 1.1 copy-start
  123.7 62.6 %all-to-all-start = ((bf16[160,8,4,128]{3,2,0,1:T(4,128)(2,1)}), bf16[160,8,4,128]{3,2,0,1:T(4,128)(2,1)}, u32[]{:S(2)}, u32[]{:S(2)}) async-start(bf16[160,8,4,128]{3,2,0,1:T(4,128)(2,1)} %copy.28), calls=%async_computation | async-start | bytes 2621440 | tf_op jit(solution)/shard_map/all_to_all | solution.py:60
  140.1 1.3 copy-start.1
  188.7 1.3 copy-start.3
  192.9 1.3 copy-start.3
  197.1 1.3 copy-start.3
  201.3 1.3 copy-start.3
  205.5 1.3 copy-start.3
  216.1 3.9 copy-start.5
  216.1 40.1 %all-to-all-start.3 = ((bf16[1280,1,4,128]{3,2,1,0:T(4,128)(2,1)}), bf16[1280,1,4,128]{3,2,1,0:T(4,128)(2,1)S(1)}, u32[]{:S(2)}, u32[]{:S(2)}) async-start(bf16[1280,1,4,128]{3,2,1,0:T(4,128)(2,1)} %copy.36), calls=%async_computation.3 | async-start | bytes 2621440 | tf_op jit(solution)/shard_map/all_to_all | solution.py:66
  258.4 227.4 %copy-start.4 = (bf16[160,2560]{1,0:T(8,128)(2,1)S(1)}, bf16[160,2560]{1,0:T(8,128)(2,1)}, u32[]{:S(2)}) copy-start(bf16[160,2560]{1,0:T(8,128)(2,1)} %param.13) | copy-start | bytes 2457604
  481.9 3.9 collective-permute-start
Sparse Core Ops, SparseCore 0:
  8.9 460.6 all-gather.2
where the time goes:
time: 495 us; the launch traced here: 494 us
  waiting for transfers between devices  362 us (73%)
  starting transfers between devices  52.8 us (11%)
  local copies, waits for them, and re-layouts  31.2 us (6%)
  matrix products  26.6 us (5%)
  between operations  14.1 us (3%)
  other arithmetic  7.72 us (2%)
    all_gather x1, waiting for transfers between devices, per_device(): lax.all_gather(weight_local, 'seq', axis=1, tiled=True)  211 us
    all_to_all x1, waiting for transfers between devices, per_device(): lax.all_to_all(query_split, 'seq', split_axis=1, concat_axis=0, tiled=True)  43.6 us
    all_to_all x1, waiting for transfers between devices, per_device(): lax.all_to_all(key_split, 'seq', split_axis=1, concat_axis=0, tiled=True)  40.9 us
    all_to_all x1, waiting for transfers between devices, per_device(): lax.all_to_all(head_major, 'seq', split_axis=0, concat_axis=1, tiled=True)  36.2 us
    all_to_all x1, waiting for transfers between devices, per_device(): lax.all_to_all(value_split, 'seq', split_axis=1, concat_axis=0, tiled=True)  28.7 us
    all_to_all x1, starting transfers between devices, per_device(): lax.all_to_all(value_split, 'seq', split_axis=1, concat_axis=0, tiled=True)  23.5 us
    all_to_all x1, starting transfers between devices, per_device(): lax.all_to_all(query_split, 'seq', split_axis=1, concat_axis=0, tiled=True)  16.4 us
    dot_general x1, matrix products, per_device(): jnp.dot(token_flat, lax.all_gather(weight_local, 'seq', axis=1, tiled=Tru...  12.3 us
  transfers between devices with their start and end apart: 6, of which 6 were waited for; matrix products, arithmetic and copies ran while one was open for 10% of the time, Pallas kernels for 0%

commit v1 on v0

v1 whole, which is shorter than its diff:
```python
import math

import jax
import jax.numpy as jnp
from jax import lax
from jax.experimental import pallas as pl
from jax.experimental.pallas import tpu as pltpu
from jax.sharding import PartitionSpec as P

HEADS = 32
CHUNKS = 2


def attend_project(queries, keys_near, keys_far, values_near, values_far, weight, block_rows, head_size):
    total_rows, features = queries.shape
    count_heads = features // head_size
    near_rows = keys_near.shape[0]
    far_rows = keys_far.shape[0]
    columns = weight.shape[1]
    scale = float(head_size) ** (-0.5) * math.log2(math.e)

    def body(q_ref, kn_ref, kf_ref, vn_ref, vf_ref, w_ref, out_ref, attended):
        head = pl.program_id(1)
        query = q_ref[...]
        contract = (((1,), (1,)), ((), ()))
        near = lax.dot_general(query, kn_ref[...], contract, preferred_element_type=jnp.float32)
        far = lax.dot_general(query, kf_ref[...], contract, preferred_element_type=jnp.float32)
        peak = jnp.maximum(
            jnp.max(near, axis=1, keepdims=True), jnp.max(far, axis=1, keepdims=True)
        )
        near = jnp.exp2((near - peak) * scale)
        far = jnp.exp2((far - peak) * scale)
        total = jnp.sum(near, axis=1, keepdims=True) + jnp.sum(far, axis=1, keepdims=True)
        mixed = jnp.dot(near.astype(jnp.bfloat16), vn_ref[...], preferred_element_type=jnp.float32)
        mixed += jnp.dot(far.astype(jnp.bfloat16), vf_ref[...], preferred_element_type=jnp.float32)
        mixed = (mixed / total).astype(jnp.bfloat16)
        for index in range(count_heads):

            @pl.when(head == index)
            def _():
                attended[:, index * head_size : (index + 1) * head_size] = mixed

        @pl.when(head == count_heads - 1)
        def _():
            out_ref[...] = jnp.dot(
                attended[...], w_ref[...], preferred_element_type=jnp.float32
            ).astype(out_ref.dtype)

    def key_spec(rows):
        return pl.BlockSpec((rows, head_size), lambda block, head: (0, head))

    return pl.pallas_call(
        body,
        grid=(total_rows // block_rows, count_heads),
        in_specs=[
            pl.BlockSpec((block_rows, head_size), lambda block, head: (block, head)),
            key_spec(near_rows),
            key_spec(far_rows),
            key_spec(near_rows),
            key_spec(far_rows),
            pl.BlockSpec((features, columns), lambda block, head: (0, 0)),
        ],
        out_specs=pl.BlockSpec((block_rows, columns), lambda block, head: (block, 0)),
        out_shape=jax.ShapeDtypeStruct((total_rows, columns), jnp.bfloat16),
        scratch_shapes=[pltpu.VMEM((block_rows, features), jnp.bfloat16)],
        compiler_params=pltpu.CompilerParams(vmem_limit_bytes=48 * 1024 * 1024),
        cost_estimate=pl.CostEstimate(
            flops=4 * total_rows * (near_rows + far_rows) * features + 2 * total_rows * features * columns,
            bytes_accessed=2 * (2 * (near_rows + far_rows) * features + features * columns),
            transcendentals=total_rows * (near_rows + far_rows) * count_heads,
        ),
    )(queries, keys_near, keys_far, values_near, values_far, weight)


def per_device(
    query_rows, key_rows, value_rows, residual, control_mask, step_index, step_gates, out_weight
):
    query, key, value, weight = query_rows[0], key_rows[0], value_rows[0], out_weight[0]
    rows, all_features = query.shape
    head_size = all_features // HEADS
    count = lax.axis_size("seq")
    half = count // 2
    shares = lax.axis_size("group")
    features = all_features // half
    columns = weight.shape[1]
    branch = lax.axis_index("branch")
    group = lax.axis_index("group")
    place = lax.axis_index("seq")
    spot = place % half
    pair = ("branch", "seq")

    def crossing(step):
        return [
            (b * count + h * half + r, h * count + b * half + (r ^ step))
            for b in range(2)
            for h in range(2)
            for r in range(half)
        ]

    def sibling(array):
        return lax.ppermute(array, "branch", [(0, 1), (1, 0)])

    def scatter_columns(array):
        parts = []
        for step in range(half):
            part = lax.dynamic_slice_in_dim(array, (spot ^ step) * features, features, axis=1)
            parts.append(lax.ppermute(part, pair, crossing(step)))
        return jnp.concatenate(parts, axis=0)

    share_rows = features // shares
    parts = []
    for step in range(half):
        start = (spot ^ step) * features + group * share_rows
        part = lax.dynamic_slice_in_dim(weight, start, share_rows, axis=0)
        parts.append(lax.ppermute(part, pair, crossing(step)))
    own = jnp.stack(parts)
    blocks = own
    if shares == 2:
        other = lax.ppermute(own, "group", [(0, 1), (1, 0)])
        blocks = jnp.where(
            group == 0,
            jnp.concatenate([own, other], axis=1),
            jnp.concatenate([other, own], axis=1),
        )
    far_blocks = sibling(blocks)
    both = jnp.concatenate([blocks, far_blocks], axis=0)
    ordered = []
    for block in range(count):
        step = (block % half) ^ spot
        where = jnp.where(branch == block // half, step, half + step)
        ordered.append(lax.dynamic_index_in_dim(both, where, 0, keepdims=False))
    weight_rows = jnp.concatenate(ordered, axis=1)

    key_near = scatter_columns(key)
    key_far = sibling(key_near)
    value_near = scatter_columns(value)
    value_far = sibling(value_near)

    step_ids = lax.broadcasted_iota(jnp.int32, (step_gates.shape[0], 1), 0)
    gate_row = jnp.sum(
        jnp.where(step_ids == step_index[0], step_gates, jnp.zeros_like(step_gates)), axis=0
    )
    is_main = branch == 1
    chunk_rows = rows // CHUNKS
    outs = []
    for chunk in range(CHUNKS):
        piece = slice(chunk * chunk_rows, (chunk + 1) * chunk_rows)
        queries = scatter_columns(query[piece])
        partial = attend_project(
            queries,
            key_near,
            key_far,
            value_near,
            value_far,
            weight_rows,
            math.gcd(half, 4) * chunk_rows,
            head_size,
        ).reshape(half, chunk_rows, count * columns)
        summed = partial[0].astype(jnp.float32)
        for step in range(1, half):
            swap = [(s, s ^ step) for s in range(count)]
            summed = summed + lax.ppermute(partial[step], "seq", swap).astype(jnp.float32)
        projected = lax.ppermute(summed.astype(jnp.bfloat16), pair, crossing(0))
        hint = jnp.where(control_mask[piece, None] == 1, projected, jnp.zeros_like(projected))
        hint_moved = lax.ppermute(hint, "branch", [(0, 1)])
        mixed = (
            residual[piece].astype(jnp.float32)
            + gate_row[None, :] * projected.astype(jnp.float32)
            + hint_moved.astype(jnp.float32)
        ).astype(jnp.bfloat16)
        outs.append(jnp.where(is_main, mixed, hint))
    return jnp.concatenate(outs, axis=0)[None]


def solution(mesh):
    placed = (
        P("branch", ("group", "seq"), None),
        P("branch", ("group", "seq"), None),
        P("branch", ("group", "seq"), None),
        P(("group", "seq"), None),
        P(("group", "seq")),
        P("group"),
        P(),
        P("branch", None, "seq"),
    )
    return jax.shard_map(
        per_device,
        mesh=mesh,
        in_specs=placed,
        out_specs=P("branch", ("group", "seq"), None),
        check_vma=False,
    )
```

time: 495 us -> 254 us (0.51)
  waiting for transfers between devices: 362 us -> 71.7 us
  starting transfers between devices: 52.8 us -> 93.3 us
  Pallas kernels: 0 us -> 28.2 us
  matrix products: 26.6 us -> 0 us
  between operations: 14.1 us -> 1.04 us
  other arithmetic: 7.72 us -> 17.7 us
  local copies, waits for them, and re-layouts: 31.2 us -> 40.5 us
    all_gather x1 -> x0, waiting for transfers between devices: 211 us -> none  [per_device(): lax.all_gather(weight_local, 'seq', axis=1, tiled=True)]
    all_to_all x4 -> x0, waiting for transfers between devices: 149 us -> none  [the longest x1 43.6 us: per_device(): lax.all_to_all(query_split, 'seq', split_axis=1, concat_axis=0, tiled=True)]
    ppermute x1 -> x34, starting transfers between devices: 1.78 us -> 93.3 us  [the longest x16 32.3 us: scatter_columns(): parts.append(lax.ppermute(part, pair, crossing(step)))]
    ppermute x1 -> x34, waiting for transfers between devices: 0.24 us -> 71.7 us  [the longest x16 24.1 us: scatter_columns(): parts.append(lax.ppermute(part, pair, crossing(step)))]
    all_to_all x4 -> x0, starting transfers between devices: 51 us -> none  [the longest x1 23.5 us: per_device(): lax.all_to_all(value_split, 'seq', split_axis=1, concat_axis=0, tiled=True)]
    pallas_call x0 -> x2, Pallas kernels: none -> 28.2 us  [attend_project(): pl.pallas_call(body, grid=(total_rows // block_rows, count_heads), in_spe...]
    dot_general x11 -> x0, matrix products: 26.6 us -> none  [the longest x1 12.3 us: per_device(): jnp.dot(token_flat, lax.all_gather(weight_local, 'seq', axis=1, tiled=Tru...]
    dynamic_slice x0 -> x13, local copies, waits for them, and re-layouts: none -> 22.3 us  [the longest x8 18.1 us: per_device(): ordered.append(lax.dynamic_index_in_dim(both, where, 0, keepdims=False))]
  transfers between devices with their start and end apart: 6 -> 34, of which waited for: 6 -> 15; matrix products, arithmetic and copies ran while one was open for 10% -> 20% of each run, Pallas kernels for 0% -> 6%
where the time goes in v1:
time: 254 us; the launch traced here: 252 us
  starting transfers between devices  93.3 us (37%)
  waiting for transfers between devices  71.7 us (28%)
  local copies, waits for them, and re-layouts  40.5 us (16%)
  Pallas kernels  28.2 us (11%)
  other arithmetic  17.7 us (7%)
    ppermute x16, starting transfers between devices, scatter_columns(): parts.append(lax.ppermute(part, pair, crossing(step)))  32.3 us
    pallas_call x2, Pallas kernels, attend_project(): pl.pallas_call(body, grid=(total_rows // block_rows, count_heads), in_spe...  28.2 us
    ppermute x3, starting transfers between devices, sibling(): return lax.ppermute(array, 'branch', [(0, 1), (1, 0)])  27.2 us
    ppermute x16, waiting for transfers between devices, scatter_columns(): parts.append(lax.ppermute(part, pair, crossing(step)))  24.1 us
    ppermute x6, waiting for transfers between devices, per_device(): lax.ppermute(partial[step], 'seq', swap).astype(jnp.float32)  19.5 us
    dynamic_slice x8, local copies, waits for them, and re-layouts, per_device(): ordered.append(lax.dynamic_index_in_dim(both, where, 0, keepdims=False))  18.1 us
    ppermute x2, starting transfers between devices, per_device(): hint_moved = lax.ppermute(hint, 'branch', [(0, 1)])  16.1 us
    ppermute x4, waiting for transfers between devices, per_device(): parts.append(lax.ppermute(part, pair, crossing(step)))  15 us
  transfers between devices with their start and end apart: 34, of which 15 were waited for; matrix products, arithmetic and copies ran while one was open for 20% of the time, Pallas kernels for 6%

profile of v1, /device:TPU:0, one launch (start us, length us, event | category | flops | bytes accessed | tf_op | source)
XLA Modules:
  0.0 252.4 jit_solution(11219503115620818525)
XLA Ops:
  2.2 3.0 %collective-permute-start.15 = (bf16[512,320]{0,1:T(8,128)(2,1)S(1)}, bf16[512,320]{0,1:T(8,128)(2,1)S(1)}, u32[]{:S(2)}, u32[]{:S(2)}) collective-permute-start(bf16[512,320]{0,1:T(8,128)(2,1)S(1)} %get-tuple-element.14), channel_id=1, source_target_pairs={{0,1},{1,0},{2,3},{3,2},{4,17},{5,16},{6,19},{7,18},{16,5},{17,4},... | collective-permute-start | bytes 983048 | tf_op jit(solution)/shard_map/ppermute | solution.py:115
  6.8 3.5 %collective-permute-done.15 = bf16[512,320]{0,1:T(8,128)(2,1)S(1)} collective-permute-done((bf16[512,320]{0,1:T(8,128)(2,1)S(1)}, bf16[512,320]{0,1:T(8,128)(2,1)S(1)}, u32[]{:S(2)}, u32[]{:S(2)}) %collective-permute-start.15) | collective-permute-done | bytes 327712 | tf_op jit(solution)/shard_map/ppermute | solution.py:115
  10.3 6.2 %collective-permute-done.16 = bf16[512,320]{0,1:T(8,128)(2,1)S(1)} collective-permute-done((bf16[512,320]{0,1:T(8,128)(2,1)S(1)}, bf16[512,320]{0,1:T(8,128)(2,1)S(1)}, u32[]{:S(2)}, u32[]{:S(2)}) %collective-permute-start.16) | collective-permute-done | bytes 327712 | tf_op jit(solution)/shard_map/ppermute | solution.py:115
  16.4 5.4 %collective-permute-done.17 = bf16[512,320]{0,1:T(8,128)(2,1)S(1)} collective-permute-done((bf16[512,320]{0,1:T(8,128)(2,1)S(1)}, bf16[512,320]{0,1:T(8,128)(2,1)S(1)}, u32[]{:S(2)}, u32[]{:S(2)}) %collective-permute-start.17) | collective-permute-done | bytes 327712 | tf_op jit(solution)/shard_map/ppermute | solution.py:115
  33.4 12.6 %collective-permute-done.18 = bf16[4,512,320]{1,2,0:T(8,128)(2,1)} collective-permute-done((bf16[4,512,320]{1,2,0:T(8,128)(2,1)S(1)}, bf16[4,512,320]{1,2,0:T(8,128)(2,1)}, u32[]{:S(2)}, u32[]{:S(2)}) %collective-permute-start.18) | collective-permute-done | bytes 1310752 | tf_op jit(solution)/shard_map/ppermute | solution.py:119
  46.0 3.3 %maximum_select_fusion = bf16[4,1024,320]{1,2,0:T(8,128)(2,1)} fusion(bf16[4,512,320]{1,2,0:T(8,128)(2,1)} %collective-permute-done.18, bf16[1,512,320]{1,2,0:T(8,128)(2,1)S(1)} %bitcast.71, bf16[1,512,320]{1,2,0:T(8,128)(2,1)S(1)} %bitcast.69, bf16[1,512,320]{1,2,0:T(8,128)(2,1)S(1)} %bitcast.67, bf16[1,512,320]{1,2,0:T(8,128)(2,1)S(1)} %bitcast.65, pred[]{:T(512)S(6)} %eq.40), kind=kLoop, calls=%fused_computation.16 | loop fusion | flops 27525120 | bytes 5242881 | tf_op jit(solution)/shard_map/jit(_where)/select_n | solution.py:120
  49.3 8.2 %collective-permute-start.19 = (bf16[4,1024,320]{1,2,0:T(8,128)(2,1)}, bf16[4,1024,320]{1,2,0:T(8,128)(2,1)}, u32[]{:S(2)}, u32[]{:S(2)}) collective-permute-start(bf16[4,1024,320]{1,2,0:T(8,128)(2,1)} %maximum_select_fusion), channel_id=1, source_target_pairs={{0,16},{16,0},{1,17},{17,1},{2,18},{18,2},{3,19},{19,3},{4,20},{20... | collective-permute-start | bytes 7864328 | tf_op jit(solution)/shard_map/ppermute | solution.py:101
  57.7 3.6 %collective-permute-start.12 = (bf16[160,1024]{1,0:T(8,128)(2,1)S(1)}, bf16[160,1024]{1,0:T(8,128)(2,1)S(1)}, u32[]{:S(2)}, u32[]{:S(2)}) collective-permute-start(bf16[160,1024]{1,0:T(8,128)(2,1)S(1)} %copy-done.12), channel_id=1, source_target_pairs={{0,3},{1,2},{2,1},{3,0},{4,19},{5,18},{6,17},{7,16},{16,7},{17,6},... | collective-permute-start | bytes 983048 | tf_op jit(solution)/shard_map/ppermute | solution.py:107
  65.8 7.4 %collective-permute-done.12 = bf16[160,1024]{1,0:T(8,128)(2,1)S(1)} collective-permute-done((bf16[160,1024]{1,0:T(8,128)(2,1)S(1)}, bf16[160,1024]{1,0:T(8,128)(2,1)S(1)}, u32[]{:S(2)}, u32[]{:S(2)}) %collective-permute-start.12) | collective-permute-done | bytes 327712 | tf_op jit(solution)/shard_map/ppermute | solution.py:107
  73.3 5.8 %collective-permute-done.5 = bf16[160,1024]{1,0:T(8,128)(2,1)S(1)} collective-permute-done((bf16[160,1024]{1,0:T(8,128)(2,1)S(1)}, bf16[160,1024]{1,0:T(8,128)(2,1)S(1)}, u32[]{:S(2)}, u32[]{:S(2)}) %collective-permute-start.5) | collective-permute-done | bytes 327712 | tf_op jit(solution)/shard_map/ppermute | solution.py:107
  82.5 18.9 %collective-permute-start.13 = (bf16[640,1024]{1,0:T(8,128)(2,1)S(1)}, bf16[640,1024]{1,0:T(8,128)(2,1)}, u32[]{:S(2)}, u32[]{:S(2)}) collective-permute-start(bf16[640,1024]{1,0:T(8,128)(2,1)S(1)} %constant_dynamic-update-slice_fusion.4.vn_ref), channel_id=1, source_target_pairs={{0,16},{16,0},{1,17},{17,1},{2,18},{18,2},{3,19},{19,3},{4,20},{20... | collective-permute-start | bytes 3932168 | tf_op jit(solution)/shard_map/ppermute | solution.py:101
  101.6 10.9 %collective-permute-start.27 = (bf16[80,1024]{1,0:T(8,128)(2,1)S(1)}, bf16[80,1024]{1,0:T(8,128)(2,1)S(1)}, u32[]{:S(2)}, u32[]{:S(2)}) collective-permute-start(bf16[80,1024]{1,0:T(8,128)(2,1)S(1)} %get-tuple-element.41), channel_id=1, source_target_pairs={{0,2},{1,3},{2,0},{3,1},{4,18},{5,19},{6,16},{7,17},{16,6},{17,7},... | collective-permute-start | bytes 491528 | tf_op jit(solution)/shard_map/ppermute | solution.py:107
  119.6 2.9 %collective-permute-start.2 = (bf16[80,1024]{1,0:T(8,128)(2,1)}, bf16[80,1024]{1,0:T(8,128)(2,1)}, u32[]{:S(2)}, u32[]{:S(2)}) collective-permute-start(bf16[80,1024]{1,0:T(8,128)(2,1)} %get-tuple-element.37), channel_id=1, source_target_pairs={{0,2},{1,3},{2,0},{3,1},{4,18},{5,19},{6,16},{7,17},{16,6},{17,7},... | collective-permute-start | bytes 491528 | tf_op jit(solution)/shard_map/ppermute | solution.py:107
  124.7 3.2 %collective-permute-start.3 = (bf16[80,1024]{1,0:T(8,128)(2,1)S(1)}, bf16[80,1024]{1,0:T(8,128)(2,1)}, u32[]{:S(2)}, u32[]{:S(2)}) collective-permute-start(bf16[80,1024]{1,0:T(8,128)(2,1)S(1)} %get-tuple-element.36), channel_id=1, source_target_pairs={{0,3},{1,2},{2,1},{3,0},{4,19},{5,18},{6,17},{7,16},{16,7},{17,6},... | collective-permute-start | bytes 491528 | tf_op jit(solution)/shard_map/ppermute | solution.py:107
  128.9 3.0 %collective-permute-done.3 = bf16[80,1024]{1,0:T(8,128)(2,1)} collective-permute-done((bf16[80,1024]{1,0:T(8,128)(2,1)S(1)}, bf16[80,1024]{1,0:T(8,128)(2,1)}, u32[]{:S(2)}, u32[]{:S(2)}) %collective-permute-start.3) | collective-permute-done | bytes 163872 | tf_op jit(solution)/shard_map/ppermute | solution.py:107
  133.1 2.8 %fusion.7 = (bf16[1,1024,320]{1,2,0:T(8,128)(2,1)}, bf16[1,1024,320]{1,2,0:T(8,128)(2,1)}) fusion(s32[]{:T(128)S(6)} %select_n.149, bf16[4,1024,320]{1,2,0:T(8,128)(2,1)} %maximum_select_fusion, bf16[4,1024,320]{1,2,0:T(8,128)(2,1)} %collective-permute-done.19, s32[]{:T(128)S(6)} %select_n.147), kind=kLoop, calls=%fused_computation.30 | loop fusion | flops 655360 | bytes 6553608 | tf_op jit(solution)/shard_map/concatenate | solution.py:126
  140.4 5.0 %fusion = (bf16[1,1024,320]{1,2,0:T(8,128)(2,1)}, bf16[1,1024,320]{1,2,0:T(8,128)(2,1)}, bf16[1,1024,320]{1,2,0:T(8,128)(2,1)}, bf16[1,1024,320]{1,2,0:T(8,128)(...) fusion(s32[]{:T(128)S(6)} %select_n.151, bf16[4,1024,320]{1,2,0:T(8,128)(2,1)} %maximum_select_fusion, ...), kind=kLoop, calls=%fused_computation.23 | loop fusion | flops 1966080 | bytes 9175064 | tf_op jit(solution)/shard_map/concatenate | solution.py:126
  159.0 9.9 %concatenate.33.w_ref = bf16[1024,2560]{1,0:T(8,128)(2,1)} concatenate(bf16[1024,320]{1,0:T(8,128)(2,1)} %bitcast.58, bf16[1024,320]{1,0:T(8,128)(2,1)} %bitcast.59, bf16[1024,320]{1,0:T(8,128)(2,1)} %bitcast.60, bf16[1024,320]{1,0:T(8,128)(2,1)} %bitcast.61, bf16[1024,320]{1,0:T(8,128)(2,1)} %bitcast.62, bf16[1024,320]{1,0:T(8,128)(2,1)} %bitcast.56, ...), dimensions={1} | concatenate | bytes 10485760 | tf_op jit(solution)/shard_map/concatenate | solution.py:132
  170.1 14.2 %shard_map.83 = bf16[320,2560]{1,0:T(8,128)(2,1)} custom-call(bf16[320,1024]{1,0:T(8,128)(2,1)S(1)} %copy-done, bf16[640,1024]{1,0:T(8,128)(2,1)S(1)} %constant_dynamic-update-slice_fusion.kn_ref, bf16[640,1024]{1,0:T(8,128)(2,1)} %collective-permute-done.8.kf_ref, bf16[640,1024]{1,0:T(8,128)(2,1)S(1)} %constant_dynamic-update-slice_fusion.4.vn_ref, ...), custom_call_target="tpu_custom_call" | custom-call | flops 3355443200 | bytes 10485760 | tf_op jit(solution)/shard_map/pallas_call | solution.py:52
  190.8 14.1 %shard_map.82 = bf16[320,2560]{1,0:T(8,128)(2,1)} custom-call(bf16[320,1024]{1,0:T(8,128)(2,1)S(1)} %pad_maximum_fusion.1.q_ref, bf16[640,1024]{1,0:T(8,128)(2,1)S(1)} %constant_dynamic-update-slice_fusion.kn_ref, bf16[640,1024]{1,0:T(8,128)(2,1)} %collective-permute-done.8.kf_ref, bf16[640,1024]{1,0:T(8,128)(2,1)S(1)} %constant_dynamic-update-slice_fusion.4.vn_ref, ...), custom_call_target="tpu_custom_call" | custom-call | flops 3355443200 | bytes 10485760 | tf_op jit(solution)/shard_map/pallas_call | solution.py:52
  211.8 4.7 %collective-permute-done.20 = bf16[80,2560]{1,0:T(8,128)(2,1)S(1)} collective-permute-done((bf16[80,2560]{1,0:T(8,128)(2,1)S(1)}, bf16[80,2560]{1,0:T(8,128)(2,1)S(1)}, u32[]{:S(2)}, u32[]{:S(2)}) %collective-permute-start.20) | collective-permute-done | bytes 409632 | tf_op jit(solution)/shard_map/ppermute | solution.py:162
  218.4 12.9 %collective-permute-done.22 = bf16[80,2560]{1,0:T(8,128)(2,1)S(1)} collective-permute-done((bf16[80,2560]{1,0:T(8,128)(2,1)S(1)}, bf16[80,2560]{1,0:T(8,128)(2,1)S(1)}, u32[]{:S(2)}, u32[]{:S(2)}) %collective-permute-start.22) | collective-permute-done | bytes 409632 | tf_op jit(solution)/shard_map/ppermute | solution.py:162
  233.3 4.9 %collective-permute-start.33 = (bf16[80,2560]{1,0:T(8,128)(2,1)S(1)}, bf16[80,2560]{1,0:T(8,128)(2,1)S(1)}, u32[]{:S(2)}, u32[]{:S(2)}) collective-permute-start(bf16[80,2560]{1,0:T(8,128)(2,1)S(1)} %broadcast_select_fusion), channel_id=1, source_target_pairs={{0,16},{1,17},{2,18},{3,19},{4,20},{5,21},{6,22},{7,23},{8,24},{9,... | collective-permute-start | bytes 1228808 | tf_op jit(solution)/shard_map/ppermute | solution.py:165
  238.4 11.2 %collective-permute-start.24 = (bf16[80,2560]{1,0:T(8,128)(2,1)S(1)}, bf16[80,2560]{1,0:T(8,128)(2,1)S(1)}, u32[]{:S(2)}, u32[]{:S(2)}) collective-permute-start(bf16[80,2560]{1,0:T(8,128)(2,1)S(1)} %broadcast_select_fusion.1), channel_id=1, source_target_pairs={{0,16},{1,17},{2,18},{3,19},{4,20},{5,21},{6,22},{7,23},{8,24},{9,... | collective-permute-start | bytes 1228808 | tf_op jit(solution)/shard_map/ppermute | solution.py:165
  (120 shorter events, 73.9 us)
Async XLA Ops:
  5.2 11.2 %collective-permute-start.16 = (bf16[512,320]{0,1:T(8,128)(2,1)S(1)}, bf16[512,320]{0,1:T(8,128)(2,1)S(1)}, u32[]{:S(2)}, u32[]{:S(2)}) collective-permute-start(bf16[512,320]{0,1:T(8,128)(2,1)S(1)} %get-tuple-element.16), channel_id=1, source_target_pairs={{0,2},{1,3},{2,0},{3,1},{4,18},{5,19},{6,16},{7,17},{16,6},{17,7},... | collective-permute-start | bytes 983048 | tf_op jit(solution)/shard_map/ppermute | solution.py:115
  6.8 15.0 %collective-permute-start.17 = (bf16[512,320]{0,1:T(8,128)(2,1)S(1)}, bf16[512,320]{0,1:T(8,128)(2,1)S(1)}, u32[]{:S(2)}, u32[]{:S(2)}) collective-permute-start(bf16[512,320]{0,1:T(8,128)(2,1)S(1)} %get-tuple-element.15), channel_id=1, source_target_pairs={{0,3},{1,2},{2,1},{3,0},{4,19},{5,18},{6,17},{7,16},{16,7},{17,6},... | collective-permute-start | bytes 983048 | tf_op jit(solution)/shard_map/ppermute | solution.py:115
  22.6 23.4 %collective-permute-start.18 = (bf16[4,512,320]{1,2,0:T(8,128)(2,1)S(1)}, bf16[4,512,320]{1,2,0:T(8,128)(2,1)}, u32[]{:S(2)}, u32[]{:S(2)}) collective-permute-start(bf16[4,512,320]{1,2,0:T(8,128)(2,1)S(1)} %pad_maximum_fusion), channel_id=1, source_target_pairs={{0,8},{8,0},{1,9},{9,1},{2,10},{10,2},{3,11},{11,3},{4,12},{12,4},... | collective-permute-start | bytes 3932168 | tf_op jit(solution)/shard_map/ppermute | solution.py:119
  25.7 32.0 %collective-permute-start.9 = (bf16[160,1024]{1,0:T(8,128)(2,1)}, bf16[160,1024]{1,0:T(8,128)(2,1)S(1)}, u32[]{:S(2)}, u32[]{:S(2)}) collective-permute-start(bf16[160,1024]{1,0:T(8,128)(2,1)} %get-tuple-element.27), channel_id=1, source_target_pairs={{0,0},{1,1},{2,2},{3,3},{4,16},{5,17},{6,18},{7,19},{16,4},{17,5},... | collective-permute-start | bytes 983048 | tf_op jit(solution)/shard_map/ppermute | solution.py:107
  27.4 35.6 %collective-permute-start.10 = (bf16[160,1024]{1,0:T(8,128)(2,1)}, bf16[160,1024]{1,0:T(8,128)(2,1)}, u32[]{:S(2)}, u32[]{:S(2)}) collective-permute-start(bf16[160,1024]{1,0:T(8,128)(2,1)} %get-tuple-element.26), channel_id=1, source_target_pairs={{0,1},{1,0},{2,3},{3,2},{4,17},{5,16},{6,19},{7,18},{16,5},{17,4},... | collective-permute-start | bytes 983048 | tf_op jit(solution)/shard_map/ppermute | solution.py:107
  29.4 34.7 %collective-permute-start.11 = (bf16[160,1024]{1,0:T(8,128)(2,1)}, bf16[160,1024]{1,0:T(8,128)(2,1)}, u32[]{:S(2)}, u32[]{:S(2)}) collective-permute-start(bf16[160,1024]{1,0:T(8,128)(2,1)} %get-tuple-element.28), channel_id=1, source_target_pairs={{0,2},{1,3},{2,0},{3,1},{4,18},{5,19},{6,16},{7,17},{16,6},{17,7},... | collective-permute-start | bytes 983048 | tf_op jit(solution)/shard_map/ppermute | solution.py:107
  32.0 29.3 %collective-permute-start.4 = (bf16[160,1024]{1,0:T(8,128)(2,1)S(1)}, bf16[160,1024]{1,0:T(8,128)(2,1)}, u32[]{:S(2)}, u32[]{:S(2)}) collective-permute-start(bf16[160,1024]{1,0:T(8,128)(2,1)S(1)} %get-tuple-element.31), channel_id=1, source_target_pairs={{0,0},{1,1},{2,2},{3,3},{4,16},{5,17},{6,18},{7,19},{16,4},{17,5},... | collective-permute-start | bytes 983048 | tf_op jit(solution)/shard_map/ppermute | solution.py:107
  49.3 83.8 %collective-permute-start.19 = (bf16[4,1024,320]{1,2,0:T(8,128)(2,1)}, bf16[4,1024,320]{1,2,0:T(8,128)(2,1)}, u32[]{:S(2)}, u32[]{:S(2)}) collective-permute-start(bf16[4,1024,320]{1,2,0:T(8,128)(2,1)} %maximum_select_fusion), channel_id=1, source_target_pairs={{0,16},{16,0},{1,17},{17,1},{2,18},{18,2},{3,19},{19,3},{4,20},{20... | collective-permute-start | bytes 7864328 | tf_op jit(solution)/shard_map/ppermute | solution.py:101
  57.7 15.6 %collective-permute-start.12 = (bf16[160,1024]{1,0:T(8,128)(2,1)S(1)}, bf16[160,1024]{1,0:T(8,128)(2,1)S(1)}, u32[]{:S(2)}, u32[]{:S(2)}) collective-permute-start(bf16[160,1024]{1,0:T(8,128)(2,1)S(1)} %copy-done.12), channel_id=1, source_target_pairs={{0,3},{1,2},{2,1},{3,0},{4,19},{5,18},{6,17},{7,16},{16,7},{17,6},... | collective-permute-start | bytes 983048 | tf_op jit(solution)/shard_map/ppermute | solution.py:107
  61.3 40.3 %collective-permute-start.25 = (bf16[80,1024]{1,0:T(8,128)(2,1)S(1)}, bf16[80,1024]{1,0:T(8,128)(2,1)S(1)}, u32[]{:S(2)}, u32[]{:S(2)}) collective-permute-start(bf16[80,1024]{1,0:T(8,128)(2,1)S(1)} %get-tuple-element.39), channel_id=1, source_target_pairs={{0,0},{1,1},{2,2},{3,3},{4,16},{5,17},{6,18},{7,19},{16,4},{17,5},... | collective-permute-start | bytes 491528 | tf_op jit(solution)/shard_map/ppermute | solution.py:107
  63.0 16.1 %collective-permute-start.5 = (bf16[160,1024]{1,0:T(8,128)(2,1)S(1)}, bf16[160,1024]{1,0:T(8,128)(2,1)S(1)}, u32[]{:S(2)}, u32[]{:S(2)}) collective-permute-start(bf16[160,1024]{1,0:T(8,128)(2,1)S(1)} %copy-done.13), channel_id=1, source_target_pairs={{0,1},{1,0},{2,3},{3,2},{4,17},{5,16},{6,19},{7,18},{16,5},{17,4},... | collective-permute-start | bytes 983048 | tf_op jit(solution)/shard_map/ppermute | solution.py:107
  64.1 18.4 %collective-permute-start.6 = (bf16[160,1024]{1,0:T(8,128)(2,1)S(1)}, bf16[160,1024]{1,0:T(8,128)(2,1)S(1)}, u32[]{:S(2)}, u32[]{:S(2)}) collective-permute-start(bf16[160,1024]{1,0:T(8,128)(2,1)S(1)} %copy-done.11), channel_id=1, source_target_pairs={{0,2},{1,3},{2,0},{3,1},{4,18},{5,19},{6,16},{7,17},{16,6},{17,7},... | collective-permute-start | bytes 983048 | tf_op jit(solution)/shard_map/ppermute | solution.py:107
  73.2 28.2 %collective-permute-start.7 = (bf16[160,1024]{1,0:T(8,128)(2,1)S(1)}, bf16[160,1024]{1,0:T(8,128)(2,1)S(1)}, u32[]{:S(2)}, u32[]{:S(2)}) collective-permute-start(bf16[160,1024]{1,0:T(8,128)(2,1)S(1)} %copy-done.10), channel_id=1, source_target_pairs={{0,3},{1,2},{2,1},{3,0},{4,19},{5,18},{6,17},{7,16},{16,7},{17,6},... | collective-permute-start | bytes 983048 | tf_op jit(solution)/shard_map/ppermute | solution.py:107
  79.1 33.4 %collective-permute-start.26 = (bf16[80,1024]{1,0:T(8,128)(2,1)S(1)}, bf16[80,1024]{1,0:T(8,128)(2,1)S(1)}, u32[]{:S(2)}, u32[]{:S(2)}) collective-permute-start(bf16[80,1024]{1,0:T(8,128)(2,1)S(1)} %get-tuple-element.42), channel_id=1, source_target_pairs={{0,1},{1,0},{2,3},{3,2},{4,17},{5,16},{6,19},{7,18},{16,5},{17,4},... | collective-permute-start | bytes 491528 | tf_op jit(solution)/shard_map/ppermute | solution.py:107
  82.5 86.5 %collective-permute-start.13 = (bf16[640,1024]{1,0:T(8,128)(2,1)S(1)}, bf16[640,1024]{1,0:T(8,128)(2,1)}, u32[]{:S(2)}, u32[]{:S(2)}) collective-permute-start(bf16[640,1024]{1,0:T(8,128)(2,1)S(1)} %constant_dynamic-update-slice_fusion.4.vn_ref), channel_id=1, source_target_pairs={{0,16},{16,0},{1,17},{17,1},{2,18},{18,2},{3,19},{19,3},{4,20},{20... | collective-permute-start | bytes 3932168 | tf_op jit(solution)/shard_map/ppermute | solution.py:101
  101.5 67.5 %collective-permute-start.8 = (bf16[640,1024]{1,0:T(8,128)(2,1)S(1)}, bf16[640,1024]{1,0:T(8,128)(2,1)}, u32[]{:S(2)}, u32[]{:S(2)}) collective-permute-start(bf16[640,1024]{1,0:T(8,128)(2,1)S(1)} %constant_dynamic-update-slice_fusion.kn_ref), channel_id=1, source_target_pairs={{0,16},{16,0},{1,17},{17,1},{2,18},{18,2},{3,19},{19,3},{4,20},{20... | collective-permute-start | bytes 3932168 | tf_op jit(solution)/shard_map/ppermute | solution.py:101
  101.6 14.2 %collective-permute-start.27 = (bf16[80,1024]{1,0:T(8,128)(2,1)S(1)}, bf16[80,1024]{1,0:T(8,128)(2,1)S(1)}, u32[]{:S(2)}, u32[]{:S(2)}) collective-permute-start(bf16[80,1024]{1,0:T(8,128)(2,1)S(1)} %get-tuple-element.41), channel_id=1, source_target_pairs={{0,2},{1,3},{2,0},{3,1},{4,18},{5,19},{6,16},{7,17},{16,6},{17,7},... | collective-permute-start | bytes 491528 | tf_op jit(solution)/shard_map/ppermute | solution.py:107
  185.6 23.5 %collective-permute-start.29 = (bf16[80,2560]{1,0:T(8,128)(2,1)S(1)}, bf16[80,2560]{1,0:T(8,128)(2,1)S(1)}, u32[]{:S(2)}, u32[]{:S(2)}) collective-permute-start(bf16[80,2560]{1,0:T(8,128)(2,1)S(1)} %get-tuple-element.20), channel_id=1, source_target_pairs={{0,1},{1,0},{2,3},{3,2},{4,5},{5,4},{6,7},{7,6},{8,9},{9,8},{10,11... | collective-permute-start | bytes 1228808 | tf_op jit(solution)/shard_map/ppermute | solution.py:162
  188.2 21.5 %collective-permute-start.30 = (bf16[80,2560]{1,0:T(8,128)(2,1)S(1)}, bf16[80,2560]{1,0:T(8,128)(2,1)S(1)}, u32[]{:S(2)}, u32[]{:S(2)}) collective-permute-start(bf16[80,2560]{1,0:T(8,128)(2,1)S(1)} %get-tuple-element.22), channel_id=1, source_target_pairs={{0,2},{1,3},{2,0},{3,1},{4,6},{5,7},{6,4},{7,5},{8,10},{9,11},{10,... | collective-permute-start | bytes 1228808 | tf_op jit(solution)/shard_map/ppermute | solution.py:162
  190.2 19.6 %collective-permute-start.31 = (bf16[80,2560]{1,0:T(8,128)(2,1)S(1)}, bf16[80,2560]{1,0:T(8,128)(2,1)S(1)}, u32[]{:S(2)}, u32[]{:S(2)}) collective-permute-start(bf16[80,2560]{1,0:T(8,128)(2,1)S(1)} %get-tuple-element.21), channel_id=1, source_target_pairs={{0,3},{1,2},{2,1},{3,0},{4,7},{5,6},{6,5},{7,4},{8,11},{9,10},{10,... | collective-permute-start | bytes 1228808 | tf_op jit(solution)/shard_map/ppermute | solution.py:162
  209.1 22.2 %collective-permute-start.22 = (bf16[80,2560]{1,0:T(8,128)(2,1)S(1)}, bf16[80,2560]{1,0:T(8,128)(2,1)S(1)}, u32[]{:S(2)}, u32[]{:S(2)}) collective-permute-start(bf16[80,2560]{1,0:T(8,128)(2,1)S(1)} %get-tuple-element.18), channel_id=1, source_target_pairs={{0,3},{1,2},{2,1},{3,0},{4,7},{5,6},{6,5},{7,4},{8,11},{9,10},{10,... | collective-permute-start | bytes 1228808 | tf_op jit(solution)/shard_map/ppermute | solution.py:162
  211.0 22.2 %collective-permute-start.32 = (bf16[80,2560]{1,0:T(8,128)(2,1)S(1)}, bf16[80,2560]{1,0:T(8,128)(2,1)S(1)}, u32[]{:S(2)}, u32[]{:S(2)}) collective-permute-start(bf16[80,2560]{1,0:T(8,128)(2,1)S(1)} %add_convert_fusion.1), channel_id=1, source_target_pairs={{0,0},{1,1},{2,2},{3,3},{4,16},{5,17},{6,18},{7,19},{16,4},{17,5},... | collective-permute-start | bytes 1228808 | tf_op jit(solution)/shard_map/ppermute | solution.py:163
  233.3 17.1 %collective-permute-start.33 = (bf16[80,2560]{1,0:T(8,128)(2,1)S(1)}, bf16[80,2560]{1,0:T(8,128)(2,1)S(1)}, u32[]{:S(2)}, u32[]{:S(2)}) collective-permute-start(bf16[80,2560]{1,0:T(8,128)(2,1)S(1)} %broadcast_select_fusion), channel_id=1, source_target_pairs={{0,16},{1,17},{2,18},{3,19},{4,20},{5,21},{6,22},{7,23},{8,24},{9,... | collective-permute-start | bytes 1228808 | tf_op jit(solution)/shard_map/ppermute | solution.py:165
  238.4 12.6 %collective-permute-start.24 = (bf16[80,2560]{1,0:T(8,128)(2,1)S(1)}, bf16[80,2560]{1,0:T(8,128)(2,1)S(1)}, u32[]{:S(2)}, u32[]{:S(2)}) collective-permute-start(bf16[80,2560]{1,0:T(8,128)(2,1)S(1)} %broadcast_select_fusion.1), channel_id=1, source_target_pairs={{0,16},{1,17},{2,18},{3,19},{4,20},{5,21},{6,22},{7,23},{8,24},{9,... | collective-permute-start | bytes 1228808 | tf_op jit(solution)/shard_map/ppermute | solution.py:165
  (27 other events, 343.1 us)

commit v2 on v1

v2 whole, which is shorter than its diff:
```python
import math

import jax
import jax.numpy as jnp
from jax import lax
from jax.experimental import pallas as pl
from jax.experimental.pallas import tpu as pltpu
from jax.sharding import PartitionSpec as P

HEADS = 32
HIDDEN = 40_000_000_000
CHUNKS = 2
JOINED = 2


def attend_project(
    query_parts, chunk_rows, context, weight_blocks, where, head_size
):
    homes, home_rows, features = context[0].shape
    home_rows = home_rows // 2
    steps = features // head_size // JOINED
    key_rows = homes * home_rows
    block_columns, share = weight_blocks[0].shape[1:]
    columns = 2 * homes * block_columns
    scale = float(head_size) ** (-0.5) * math.log2(math.e)
    together = math.gcd(homes, 4)
    block_rows = together * chunk_rows
    contract = (((1,), (1,)), ((), ()))

    def body(where, *refs):
        q_refs, refs = refs[:homes], refs[homes:]
        context_refs, weight_refs, refs = refs[:2], refs[2:6], refs[6:]
        out_refs, (attended, w_held, w_sem) = refs[:homes], refs[homes:]
        step = pl.program_id(0)
        side, mine, spot = where[0], where[1], where[2]

        def each_fetch(act):
            for index, ref in enumerate(weight_refs):
                at_side = side if index < 2 else 1 - side
                at_group = mine if index % 2 == 0 else 1 - mine
                for home in range(homes):
                    block = at_side * homes + (spot ^ home)
                    act(
                        pltpu.make_async_copy(
                            ref.at[home],
                            w_held.at[
                                pl.ds(pl.multiple_of(block * block_columns, block_columns), block_columns),
                                pl.ds(pl.multiple_of(at_group * share, share), share),
                            ],
                            w_sem.at[index, home],
                        )
                    )

        @pl.when(step == 0)
        def _():
            each_fetch(lambda copy: copy.start())

        for index in range(JOINED):
            cols = slice(index * head_size, (index + 1) * head_size)
            near_keys, far_keys, near_values, far_values = (
                ref[:, kind * home_rows : (kind + 1) * home_rows, cols].reshape(key_rows, head_size)
                for kind in range(2)
                for ref in context_refs
            )
            for first in range(0, homes, together):
                query = jnp.concatenate([ref[:, cols] for ref in q_refs[first : first + together]], axis=0)
                near = lax.dot_general(query, near_keys, contract, preferred_element_type=jnp.float32)
                far = lax.dot_general(query, far_keys, contract, preferred_element_type=jnp.float32)
                peak = jnp.maximum(
                    jnp.max(near, axis=1, keepdims=True), jnp.max(far, axis=1, keepdims=True)
                )
                near = jnp.exp2((near - peak) * scale)
                far = jnp.exp2((far - peak) * scale)
                total = jnp.sum(near, axis=1, keepdims=True) + jnp.sum(far, axis=1, keepdims=True)
                mixed = jnp.dot(near.astype(jnp.bfloat16), near_values, preferred_element_type=jnp.float32)
                mixed += jnp.dot(far.astype(jnp.bfloat16), far_values, preferred_element_type=jnp.float32)
                mixed = (mixed / total).astype(jnp.bfloat16)
                for at in range(steps):

                    @pl.when(step == at)
                    def _():
                        begin = (at * JOINED + index) * head_size
                        attended[
                            first * chunk_rows : first * chunk_rows + block_rows, begin : begin + head_size
                        ] = mixed

        @pl.when(step == steps - 1)
        def _():
            each_fetch(lambda copy: copy.wait())
            for first in range(0, homes, together):
                product = lax.dot_general(
                    attended[first * chunk_rows : first * chunk_rows + block_rows],
                    w_held[...],
                    contract,
                    preferred_element_type=jnp.float32,
                )
                for at, ref in enumerate(out_refs[first : first + together]):
                    ref[...] = product[at * chunk_rows : (at + 1) * chunk_rows].astype(ref.dtype)

    width = JOINED * head_size
    stacked = pl.BlockSpec((homes, 2 * home_rows, width), lambda step, _: (0, 0, step))
    return pl.pallas_call(
        body,
        grid_spec=pltpu.PrefetchScalarGridSpec(
            num_scalar_prefetch=1,
            grid=(steps,),
            in_specs=[
                *[pl.BlockSpec((chunk_rows, width), lambda step, _: (0, step))] * homes,
                *[stacked] * 2,
                *[pl.BlockSpec(memory_space=pl.ANY)] * 4,
            ],
            out_specs=[pl.BlockSpec((chunk_rows, columns), lambda step, _: (0, 0))] * homes,
            scratch_shapes=[
                pltpu.VMEM((homes * chunk_rows, features), jnp.bfloat16),
                pltpu.VMEM((columns, features), jnp.bfloat16),
                pltpu.SemaphoreType.DMA((4, homes)),
            ],
        ),
        out_shape=[
            jax.ShapeDtypeStruct((chunk_rows, columns), jnp.float32 if home == 0 else jnp.bfloat16)
            for home in range(homes)
        ],
        compiler_params=pltpu.CompilerParams(vmem_limit_bytes=(28 if homes <= 4 else 56) * 1024 * 1024),
        cost_estimate=pl.CostEstimate(
            flops=homes * chunk_rows * features * (8 * key_rows + 2 * columns) + 0,
            bytes_accessed=2 * features * (4 * key_rows + columns),
            transcendentals=homes * chunk_rows * 2 * key_rows * (features // head_size),
        ),
    )(where, *query_parts, *context, *weight_blocks)


def gathered(parts, rows, hidden):
    homes, width = len(parts), parts[0].shape[1]

    def body(*refs):
        part_refs, out_ref = refs[:homes], refs[homes]
        for home, ref in enumerate(part_refs):
            out_ref[home] = ref[:rows]

    return pl.pallas_call(
        body,
        out_shape=jax.ShapeDtypeStruct((homes, rows, width), parts[0].dtype),
        compiler_params=pltpu.CompilerParams(vmem_limit_bytes=16 * 1024 * 1024),
        cost_estimate=pl.CostEstimate(flops=hidden, bytes_accessed=8 * homes * rows * width, transcendentals=0),
    )(*parts)


def per_device(
    query_rows, key_rows, value_rows, residual, control_mask, step_index, step_gates, out_weight
):
    query, key, value = query_rows[0], key_rows[0], value_rows[0]
    weight = jnp.swapaxes(out_weight[0], 0, 1)
    rows, all_features = query.shape
    head_size = all_features // HEADS
    count = lax.axis_size("seq")
    half = count // 2
    shares = lax.axis_size("group")
    features = all_features // half
    columns = weight.shape[0]
    branch = lax.axis_index("branch")
    group = lax.axis_index("group")
    place = lax.axis_index("seq")
    spot = place % half
    pair = ("branch", "seq")

    def crossing(step):
        return [
            (b * count + h * half + r, h * count + b * half + (r ^ step))
            for b in range(2)
            for h in range(2)
            for r in range(half)
        ]

    def send(array, step):
        return lax.ppermute(array, pair, crossing(step))

    def sibling(array):
        return lax.ppermute(array, "branch", [(0, 1), (1, 0)])

    def after(*arrays):
        return lax.optimization_barrier(arrays)

    def mine(array, step):
        return lax.dynamic_slice_in_dim(array, (spot ^ step) * features, features, axis=-1)

    chunk_rows = rows // CHUNKS
    pieces = [slice(chunk * chunk_rows, (chunk + 1) * chunk_rows) for chunk in range(CHUNKS)]

    share = features // shares
    weight_parts = [
        send(lax.dynamic_slice_in_dim(weight, (spot ^ step) * features + group * share, share, axis=1), step)
        for step in range(half)
    ]
    own = jnp.stack(weight_parts)
    other = lax.ppermute(own, "group", [(0, 1), (1, 0)])
    where = jnp.stack([branch, group, spot]).astype(jnp.int32)
    pair_parts = []
    for step in range(half):
        part = jnp.concatenate([mine(key, step), mine(value, step)], axis=0)
        if step > 0:
            part, weight_parts[step - 1] = after(part, weight_parts[step - 1])
        pair_parts.append(send(part, step))
    own, pair_parts[0] = after(own, pair_parts[0])
    own_far, other_far = sibling(own), sibling(other)
    queries = [[mine(query[piece], step) for step in range(half)] for piece in pieces]
    for step in range(half):
        at = min(step, half - 2)
        queries[0][step], pair_parts[at] = after(queries[0][step], pair_parts[at])
    queries[0][0], own_far = after(queries[0][0], own_far)
    queries[0][2], other_far = after(queries[0][2], other_far)
    query_parts = [send(part, step) for step, part in enumerate(queries[0])]
    near = gathered(pair_parts, 2 * rows, 0)
    far = sibling(near)
    queries[1][0], far = after(queries[1][0], far)
    query_parts = [query_parts, [send(part, step) for step, part in enumerate(queries[1])]]
    weight_blocks = (own, other, own_far, other_far)

    partials = [
        attend_project(
            parts,
            chunk_rows,
            (near, far),
            weight_blocks,
            where,
            head_size,
        )
        for parts in query_parts
    ]

    step_ids = lax.broadcasted_iota(jnp.int32, (step_gates.shape[0], 1), 0)
    gate_row = jnp.sum(
        jnp.where(step_ids == step_index[0], step_gates, jnp.zeros_like(step_gates)), axis=0
    )
    is_main = branch == 1
    outs = []
    for piece, partial in zip(pieces, partials):
        summed = partial[0]
        for step in range(1, half):
            swap = [(s, s ^ step) for s in range(count)]
            summed = summed + lax.ppermute(partial[step], "seq", swap).astype(jnp.float32)
        projected = send(summed.astype(jnp.bfloat16), 0)
        hint = jnp.where(control_mask[piece, None] == 1, projected, jnp.zeros_like(projected))
        hint_moved = lax.ppermute(hint, "branch", [(0, 1)])
        mixed = (
            residual[piece].astype(jnp.float32)
            + gate_row[None, :] * projected.astype(jnp.float32)
            + hint_moved.astype(jnp.float32)
        ).astype(jnp.bfloat16)
        outs.append(jnp.where(is_main, mixed, hint))
    return jnp.concatenate(outs, axis=0)[None]


def solution(mesh):
    placed = (
        P("branch", ("group", "seq"), None),
        P("branch", ("group", "seq"), None),
        P("branch", ("group", "seq"), None),
        P(("group", "seq"), None),
        P(("group", "seq")),
        P("group"),
        P(),
        P("branch", None, "seq"),
    )
    return jax.shard_map(
        per_device,
        mesh=mesh,
        in_specs=placed,
        out_specs=P("branch", ("group", "seq"), None),
        check_vma=False,
    )
```

time: 254 us -> 188 us (0.74)
  local copies, waits for them, and re-layouts: 40.5 us -> 3.66 us
  other arithmetic: 17.7 us -> 5.54 us
  waiting for transfers between devices: 71.7 us -> 61.2 us
  Pallas kernels: 28.2 us -> 23.3 us
    dynamic_slice x13 -> x4, local copies, waits for them, and re-layouts: 22.3 us -> 3.46 us  [the longest x1 2.39 us: per_device(): lax.dynamic_slice_in_dim(weight, (spot ^ step) * features + group * share...]
    ppermute x1, waiting for transfers between devices: 12.6 us -> 0.01 us  [per_device(): other = lax.ppermute(own, 'group', [(0, 1), (1, 0)])]
    concatenate x3 -> x0, local copies, waits for them, and re-layouts: 9.99 us -> none  [the longest x1 9.94 us: per_device(): weight_rows = jnp.concatenate(ordered, axis=1)]
    concatenate x4, other arithmetic: 9.9 us -> 0.18 us  [per_device(): part = jnp.concatenate([mine(key, step), mine(value, step)], axis=0)]
    unnamed x40 -> x14, local copies, waits for them, and re-layouts: 5.42 us -> 0.1 us
    pallas_call x2 -> x3, Pallas kernels: 28.2 us -> 23.3 us  [the longest x2 23.1 us: attend_project(): pl.pallas_call(body, grid_spec=pltpu.PrefetchScalarGridSpec(num_scalar_pr...]
    ppermute x2, starting transfers between devices: 16.1 us -> 19.5 us  [per_device(): hint_moved = lax.ppermute(hint, 'branch', [(0, 1)])]
    select_n x1 -> x0, other arithmetic: 3.31 us -> none  [per_device(): jnp.where(group == 0, jnp.concatenate([own, other], axis=1), jnp.concaten...]
  transfers between devices with their start and end apart: 34 -> 30, of which waited for: 15 -> 8; matrix products, arithmetic and copies ran while one was open for 20% -> 3% of each run, Pallas kernels for 6% -> 12%
where the time goes in v2:
time: 188 us; the launch traced here: 187 us
  starting transfers between devices  92.6 us (49%)
  waiting for transfers between devices  61.2 us (33%)
  Pallas kernels  23.3 us (12%)
  other arithmetic  5.54 us (3%)
  local copies, waits for them, and re-layouts  3.66 us (2%)
    ppermute x18, starting transfers between devices, send(): return lax.ppermute(array, pair, crossing(step))  38.9 us
    ppermute x18, waiting for transfers between devices, send(): return lax.ppermute(array, pair, crossing(step))  37.8 us
    ppermute x3, starting transfers between devices, sibling(): return lax.ppermute(array, 'branch', [(0, 1), (1, 0)])  25.2 us
    pallas_call x2, Pallas kernels, attend_project(): pl.pallas_call(body, grid_spec=pltpu.PrefetchScalarGridSpec(num_scalar_pr...  23.1 us
    ppermute x6, waiting for transfers between devices, per_device(): lax.ppermute(partial[step], 'seq', swap).astype(jnp.float32)  22.7 us
    ppermute x2, starting transfers between devices, per_device(): hint_moved = lax.ppermute(hint, 'branch', [(0, 1)])  19.5 us
    ppermute x6, starting transfers between devices, per_device(): lax.ppermute(partial[step], 'seq', swap).astype(jnp.float32)  7.11 us
  transfers between devices with their start and end apart: 30, of which 8 were waited for; matrix products, arithmetic and copies ran while one was open for 3% of the time, Pallas kernels for 12%

profile of v2, /device:TPU:0, one launch (start us, length us, event | category | flops | bytes accessed | tf_op | source)
XLA Modules:
  0.0 187.2 jit_solution(15175215379200202821)
XLA Ops:
  0.0 2.4 %dynamic-slice_bitcast_fusion.11 = (bf16[320,512]{1,0:T(8,128)(2,1)}, bf16[320,512]{1,0:T(8,128)(2,1)}, bf16[320,512]{1,0:T(8,128)(2,1)S(1)}, bf16[320,512]{1,0:T(8,128)(2,1)}) fusion(bf16[1,4096,320]{1,2,0:T(8,128)(2,1)} %param.15, s32[]{:T(128)S(6)} %select_n.70, s32[]{:T(128)S(6)} %select_n.71, s32[]{:T(128)S(6)} %select_n.73, s32[]{:T(128)S(6)} %select_n.72), kind=kLoop, calls=%fused_computation.26 | loop fusion | bytes 2621456 | tf_op jit(solution)/shard_map/dynamic_slice | solution.py:191
  2.4 2.9 %collective-permute-start.1 = (bf16[320,512]{1,0:T(8,128)(2,1)}, bf16[320,512]{1,0:T(8,128)(2,1)S(1)}, u32[]{:S(2)}, u32[]{:S(2)}) collective-permute-start(bf16[320,512]{1,0:T(8,128)(2,1)} %get-tuple-element.60), channel_id=1, source_target_pairs={{0,1},{1,0},{2,3},{3,2},{4,17},{5,16},{6,19},{7,18},{16,5},{17,4},... | collective-permute-start | bytes 983048 | tf_op jit(solution)/shard_map/ppermute | solution.py:175
  5.3 3.9 %collective-permute-start = (bf16[320,512]{1,0:T(8,128)(2,1)}, bf16[320,512]{1,0:T(8,128)(2,1)}, u32[]{:S(2)}, u32[]{:S(2)}) collective-permute-start(bf16[320,512]{1,0:T(8,128)(2,1)} %get-tuple-element.59), channel_id=1, source_target_pairs={{0,0},{1,1},{2,2},{3,3},{4,16},{5,17},{6,18},{7,19},{16,4},{17,5},... | collective-permute-start | bytes 983048 | tf_op jit(solution)/shard_map/ppermute | solution.py:175
  10.4 1.6 collective-permute-start.2
  12.2 4.0 %collective-permute-start.9 = (bf16[320,1024]{1,0:T(8,128)(2,1)S(1)}, bf16[320,1024]{1,0:T(8,128)(2,1)S(1)}, u32[]{:S(2)}, u32[]{:S(2)}) collective-permute-start(bf16[320,1024]{1,0:T(8,128)(2,1)S(1)} %pad_maximum_fusion.3), channel_id=1, source_target_pairs={{0,2},{1,3},{2,0},{3,1},{4,18},{5,19},{6,16},{7,17},{16,6},{17,7},... | collective-permute-start | bytes 1966088 | tf_op jit(solution)/shard_map/ppermute | solution.py:175
  16.2 1.5 collective-permute-start.7
  17.7 4.0 %collective-permute-done.2 = bf16[320,512]{1,0:T(8,128)(2,1)S(1)} collective-permute-done((bf16[320,512]{1,0:T(8,128)(2,1)S(1)}, bf16[320,512]{1,0:T(8,128)(2,1)S(1)}, u32[]{:S(2)}, u32[]{:S(2)}) %collective-permute-start.2) | collective-permute-done | bytes 327712 | tf_op jit(solution)/shard_map/ppermute | solution.py:175
  22.6 5.6 %collective-permute-done.3 = bf16[320,512]{1,0:T(8,128)(2,1)S(1)} collective-permute-done((bf16[320,512]{1,0:T(8,128)(2,1)S(1)}, bf16[320,512]{1,0:T(8,128)(2,1)S(1)}, u32[]{:S(2)}, u32[]{:S(2)}) %collective-permute-start.3) | collective-permute-done | bytes 327712 | tf_op jit(solution)/shard_map/ppermute | solution.py:175
  28.3 2.3 %pad_maximum_fusion.refs_6_ = bf16[4,320,512]{2,1,0:T(8,128)(2,1)} fusion(bf16[1,320,512]{2,1,0:T(8,128)(2,1)S(1)} %bitcast.61, bf16[1,320,512]{2,1,0:T(8,128)(2,1)S(1)} %bitcast.60, bf16[1,320,512]{2,1,0:T(8,128)(2,1)S(1)} %bitcast.59, bf16[1,320,512]{2,1,0:T(8,128)(2,1)} %bitcast.7), kind=kLoop, calls=%fused_computation | loop fusion | flops 1966080 | bytes 2621440 | tf_op jit(solution)/shard_map/stack | solution.py:194
  30.6 1.9 %collective-permute-start.10 = (bf16[4,320,512]{2,1,0:T(8,128)(2,1)}, bf16[4,320,512]{2,1,0:T(8,128)(2,1)}, u32[]{:S(2)}, u32[]{:S(2)}) collective-permute-start(bf16[4,320,512]{2,1,0:T(8,128)(2,1)} %pad_maximum_fusion.refs_6_), channel_id=1, source_target_pairs={{0,8},{8,0},{1,9},{9,1},{2,10},{10,2},{3,11},{11,3},{4,12},{12,4},... | collective-permute-start | bytes 3932168 | tf_op jit(solution)/shard_map/ppermute | solution.py:195
  33.4 11.9 %collective-permute-done.9.refs_2_ = bf16[320,1024]{1,0:T(8,128)(2,1)S(1)} collective-permute-done((bf16[320,1024]{1,0:T(8,128)(2,1)S(1)}, bf16[320,1024]{1,0:T(8,128)(2,1)S(1)}, u32[]{:S(2)}, u32[]{:S(2)}) %collective-permute-start.9) | collective-permute-done | bytes 655392 | tf_op jit(solution)/shard_map/ppermute | solution.py:175
  45.3 16.3 %collective-permute-done.14.refs_3_ = bf16[320,1024]{1,0:T(8,128)(2,1)S(1)} collective-permute-done((bf16[320,1024]{1,0:T(8,128)(2,1)S(1)}, bf16[320,1024]{1,0:T(8,128)(2,1)S(1)}, u32[]{:S(2)}, u32[]{:S(2)}) %collective-permute-start.14) | collective-permute-done | bytes 655392 | tf_op jit(solution)/shard_map/ppermute | solution.py:175
  61.7 24.7 %collective-permute-start.15 = (bf16[4,320,1024]{2,1,0:T(8,128)(2,1)S(1)}, bf16[4,320,1024]{2,1,0:T(8,128)(2,1)}, u32[]{:S(2)}, u32[]{:S(2)}) collective-permute-start(bf16[4,320,1024]{2,1,0:T(8,128)(2,1)S(1)} %shard_map.82.refs_4_), channel_id=1, source_target_pairs={{0,16},{16,0},{1,17},{17,1},{2,18},{18,2},{3,19},{19,3},{4,20},{20... | collective-permute-start | bytes 7864328 | tf_op jit(solution)/shard_map/ppermute | solution.py:178
  86.9 10.0 %collective-permute-start.13 = (bf16[80,1024]{1,0:T(8,128)(2,1)}, bf16[80,1024]{1,0:T(8,128)(2,1)S(1)}, u32[]{:S(2)}, u32[]{:S(2)}) collective-permute-start(bf16[80,1024]{1,0:T(8,128)(2,1)} %get-tuple-element.42), channel_id=1, source_target_pairs={{0,3},{1,2},{2,1},{3,0},{4,19},{5,18},{6,17},{7,16},{16,7},{17,6},... | collective-permute-start | bytes 491528 | tf_op jit(solution)/shard_map/ppermute | solution.py:175
  97.7 1.6 collective-permute-start.6
  99.3 5.1 %collective-permute-start.12 = (bf16[80,1024]{1,0:T(8,128)(2,1)S(1)}, bf16[80,1024]{1,0:T(8,128)(2,1)S(1)}, u32[]{:S(2)}, u32[]{:S(2)}) collective-permute-start(bf16[80,1024]{1,0:T(8,128)(2,1)S(1)} %get-tuple-element.40), channel_id=1, source_target_pairs={{0,2},{1,3},{2,0},{3,1},{4,18},{5,19},{6,16},{7,17},{16,6},{17,7},... | collective-permute-start | bytes 491528 | tf_op jit(solution)/shard_map/ppermute | solution.py:175
  105.8 2.2 %collective-permute-start.24 = (bf16[80,1024]{1,0:T(8,128)(2,1)S(1)}, bf16[80,1024]{1,0:T(8,128)(2,1)S(1)}, u32[]{:S(2)}, u32[]{:S(2)}) collective-permute-start(bf16[80,1024]{1,0:T(8,128)(2,1)S(1)} %get-tuple-element.75), channel_id=1, source_target_pairs={{0,3},{1,2},{2,1},{3,0},{4,19},{5,18},{6,17},{7,16},{16,7},{17,6},... | collective-permute-start | bytes 491528 | tf_op jit(solution)/shard_map/ppermute | solution.py:175
  108.8 11.6 %shard_map.83 = (f32[80,2560]{1,0:T(8,128)S(1)}, bf16[80,2560]{1,0:T(8,128)(2,1)S(1)}, bf16[80,2560]{1,0:T(8,128)(2,1)S(1)}, bf16[80,2560]{1,0:T(8,128)(2,1)S(1)}) custom-call(s32[3]{0:T(128)S(1)} %pad_add_fusion.where, bf16[80,1024]{1,0:T(8,128)(2,1)S(1)} %collective-permute-done.6.refs_0_, bf16[80,1024]{1,0:T(8,128)(2,1)S(1)} %collective-permute-done.8.refs_1_, ...), custom_call_target="tpu_custom_call" | custom-call | flops 3355443200 | bytes 10485760 | tf_op jit(solution)/shard_map/pallas_call | solution.py:102
  124.0 11.6 %shard_map.84 = (f32[80,2560]{1,0:T(8,128)S(1)}, bf16[80,2560]{1,0:T(8,128)(2,1)S(1)}, bf16[80,2560]{1,0:T(8,128)(2,1)S(1)}, bf16[80,2560]{1,0:T(8,128)(2,1)S(1)}) custom-call(s32[3]{0:T(128)S(1)} %pad_add_fusion.where, bf16[80,1024]{1,0:T(8,128)(2,1)S(1)} %collective-permute-done.21.refs_0_, bf16[80,1024]{1,0:T(8,128)(2,1)S(1)} %collective-permute-done.22.refs_1_, ...), custom_call_target="tpu_custom_call" | custom-call | flops 3355443200 | bytes 10485760 | tf_op jit(solution)/shard_map/pallas_call | solution.py:102
  139.1 1.4 collective-permute-done.18
  141.4 9.9 %collective-permute-done.25 = bf16[80,2560]{1,0:T(8,128)(2,1)S(1)} collective-permute-done((bf16[80,2560]{1,0:T(8,128)(2,1)S(1)}, bf16[80,2560]{1,0:T(8,128)(2,1)S(1)}, u32[]{:S(2)}, u32[]{:S(2)}) %collective-permute-start.25) | collective-permute-done | bytes 409632 | tf_op jit(solution)/shard_map/ppermute | solution.py:240
  151.3 11.4 %collective-permute-done.27 = bf16[80,2560]{1,0:T(8,128)(2,1)S(1)} collective-permute-done((bf16[80,2560]{1,0:T(8,128)(2,1)S(1)}, bf16[80,2560]{1,0:T(8,128)(2,1)S(1)}, u32[]{:S(2)}, u32[]{:S(2)}) %collective-permute-start.27) | collective-permute-done | bytes 409632 | tf_op jit(solution)/shard_map/ppermute | solution.py:240
  163.8 8.2 %collective-permute-start.20 = (bf16[80,2560]{1,0:T(8,128)(2,1)S(1)}, bf16[80,2560]{1,0:T(8,128)(2,1)S(1)}, u32[]{:S(2)}, u32[]{:S(2)}) collective-permute-start(bf16[80,2560]{1,0:T(8,128)(2,1)S(1)} %broadcast_select_fusion.1), channel_id=1, source_target_pairs={{0,16},{1,17},{2,18},{3,19},{4,20},{5,21},{6,22},{7,23},{8,24},{9,... | collective-permute-start | bytes 1228808 | tf_op jit(solution)/shard_map/ppermute | solution.py:243
  172.9 11.3 %collective-permute-start.29 = (bf16[80,2560]{1,0:T(8,128)(2,1)}, bf16[80,2560]{1,0:T(8,128)(2,1)S(1)}, u32[]{:S(2)}, u32[]{:S(2)}) collective-permute-start(bf16[80,2560]{1,0:T(8,128)(2,1)} %broadcast_select_fusion), channel_id=1, source_target_pairs={{0,16},{1,17},{2,18},{3,19},{4,20},{5,21},{6,22},{7,23},{8,24},{9,... | collective-permute-start | bytes 1228808 | tf_op jit(solution)/shard_map/ppermute | solution.py:243
  (73 shorter events, 19.2 us)
Async XLA Ops:
  9.5 23.9 %collective-permute-start.4 = (bf16[320,1024]{1,0:T(8,128)(2,1)S(1)}, bf16[320,1024]{1,0:T(8,128)(2,1)S(1)}, u32[]{:S(2)}, u32[]{:S(2)}) collective-permute-start(bf16[320,1024]{1,0:T(8,128)(2,1)S(1)} %pad_maximum_fusion.1), channel_id=1, source_target_pairs={{0,0},{1,1},{2,2},{3,3},{4,16},{5,17},{6,18},{7,19},{16,4},{17,5},... | collective-permute-start | bytes 1966088 | tf_op jit(solution)/shard_map/ppermute | solution.py:175
  10.4 11.2 %collective-permute-start.2 = (bf16[320,512]{1,0:T(8,128)(2,1)S(1)}, bf16[320,512]{1,0:T(8,128)(2,1)S(1)}, u32[]{:S(2)}, u32[]{:S(2)}) collective-permute-start(bf16[320,512]{1,0:T(8,128)(2,1)S(1)} %copy-done.5), channel_id=1, source_target_pairs={{0,2},{1,3},{2,0},{3,1},{4,18},{5,19},{6,16},{7,17},{16,6},{17,7},... | collective-permute-start | bytes 983048 | tf_op jit(solution)/shard_map/ppermute | solution.py:175
  12.0 16.2 %collective-permute-start.3 = (bf16[320,512]{1,0:T(8,128)(2,1)S(1)}, bf16[320,512]{1,0:T(8,128)(2,1)S(1)}, u32[]{:S(2)}, u32[]{:S(2)}) collective-permute-start(bf16[320,512]{1,0:T(8,128)(2,1)S(1)} %get-tuple-element.61), channel_id=1, source_target_pairs={{0,3},{1,2},{2,1},{3,0},{4,19},{5,18},{6,17},{7,16},{16,7},{17,6},... | collective-permute-start | bytes 983048 | tf_op jit(solution)/shard_map/ppermute | solution.py:175
  12.2 33.0 %collective-permute-start.9 = (bf16[320,1024]{1,0:T(8,128)(2,1)S(1)}, bf16[320,1024]{1,0:T(8,128)(2,1)S(1)}, u32[]{:S(2)}, u32[]{:S(2)}) collective-permute-start(bf16[320,1024]{1,0:T(8,128)(2,1)S(1)} %pad_maximum_fusion.3), channel_id=1, source_target_pairs={{0,2},{1,3},{2,0},{3,1},{4,18},{5,19},{6,16},{7,17},{16,6},{17,7},... | collective-permute-start | bytes 1966088 | tf_op jit(solution)/shard_map/ppermute | solution.py:175
  16.2 29.0 %collective-permute-start.7 = (bf16[320,1024]{1,0:T(8,128)(2,1)S(1)}, bf16[320,1024]{1,0:T(8,128)(2,1)S(1)}, u32[]{:S(2)}, u32[]{:S(2)}) collective-permute-start(bf16[320,1024]{1,0:T(8,128)(2,1)S(1)} %pad_maximum_fusion.2), channel_id=1, source_target_pairs={{0,1},{1,0},{2,3},{3,2},{4,17},{5,16},{6,19},{7,18},{16,5},{17,4},... | collective-permute-start | bytes 1966088 | tf_op jit(solution)/shard_map/ppermute | solution.py:175
  21.7 39.9 %collective-permute-start.14 = (bf16[320,1024]{1,0:T(8,128)(2,1)S(1)}, bf16[320,1024]{1,0:T(8,128)(2,1)S(1)}, u32[]{:S(2)}, u32[]{:S(2)}) collective-permute-start(bf16[320,1024]{1,0:T(8,128)(2,1)S(1)} %pad_maximum_fusion.4), channel_id=1, source_target_pairs={{0,3},{1,2},{2,1},{3,0},{4,19},{5,18},{6,17},{7,16},{16,7},{17,6},... | collective-permute-start | bytes 1966088 | tf_op jit(solution)/shard_map/ppermute | solution.py:175
  30.6 56.0 %collective-permute-start.10 = (bf16[4,320,512]{2,1,0:T(8,128)(2,1)}, bf16[4,320,512]{2,1,0:T(8,128)(2,1)}, u32[]{:S(2)}, u32[]{:S(2)}) collective-permute-start(bf16[4,320,512]{2,1,0:T(8,128)(2,1)} %pad_maximum_fusion.refs_6_), channel_id=1, source_target_pairs={{0,8},{8,0},{1,9},{9,1},{2,10},{10,2},{3,11},{11,3},{4,12},{12,4},... | collective-permute-start | bytes 3932168 | tf_op jit(solution)/shard_map/ppermute | solution.py:195
  61.7 42.8 %collective-permute-start.15 = (bf16[4,320,1024]{2,1,0:T(8,128)(2,1)S(1)}, bf16[4,320,1024]{2,1,0:T(8,128)(2,1)}, u32[]{:S(2)}, u32[]{:S(2)}) collective-permute-start(bf16[4,320,1024]{2,1,0:T(8,128)(2,1)S(1)} %shard_map.82.refs_4_), channel_id=1, source_target_pairs={{0,16},{16,0},{1,17},{17,1},{2,18},{18,2},{3,19},{19,3},{4,20},{20... | collective-permute-start | bytes 7864328 | tf_op jit(solution)/shard_map/ppermute | solution.py:178
  86.4 11.3 %collective-permute-start.5 = (bf16[4,320,512]{2,1,0:T(8,128)(2,1)}, bf16[4,320,512]{2,1,0:T(8,128)(2,1)}, u32[]{:S(2)}, u32[]{:S(2)}) collective-permute-start(bf16[4,320,512]{2,1,0:T(8,128)(2,1)} %pad_maximum_fusion.refs_6_), channel_id=1, source_target_pairs={{0,16},{16,0},{1,17},{17,1},{2,18},{18,2},{3,19},{19,3},{4,20},{20... | collective-permute-start | bytes 3932168 | tf_op jit(solution)/shard_map/ppermute | solution.py:178
  86.5 12.8 %collective-permute-start.11 = (bf16[4,320,512]{2,1,0:T(8,128)(2,1)}, bf16[4,320,512]{2,1,0:T(8,128)(2,1)}, u32[]{:S(2)}, u32[]{:S(2)}) collective-permute-start(bf16[4,320,512]{2,1,0:T(8,128)(2,1)} %collective-permute-done.10.refs_7_), channel_id=1, source_target_pairs={{0,16},{16,0},{1,17},{17,1},{2,18},{18,2},{3,19},{19,3},{4,20},{20... | collective-permute-start | bytes 3932168 | tf_op jit(solution)/shard_map/ppermute | solution.py:178
  86.9 18.9 %collective-permute-start.13 = (bf16[80,1024]{1,0:T(8,128)(2,1)}, bf16[80,1024]{1,0:T(8,128)(2,1)S(1)}, u32[]{:S(2)}, u32[]{:S(2)}) collective-permute-start(bf16[80,1024]{1,0:T(8,128)(2,1)} %get-tuple-element.42), channel_id=1, source_target_pairs={{0,3},{1,2},{2,1},{3,0},{4,19},{5,18},{6,17},{7,16},{16,7},{17,6},... | collective-permute-start | bytes 491528 | tf_op jit(solution)/shard_map/ppermute | solution.py:175
  104.5 17.1 %collective-permute-start.22 = (bf16[80,1024]{1,0:T(8,128)(2,1)S(1)}, bf16[80,1024]{1,0:T(8,128)(2,1)S(1)}, u32[]{:S(2)}, u32[]{:S(2)}) collective-permute-start(bf16[80,1024]{1,0:T(8,128)(2,1)S(1)} %get-tuple-element.77), channel_id=1, source_target_pairs={{0,1},{1,0},{2,3},{3,2},{4,17},{5,16},{6,19},{7,18},{16,5},{17,4},... | collective-permute-start | bytes 491528 | tf_op jit(solution)/shard_map/ppermute | solution.py:175
  105.8 16.8 %collective-permute-start.23 = (bf16[80,1024]{1,0:T(8,128)(2,1)S(1)}, bf16[80,1024]{1,0:T(8,128)(2,1)S(1)}, u32[]{:S(2)}, u32[]{:S(2)}) collective-permute-start(bf16[80,1024]{1,0:T(8,128)(2,1)S(1)} %get-tuple-element.76), channel_id=1, source_target_pairs={{0,2},{1,3},{2,0},{3,1},{4,18},{5,19},{6,16},{7,17},{16,6},{17,7},... | collective-permute-start | bytes 491528 | tf_op jit(solution)/shard_map/ppermute | solution.py:175
  105.8 18.1 %collective-permute-start.24 = (bf16[80,1024]{1,0:T(8,128)(2,1)S(1)}, bf16[80,1024]{1,0:T(8,128)(2,1)S(1)}, u32[]{:S(2)}, u32[]{:S(2)}) collective-permute-start(bf16[80,1024]{1,0:T(8,128)(2,1)S(1)} %get-tuple-element.75), channel_id=1, source_target_pairs={{0,3},{1,2},{2,1},{3,0},{4,19},{5,18},{6,17},{7,16},{16,7},{17,6},... | collective-permute-start | bytes 491528 | tf_op jit(solution)/shard_map/ppermute | solution.py:175
  108.1 15.9 %collective-permute-start.21 = (bf16[80,1024]{1,0:T(8,128)(2,1)S(1)}, bf16[80,1024]{1,0:T(8,128)(2,1)S(1)}, u32[]{:S(2)}, u32[]{:S(2)}) collective-permute-start(bf16[80,1024]{1,0:T(8,128)(2,1)S(1)} %get-tuple-element.54), channel_id=1, source_target_pairs={{0,0},{1,1},{2,2},{3,3},{4,16},{5,17},{6,18},{7,19},{16,4},{17,5},... | collective-permute-start | bytes 491528 | tf_op jit(solution)/shard_map/ppermute | solution.py:175
  120.3 17.5 %collective-permute-start.16 = (bf16[80,2560]{1,0:T(8,128)(2,1)S(1)}, bf16[80,2560]{1,0:T(8,128)(2,1)S(1)}, u32[]{:S(2)}, u32[]{:S(2)}) collective-permute-start(bf16[80,2560]{1,0:T(8,128)(2,1)S(1)} %get-tuple-element.51), channel_id=1, source_target_pairs={{0,1},{1,0},{2,3},{3,2},{4,5},{5,4},{6,7},{7,6},{8,9},{9,8},{10,11... | collective-permute-start | bytes 1228808 | tf_op jit(solution)/shard_map/ppermute | solution.py:240
  121.7 17.5 %collective-permute-start.17 = (bf16[80,2560]{1,0:T(8,128)(2,1)S(1)}, bf16[80,2560]{1,0:T(8,128)(2,1)S(1)}, u32[]{:S(2)}, u32[]{:S(2)}) collective-permute-start(bf16[80,2560]{1,0:T(8,128)(2,1)S(1)} %get-tuple-element.52), channel_id=1, source_target_pairs={{0,2},{1,3},{2,0},{3,1},{4,6},{5,7},{6,4},{7,5},{8,10},{9,11},{10,... | collective-permute-start | bytes 1228808 | tf_op jit(solution)/shard_map/ppermute | solution.py:240
  122.6 17.9 %collective-permute-start.18 = (bf16[80,2560]{1,0:T(8,128)(2,1)S(1)}, bf16[80,2560]{1,0:T(8,128)(2,1)S(1)}, u32[]{:S(2)}, u32[]{:S(2)}) collective-permute-start(bf16[80,2560]{1,0:T(8,128)(2,1)S(1)} %get-tuple-element.53), channel_id=1, source_target_pairs={{0,3},{1,2},{2,1},{3,0},{4,7},{5,6},{6,5},{7,4},{8,11},{9,10},{10,... | collective-permute-start | bytes 1228808 | tf_op jit(solution)/shard_map/ppermute | solution.py:240
  135.6 15.7 %collective-permute-start.25 = (bf16[80,2560]{1,0:T(8,128)(2,1)S(1)}, bf16[80,2560]{1,0:T(8,128)(2,1)S(1)}, u32[]{:S(2)}, u32[]{:S(2)}) collective-permute-start(bf16[80,2560]{1,0:T(8,128)(2,1)S(1)} %get-tuple-element.56), channel_id=1, source_target_pairs={{0,1},{1,0},{2,3},{3,2},{4,5},{5,4},{6,7},{7,6},{8,9},{9,8},{10,11... | collective-permute-start | bytes 1228808 | tf_op jit(solution)/shard_map/ppermute | solution.py:240
  136.9 14.4 %collective-permute-start.26 = (bf16[80,2560]{1,0:T(8,128)(2,1)S(1)}, bf16[80,2560]{1,0:T(8,128)(2,1)S(1)}, u32[]{:S(2)}, u32[]{:S(2)}) collective-permute-start(bf16[80,2560]{1,0:T(8,128)(2,1)S(1)} %get-tuple-element.57), channel_id=1, source_target_pairs={{0,2},{1,3},{2,0},{3,1},{4,6},{5,7},{6,4},{7,5},{8,10},{9,11},{10,... | collective-permute-start | bytes 1228808 | tf_op jit(solution)/shard_map/ppermute | solution.py:240
  137.8 24.9 %collective-permute-start.27 = (bf16[80,2560]{1,0:T(8,128)(2,1)S(1)}, bf16[80,2560]{1,0:T(8,128)(2,1)S(1)}, u32[]{:S(2)}, u32[]{:S(2)}) collective-permute-start(bf16[80,2560]{1,0:T(8,128)(2,1)S(1)} %get-tuple-element.58), channel_id=1, source_target_pairs={{0,3},{1,2},{2,1},{3,0},{4,7},{5,6},{6,5},{7,4},{8,11},{9,10},{10,... | collective-permute-start | bytes 1228808 | tf_op jit(solution)/shard_map/ppermute | solution.py:240
  140.7 23.0 %collective-permute-start.19 = (bf16[80,2560]{1,0:T(8,128)(2,1)S(1)}, bf16[80,2560]{1,0:T(8,128)(2,1)S(1)}, u32[]{:S(2)}, u32[]{:S(2)}) collective-permute-start(bf16[80,2560]{1,0:T(8,128)(2,1)S(1)} %add_convert_fusion.3), channel_id=1, source_target_pairs={{0,0},{1,1},{2,2},{3,3},{4,16},{5,17},{6,18},{7,19},{16,4},{17,5},... | collective-permute-start | bytes 1228808 | tf_op jit(solution)/shard_map/ppermute | solution.py:175
  163.8 21.2 %collective-permute-start.20 = (bf16[80,2560]{1,0:T(8,128)(2,1)S(1)}, bf16[80,2560]{1,0:T(8,128)(2,1)S(1)}, u32[]{:S(2)}, u32[]{:S(2)}) collective-permute-start(bf16[80,2560]{1,0:T(8,128)(2,1)S(1)} %broadcast_select_fusion.1), channel_id=1, source_target_pairs={{0,16},{1,17},{2,18},{3,19},{4,20},{5,21},{6,22},{7,23},{8,24},{9,... | collective-permute-start | bytes 1228808 | tf_op jit(solution)/shard_map/ppermute | solution.py:243
  172.9 12.9 %collective-permute-start.29 = (bf16[80,2560]{1,0:T(8,128)(2,1)}, bf16[80,2560]{1,0:T(8,128)(2,1)S(1)}, u32[]{:S(2)}, u32[]{:S(2)}) collective-permute-start(bf16[80,2560]{1,0:T(8,128)(2,1)} %broadcast_select_fusion), channel_id=1, source_target_pairs={{0,16},{1,17},{2,18},{3,19},{4,20},{5,21},{6,22},{7,23},{8,24},{9,... | collective-permute-start | bytes 1228808 | tf_op jit(solution)/shard_map/ppermute | solution.py:243
  (13 other events, 145.1 us)

commit v3 on v2

--- a/solution.py
+++ b/solution.py
@@ -8,17 +8,18 @@
 from jax.sharding import PartitionSpec as P
 
 HEADS = 32
-HIDDEN = 40_000_000_000
-CHUNKS = 2
-JOINED = 2
+CHUNKS = (1, 1)
+JOINED = 4
 
 
 def attend_project(
-    query_parts, chunk_rows, context, weight_blocks, where, head_size
+    query_parts, context, weight_blocks, where, head_size
 ):
     homes, home_rows, features = context[0].shape
     home_rows = home_rows // 2
-    steps = features // head_size // JOINED
+    chunk_rows = query_parts[0].shape[0]
+    joined = math.gcd(features // head_size, JOINED)
+    steps = features // head_size // joined
     key_rows = homes * home_rows
     block_columns, share = weight_blocks[0].shape[1:]
     columns = 2 * homes * block_columns
@@ -55,34 +56,52 @@
         def _():
             each_fetch(lambda copy: copy.start())
 
-        for index in range(JOINED):
-            cols = slice(index * head_size, (index + 1) * head_size)
-            near_keys, far_keys, near_values, far_values = (
-                ref[:, kind * home_rows : (kind + 1) * home_rows, cols].reshape(key_rows, head_size)
-                for kind in range(2)
+        def columns_of(index):
+            return slice(index * head_size, (index + 1) * head_size)
+
+        def held(kind, index):
+            return [
+                ref[:, kind * home_rows : (kind + 1) * home_rows, columns_of(index)].reshape(key_rows, head_size)
                 for ref in context_refs
+            ]
+
+        def scored(first, index):
+            query = jnp.concatenate([ref[:, columns_of(index)] for ref in q_refs[first : first + together]], axis=0)
+            return [
+                lax.dot_general(query, keys, contract, preferred_element_type=jnp.float32)
+                for keys in held(0, index)
+            ]
+
+        def weighed(scores):
+            peaks = [jnp.max(score, axis=1, keepdims=True) for score in scores]
+            peak = jnp.maximum(*peaks)
+            expo = [jnp.exp2((score - peak) * scale) for score in scores]
+            total = sum(jnp.sum(part, axis=1, keepdims=True) for part in expo)
+            return [part.astype(jnp.bfloat16) for part in expo], total
+
+        def mix(first, index, probs, total):
+            near, far = (
+                jnp.dot(prob, values, preferred_element_type=jnp.float32)
+                for prob, values in zip(probs, held(1, index))
             )
-            for first in range(0, homes, together):
-                query = jnp.concatenate([ref[:, cols] for ref in q_refs[first : first + together]], axis=0)
-                near = lax.dot_general(query, near_keys, contract, preferred_element_type=jnp.float32)
-                far = lax.dot_general(query, far_keys, contract, preferred_element_type=jnp.float32)
-                peak = jnp.maximum(
-                    jnp.max(near, axis=1, keepdims=True), jnp.max(far, axis=1, keepdims=True)
-                )
-                near = jnp.exp2((near - peak) * scale)
-                far = jnp.exp2((far - peak) * scale)
-                total = jnp.sum(near, axis=1, keepdims=True) + jnp.sum(far, axis=1, keepdims=True)
-                mixed = jnp.dot(near.astype(jnp.bfloat16), near_values, preferred_element_type=jnp.float32)
-                mixed += jnp.dot(far.astype(jnp.bfloat16), far_values, preferred_element_type=jnp.float32)
-                mixed = (mixed / total).astype(jnp.bfloat16)
-                for at in range(steps):
-
-                    @pl.when(step == at)
-                    def _():
-                        begin = (at * JOINED + index) * head_size
-                        attended[
-                            first * chunk_rows : first * chunk_rows + block_rows, begin : begin + head_size
-                        ] = mixed
+            mixed = ((near + far) / total).astype(jnp.bfloat16)
+            for at in range(steps):
+
+                @pl.when(step == at)
+                def _():
+                    begin = (at * joined + index) * head_size
+                    attended[first * chunk_rows : first * chunk_rows + block_rows, begin : begin + head_size] = mixed
+
+        work = [(first, index) for first in range(0, homes, together) for index in range(joined)]
+        scores = scored(*work[0])
+        waiting = None
+        for position, item in enumerate(work):
+            ahead = scored(*work[position + 1]) if position + 1 < len(work) else None
+            current = weighed(scores)
+            if waiting is not None:
+                mix(*work[position - 1], *waiting)
+            scores, waiting = ahead, current
+        mix(*work[-1], *waiting)
 
         @pl.when(step == steps - 1)
         def _():
@@ -97,7 +116,7 @@
                 for at, ref in enumerate(out_refs[first : first + together]):
                     ref[...] = product[at * chunk_rows : (at + 1) * chunk_rows].astype(ref.dtype)
 
-    width = JOINED * head_size
+    width = joined * head_size
     stacked = pl.BlockSpec((homes, 2 * home_rows, width), lambda step, _: (0, 0, step))
     return pl.pallas_call(
         body,
@@ -183,8 +202,8 @@
     def mine(array, step):
         return lax.dynamic_slice_in_dim(array, (spot ^ step) * features, features, axis=-1)
 
-    chunk_rows = rows // CHUNKS
-    pieces = [slice(chunk * chunk_rows, (chunk + 1) * chunk_rows) for chunk in range(CHUNKS)]
+    ends = [rows * sum(CHUNKS[: chunk + 1]) // sum(CHUNKS) for chunk in range(len(CHUNKS))]
+    pieces = [slice(first, last) for first, last in zip([0, *ends], ends)]
 
     share = features // shares
     weight_parts = [
@@ -206,19 +225,20 @@
     for step in range(half):
         at = min(step, half - 2)
         queries[0][step], pair_parts[at] = after(queries[0][step], pair_parts[at])
-    queries[0][0], own_far = after(queries[0][0], own_far)
-    queries[0][2], other_far = after(queries[0][2], other_far)
+    queries[0][2], own_far = after(queries[0][2], own_far)
     query_parts = [send(part, step) for step, part in enumerate(queries[0])]
     near = gathered(pair_parts, 2 * rows, 0)
     far = sibling(near)
+    queries[1][0], other_far = after(queries[1][0], other_far)
     queries[1][0], far = after(queries[1][0], far)
-    query_parts = [query_parts, [send(part, step) for step, part in enumerate(queries[1])]]
+    query_parts = [query_parts] + [
+        [send(part, step) for step, part in enumerate(parts)] for parts in queries[1:]
+    ]
     weight_blocks = (own, other, own_far, other_far)
 
     partials = [
         attend_project(
             parts,
-            chunk_rows,
             (near, far),
             weight_blocks,
             where,
@@ -232,22 +252,23 @@
         jnp.where(step_ids == step_index[0], step_gates, jnp.zeros_like(step_gates)), axis=0
     )
     is_main = branch == 1
-    outs = []
+    wanted = control_mask[:, None] == 1
+    result = jnp.zeros_like(residual)
     for piece, partial in zip(pieces, partials):
         summed = partial[0]
         for step in range(1, half):
             swap = [(s, s ^ step) for s in range(count)]
             summed = summed + lax.ppermute(partial[step], "seq", swap).astype(jnp.float32)
         projected = send(summed.astype(jnp.bfloat16), 0)
-        hint = jnp.where(control_mask[piece, None] == 1, projected, jnp.zeros_like(projected))
-        hint_moved = lax.ppermute(hint, "branch", [(0, 1)])
+        context_rows = jnp.where(is_main, lax.ppermute(projected, "branch", [(0, 1)]), projected)
+        hint = jnp.where(wanted[piece], context_rows, jnp.zeros_like(projected))
         mixed = (
             residual[piece].astype(jnp.float32)
             + gate_row[None, :] * projected.astype(jnp.float32)
-            + hint_moved.astype(jnp.float32)
+            + hint.astype(jnp.float32)
         ).astype(jnp.bfloat16)
-        outs.append(jnp.where(is_main, mixed, hint))
-    return jnp.concatenate(outs, axis=0)[None]
+        result = lax.dynamic_update_slice(result, jnp.where(is_main, mixed, hint), (piece.start, 0))
+    return result[None]
 
 
 def solution(mesh):

time: 188 us -> 184 us (0.979)
  Pallas kernels: 23.3 us -> 20 us
  waiting for transfers between devices: 61.2 us -> 64.2 us
  starting transfers between devices: 92.6 us -> 89.9 us
    pallas_call x2, Pallas kernels: 23.1 us -> 19.8 us  [attend_project(): pl.pallas_call(body, grid_spec=pltpu.PrefetchScalarGridSpec(num_scalar_pr...]
    ppermute x6, waiting for transfers between devices: 22.7 us -> 24.6 us  [per_device(): lax.ppermute(partial[step], 'seq', swap).astype(jnp.float32)]
  transfers between devices with their start and end apart: 30 -> 30, of which waited for: 8 -> 9; matrix products, arithmetic and copies ran while one was open for 3% -> 2% of each run, Pallas kernels for 12% -> 11%
where the time goes in v3:
time: 184 us; the launch traced here: 183 us
  starting transfers between devices  89.9 us (49%)
  waiting for transfers between devices  64.2 us (35%)
  Pallas kernels  20 us (11%)
  other arithmetic  4.54 us (2%)
  local copies, waits for them, and re-layouts  3.73 us (2%)
    ppermute x18, waiting for transfers between devices, send(): return lax.ppermute(array, pair, crossing(step))  38.3 us
    ppermute x18, starting transfers between devices, send(): return lax.ppermute(array, pair, crossing(step))  37.6 us
    ppermute x3, starting transfers between devices, sibling(): return lax.ppermute(array, 'branch', [(0, 1), (1, 0)])  25.2 us
    ppermute x6, waiting for transfers between devices, per_device(): lax.ppermute(partial[step], 'seq', swap).astype(jnp.float32)  24.6 us
    pallas_call x2, Pallas kernels, attend_project(): pl.pallas_call(body, grid_spec=pltpu.PrefetchScalarGridSpec(num_scalar_pr...  19.8 us
    ppermute x2, starting transfers between devices, per_device(): lax.ppermute(projected, 'branch', [(0, 1)])  18.1 us
    ppermute x6, starting transfers between devices, per_device(): lax.ppermute(partial[step], 'seq', swap).astype(jnp.float32)  7.11 us
  transfers between devices with their start and end apart: 30, of which 9 were waited for; matrix products, arithmetic and copies ran while one was open for 2% of the time, Pallas kernels for 11%

profile of v3, /device:TPU:0, one launch (start us, length us, event | category | flops | bytes accessed | tf_op | source)
XLA Modules:
  0.0 183.2 jit_solution(6110156434827506848)
XLA Ops:
  0.0 2.4 %dynamic-slice_bitcast_fusion.11 = (bf16[320,512]{1,0:T(8,128)(2,1)}, bf16[320,512]{1,0:T(8,128)(2,1)}, bf16[320,512]{1,0:T(8,128)(2,1)S(1)}, bf16[320,512]{1,0:T(8,128)(2,1)}) fusion(bf16[1,4096,320]{1,2,0:T(8,128)(2,1)} %param.15, s32[]{:T(128)S(6)} %select_n.78, s32[]{:T(128)S(6)} %select_n.79, s32[]{:T(128)S(6)} %select_n.81, s32[]{:T(128)S(6)} %select_n.80), kind=kLoop, calls=%fused_computation.24 | loop fusion | bytes 2621456 | tf_op jit(solution)/shard_map/dynamic_slice | solution.py:210
  2.4 2.9 %collective-permute-start.1 = (bf16[320,512]{1,0:T(8,128)(2,1)}, bf16[320,512]{1,0:T(8,128)(2,1)S(1)}, u32[]{:S(2)}, u32[]{:S(2)}) collective-permute-start(bf16[320,512]{1,0:T(8,128)(2,1)} %get-tuple-element.60), channel_id=1, source_target_pairs={{0,1},{1,0},{2,3},{3,2},{4,17},{5,16},{6,19},{7,18},{16,5},{17,4},... | collective-permute-start | bytes 983048 | tf_op jit(solution)/shard_map/ppermute | solution.py:194
  5.3 3.9 %collective-permute-start = (bf16[320,512]{1,0:T(8,128)(2,1)}, bf16[320,512]{1,0:T(8,128)(2,1)}, u32[]{:S(2)}, u32[]{:S(2)}) collective-permute-start(bf16[320,512]{1,0:T(8,128)(2,1)} %get-tuple-element.59), channel_id=1, source_target_pairs={{0,0},{1,1},{2,2},{3,3},{4,16},{5,17},{6,18},{7,19},{16,4},{17,5},... | collective-permute-start | bytes 983048 | tf_op jit(solution)/shard_map/ppermute | solution.py:194
  10.4 1.6 collective-permute-start.2
  12.2 4.0 %collective-permute-start.8 = (bf16[320,1024]{1,0:T(8,128)(2,1)S(1)}, bf16[320,1024]{1,0:T(8,128)(2,1)S(1)}, u32[]{:S(2)}, u32[]{:S(2)}) collective-permute-start(bf16[320,1024]{1,0:T(8,128)(2,1)S(1)} %pad_maximum_fusion.3), channel_id=1, source_target_pairs={{0,2},{1,3},{2,0},{3,1},{4,18},{5,19},{6,16},{7,17},{16,6},{17,7},... | collective-permute-start | bytes 1966088 | tf_op jit(solution)/shard_map/ppermute | solution.py:194
  17.7 4.0 %collective-permute-done.2 = bf16[320,512]{1,0:T(8,128)(2,1)S(1)} collective-permute-done((bf16[320,512]{1,0:T(8,128)(2,1)S(1)}, bf16[320,512]{1,0:T(8,128)(2,1)S(1)}, u32[]{:S(2)}, u32[]{:S(2)}) %collective-permute-start.2) | collective-permute-done | bytes 327712 | tf_op jit(solution)/shard_map/ppermute | solution.py:194
  22.6 5.6 %collective-permute-done.3 = bf16[320,512]{1,0:T(8,128)(2,1)S(1)} collective-permute-done((bf16[320,512]{1,0:T(8,128)(2,1)S(1)}, bf16[320,512]{1,0:T(8,128)(2,1)S(1)}, u32[]{:S(2)}, u32[]{:S(2)}) %collective-permute-start.3) | collective-permute-done | bytes 327712 | tf_op jit(solution)/shard_map/ppermute | solution.py:194
  28.3 2.3 %pad_maximum_fusion.refs_6_ = bf16[4,320,512]{2,1,0:T(8,128)(2,1)} fusion(bf16[1,320,512]{2,1,0:T(8,128)(2,1)S(1)} %bitcast.61, bf16[1,320,512]{2,1,0:T(8,128)(2,1)S(1)} %bitcast.60, bf16[1,320,512]{2,1,0:T(8,128)(2,1)S(1)} %bitcast.59, bf16[1,320,512]{2,1,0:T(8,128)(2,1)} %bitcast.7), kind=kLoop, calls=%fused_computation | loop fusion | flops 1966080 | bytes 2621440 | tf_op jit(solution)/shard_map/stack | solution.py:213
  30.6 1.9 %collective-permute-start.13 = (bf16[4,320,512]{2,1,0:T(8,128)(2,1)}, bf16[4,320,512]{2,1,0:T(8,128)(2,1)}, u32[]{:S(2)}, u32[]{:S(2)}) collective-permute-start(bf16[4,320,512]{2,1,0:T(8,128)(2,1)} %pad_maximum_fusion.refs_6_), channel_id=1, source_target_pairs={{0,8},{8,0},{1,9},{9,1},{2,10},{10,2},{3,11},{11,3},{4,12},{12,4},... | collective-permute-start | bytes 3932168 | tf_op jit(solution)/shard_map/ppermute | solution.py:214
  33.4 11.9 %collective-permute-done.8.refs_2_ = bf16[320,1024]{1,0:T(8,128)(2,1)S(1)} collective-permute-done((bf16[320,1024]{1,0:T(8,128)(2,1)S(1)}, bf16[320,1024]{1,0:T(8,128)(2,1)S(1)}, u32[]{:S(2)}, u32[]{:S(2)}) %collective-permute-start.8) | collective-permute-done | bytes 655392 | tf_op jit(solution)/shard_map/ppermute | solution.py:194
  45.3 16.3 %collective-permute-done.12.refs_3_ = bf16[320,1024]{1,0:T(8,128)(2,1)S(1)} collective-permute-done((bf16[320,1024]{1,0:T(8,128)(2,1)S(1)}, bf16[320,1024]{1,0:T(8,128)(2,1)S(1)}, u32[]{:S(2)}, u32[]{:S(2)}) %collective-permute-start.12) | collective-permute-done | bytes 655392 | tf_op jit(solution)/shard_map/ppermute | solution.py:194
  61.7 24.7 %collective-permute-start.15 = (bf16[4,320,1024]{2,1,0:T(8,128)(2,1)S(1)}, bf16[4,320,1024]{2,1,0:T(8,128)(2,1)}, u32[]{:S(2)}, u32[]{:S(2)}) collective-permute-start(bf16[4,320,1024]{2,1,0:T(8,128)(2,1)S(1)} %shard_map.82.refs_4_), channel_id=1, source_target_pairs={{0,16},{16,0},{1,17},{17,1},{2,18},{18,2},{3,19},{19,3},{4,20},{20... | collective-permute-start | bytes 7864328 | tf_op jit(solution)/shard_map/ppermute | solution.py:197
  88.5 8.3 %collective-permute-start.11 = (bf16[80,1024]{1,0:T(8,128)(2,1)}, bf16[80,1024]{1,0:T(8,128)(2,1)S(1)}, u32[]{:S(2)}, u32[]{:S(2)}) collective-permute-start(bf16[80,1024]{1,0:T(8,128)(2,1)} %get-tuple-element.41), channel_id=1, source_target_pairs={{0,3},{1,2},{2,1},{3,0},{4,19},{5,18},{6,17},{7,16},{16,7},{17,6},... | collective-permute-start | bytes 491528 | tf_op jit(solution)/shard_map/ppermute | solution.py:194
  97.7 5.1 %collective-permute-start.10 = (bf16[80,1024]{1,0:T(8,128)(2,1)S(1)}, bf16[80,1024]{1,0:T(8,128)(2,1)S(1)}, u32[]{:S(2)}, u32[]{:S(2)}) collective-permute-start(bf16[80,1024]{1,0:T(8,128)(2,1)S(1)} %get-tuple-element.39), channel_id=1, source_target_pairs={{0,2},{1,3},{2,0},{3,1},{4,18},{5,19},{6,16},{7,17},{16,6},{17,7},... | collective-permute-start | bytes 491528 | tf_op jit(solution)/shard_map/ppermute | solution.py:194
  104.1 2.4 %collective-permute-start.24 = (bf16[80,1024]{1,0:T(8,128)(2,1)S(1)}, bf16[80,1024]{1,0:T(8,128)(2,1)S(1)}, u32[]{:S(2)}, u32[]{:S(2)}) collective-permute-start(bf16[80,1024]{1,0:T(8,128)(2,1)S(1)} %get-tuple-element.75), channel_id=1, source_target_pairs={{0,3},{1,2},{2,1},{3,0},{4,19},{5,18},{6,17},{7,16},{16,7},{17,6},... | collective-permute-start | bytes 491528 | tf_op jit(solution)/shard_map/ppermute | solution.py:194
  107.8 9.9 %shard_map.83 = (f32[80,2560]{1,0:T(8,128)S(1)}, bf16[80,2560]{1,0:T(8,128)(2,1)S(1)}, bf16[80,2560]{1,0:T(8,128)(2,1)S(1)}, bf16[80,2560]{1,0:T(8,128)(2,1)S(1)}) custom-call(s32[3]{0:T(128)S(1)} %pad_add_fusion.where, bf16[80,1024]{1,0:T(8,128)(2,1)S(1)} %collective-permute-done.5.refs_0_, bf16[80,1024]{1,0:T(8,128)(2,1)S(1)} %collective-permute-done.7.refs_1_, ...), custom_call_target="tpu_custom_call" | custom-call | flops 3355443200 | bytes 10485760 | tf_op jit(solution)/shard_map/pallas_call | solution.py:121
  118.9 2.1 %collective-permute-start.17 = (bf16[80,2560]{1,0:T(8,128)(2,1)S(1)}, bf16[80,2560]{1,0:T(8,128)(2,1)S(1)}, u32[]{:S(2)}, u32[]{:S(2)}) collective-permute-start(bf16[80,2560]{1,0:T(8,128)(2,1)S(1)} %get-tuple-element.52), channel_id=1, source_target_pairs={{0,2},{1,3},{2,0},{3,1},{4,6},{5,7},{6,4},{7,5},{8,10},{9,11},{10,... | collective-permute-start | bytes 1228808 | tf_op jit(solution)/shard_map/ppermute | solution.py:261
  121.3 9.9 %shard_map.84 = (f32[80,2560]{1,0:T(8,128)S(1)}, bf16[80,2560]{1,0:T(8,128)(2,1)S(1)}, bf16[80,2560]{1,0:T(8,128)(2,1)S(1)}, bf16[80,2560]{1,0:T(8,128)(2,1)S(1)}) custom-call(s32[3]{0:T(128)S(1)} %pad_add_fusion.where, bf16[80,1024]{1,0:T(8,128)(2,1)S(1)} %collective-permute-done.21.refs_0_, bf16[80,1024]{1,0:T(8,128)(2,1)S(1)} %collective-permute-done.22.refs_1_, ...), custom_call_target="tpu_custom_call" | custom-call | flops 3355443200 | bytes 10485760 | tf_op jit(solution)/shard_map/pallas_call | solution.py:121
  132.4 2.0 %collective-permute-start.26 = (bf16[80,2560]{1,0:T(8,128)(2,1)S(1)}, bf16[80,2560]{1,0:T(8,128)(2,1)S(1)}, u32[]{:S(2)}, u32[]{:S(2)}) collective-permute-start(bf16[80,2560]{1,0:T(8,128)(2,1)S(1)} %get-tuple-element.57), channel_id=1, source_target_pairs={{0,2},{1,3},{2,0},{3,1},{4,6},{5,7},{6,4},{7,5},{8,10},{9,11},{10,... | collective-permute-start | bytes 1228808 | tf_op jit(solution)/shard_map/ppermute | solution.py:261
  134.8 3.7 %collective-permute-done.18 = bf16[80,2560]{1,0:T(8,128)(2,1)S(1)} collective-permute-done((bf16[80,2560]{1,0:T(8,128)(2,1)S(1)}, bf16[80,2560]{1,0:T(8,128)(2,1)S(1)}, u32[]{:S(2)}, u32[]{:S(2)}) %collective-permute-start.18) | collective-permute-done | bytes 409632 | tf_op jit(solution)/shard_map/ppermute | solution.py:261
  139.5 9.3 %collective-permute-done.25 = bf16[80,2560]{1,0:T(8,128)(2,1)S(1)} collective-permute-done((bf16[80,2560]{1,0:T(8,128)(2,1)S(1)}, bf16[80,2560]{1,0:T(8,128)(2,1)S(1)}, u32[]{:S(2)}, u32[]{:S(2)}) %collective-permute-start.25) | collective-permute-done | bytes 409632 | tf_op jit(solution)/shard_map/ppermute | solution.py:261
  148.9 11.6 %collective-permute-done.27 = bf16[80,2560]{1,0:T(8,128)(2,1)S(1)} collective-permute-done((bf16[80,2560]{1,0:T(8,128)(2,1)S(1)}, bf16[80,2560]{1,0:T(8,128)(2,1)S(1)}, u32[]{:S(2)}, u32[]{:S(2)}) %collective-permute-start.27) | collective-permute-done | bytes 409632 | tf_op jit(solution)/shard_map/ppermute | solution.py:261
  162.3 7.5 %collective-permute-start.20 = (bf16[80,2560]{1,0:T(8,128)(2,1)S(1)}, bf16[80,2560]{1,0:T(8,128)(2,1)S(1)}, u32[]{:S(2)}, u32[]{:S(2)}) collective-permute-start(bf16[80,2560]{1,0:T(8,128)(2,1)S(1)} %collective-permute-done.19), channel_id=1, source_target_pairs={{0,16},{1,17},{2,18},{3,19},{4,20},{5,21},{6,22},{7,23},{8,24},{9,... | collective-permute-start | bytes 1228808 | tf_op jit(solution)/shard_map/ppermute | solution.py:263
  169.8 10.5 %collective-permute-start.29 = (bf16[80,2560]{1,0:T(8,128)(2,1)S(1)}, bf16[80,2560]{1,0:T(8,128)(2,1)S(1)}, u32[]{:S(2)}, u32[]{:S(2)}) collective-permute-start(bf16[80,2560]{1,0:T(8,128)(2,1)S(1)} %collective-permute-done.28), channel_id=1, source_target_pairs={{0,16},{1,17},{2,18},{3,19},{4,20},{5,21},{6,22},{7,23},{8,24},{9,... | collective-permute-start | bytes 1228808 | tf_op jit(solution)/shard_map/ppermute | solution.py:263
  (72 shorter events, 18.6 us)
Async XLA Ops:
  9.5 23.9 %collective-permute-start.4 = (bf16[320,1024]{1,0:T(8,128)(2,1)S(1)}, bf16[320,1024]{1,0:T(8,128)(2,1)S(1)}, u32[]{:S(2)}, u32[]{:S(2)}) collective-permute-start(bf16[320,1024]{1,0:T(8,128)(2,1)S(1)} %pad_maximum_fusion.1), channel_id=1, source_target_pairs={{0,0},{1,1},{2,2},{3,3},{4,16},{5,17},{6,18},{7,19},{16,4},{17,5},... | collective-permute-start | bytes 1966088 | tf_op jit(solution)/shard_map/ppermute | solution.py:194
  10.4 11.2 %collective-permute-start.2 = (bf16[320,512]{1,0:T(8,128)(2,1)S(1)}, bf16[320,512]{1,0:T(8,128)(2,1)S(1)}, u32[]{:S(2)}, u32[]{:S(2)}) collective-permute-start(bf16[320,512]{1,0:T(8,128)(2,1)S(1)} %copy-done.5), channel_id=1, source_target_pairs={{0,2},{1,3},{2,0},{3,1},{4,18},{5,19},{6,16},{7,17},{16,6},{17,7},... | collective-permute-start | bytes 983048 | tf_op jit(solution)/shard_map/ppermute | solution.py:194
  12.0 16.2 %collective-permute-start.3 = (bf16[320,512]{1,0:T(8,128)(2,1)S(1)}, bf16[320,512]{1,0:T(8,128)(2,1)S(1)}, u32[]{:S(2)}, u32[]{:S(2)}) collective-permute-start(bf16[320,512]{1,0:T(8,128)(2,1)S(1)} %get-tuple-element.61), channel_id=1, source_target_pairs={{0,3},{1,2},{2,1},{3,0},{4,19},{5,18},{6,17},{7,16},{16,7},{17,6},... | collective-permute-start | bytes 983048 | tf_op jit(solution)/shard_map/ppermute | solution.py:194
  12.2 33.0 %collective-permute-start.8 = (bf16[320,1024]{1,0:T(8,128)(2,1)S(1)}, bf16[320,1024]{1,0:T(8,128)(2,1)S(1)}, u32[]{:S(2)}, u32[]{:S(2)}) collective-permute-start(bf16[320,1024]{1,0:T(8,128)(2,1)S(1)} %pad_maximum_fusion.3), channel_id=1, source_target_pairs={{0,2},{1,3},{2,0},{3,1},{4,18},{5,19},{6,16},{7,17},{16,6},{17,7},... | collective-permute-start | bytes 1966088 | tf_op jit(solution)/shard_map/ppermute | solution.py:194
  16.2 29.0 %collective-permute-start.6 = (bf16[320,1024]{1,0:T(8,128)(2,1)S(1)}, bf16[320,1024]{1,0:T(8,128)(2,1)S(1)}, u32[]{:S(2)}, u32[]{:S(2)}) collective-permute-start(bf16[320,1024]{1,0:T(8,128)(2,1)S(1)} %pad_maximum_fusion.2), channel_id=1, source_target_pairs={{0,1},{1,0},{2,3},{3,2},{4,17},{5,16},{6,19},{7,18},{16,5},{17,4},... | collective-permute-start | bytes 1966088 | tf_op jit(solution)/shard_map/ppermute | solution.py:194
  21.7 39.9 %collective-permute-start.12 = (bf16[320,1024]{1,0:T(8,128)(2,1)S(1)}, bf16[320,1024]{1,0:T(8,128)(2,1)S(1)}, u32[]{:S(2)}, u32[]{:S(2)}) collective-permute-start(bf16[320,1024]{1,0:T(8,128)(2,1)S(1)} %pad_maximum_fusion.4), channel_id=1, source_target_pairs={{0,3},{1,2},{2,1},{3,0},{4,19},{5,18},{6,17},{7,16},{16,7},{17,6},... | collective-permute-start | bytes 1966088 | tf_op jit(solution)/shard_map/ppermute | solution.py:194
  30.6 56.0 %collective-permute-start.13 = (bf16[4,320,512]{2,1,0:T(8,128)(2,1)}, bf16[4,320,512]{2,1,0:T(8,128)(2,1)}, u32[]{:S(2)}, u32[]{:S(2)}) collective-permute-start(bf16[4,320,512]{2,1,0:T(8,128)(2,1)} %pad_maximum_fusion.refs_6_), channel_id=1, source_target_pairs={{0,8},{8,0},{1,9},{9,1},{2,10},{10,2},{3,11},{11,3},{4,12},{12,4},... | collective-permute-start | bytes 3932168 | tf_op jit(solution)/shard_map/ppermute | solution.py:214
  61.7 41.2 %collective-permute-start.15 = (bf16[4,320,1024]{2,1,0:T(8,128)(2,1)S(1)}, bf16[4,320,1024]{2,1,0:T(8,128)(2,1)}, u32[]{:S(2)}, u32[]{:S(2)}) collective-permute-start(bf16[4,320,1024]{2,1,0:T(8,128)(2,1)S(1)} %shard_map.82.refs_4_), channel_id=1, source_target_pairs={{0,16},{16,0},{1,17},{17,1},{2,18},{18,2},{3,19},{19,3},{4,20},{20... | collective-permute-start | bytes 7864328 | tf_op jit(solution)/shard_map/ppermute | solution.py:197
  86.5 11.2 %collective-permute-start.14 = (bf16[4,320,512]{2,1,0:T(8,128)(2,1)}, bf16[4,320,512]{2,1,0:T(8,128)(2,1)}, u32[]{:S(2)}, u32[]{:S(2)}) collective-permute-start(bf16[4,320,512]{2,1,0:T(8,128)(2,1)} %collective-permute-done.13.refs_7_), channel_id=1, source_target_pairs={{0,16},{16,0},{1,17},{17,1},{2,18},{18,2},{3,19},{19,3},{4,20},{20... | collective-permute-start | bytes 3932168 | tf_op jit(solution)/shard_map/ppermute | solution.py:197
  86.9 17.1 %collective-permute-start.5 = (bf16[80,1024]{1,0:T(8,128)(2,1)}, bf16[80,1024]{1,0:T(8,128)(2,1)S(1)}, u32[]{:S(2)}, u32[]{:S(2)}) collective-permute-start(bf16[80,1024]{1,0:T(8,128)(2,1)} %get-tuple-element.33), channel_id=1, source_target_pairs={{0,0},{1,1},{2,2},{3,3},{4,16},{5,17},{6,18},{7,19},{16,4},{17,5},... | collective-permute-start | bytes 491528 | tf_op jit(solution)/shard_map/ppermute | solution.py:194
  88.5 15.6 %collective-permute-start.11 = (bf16[80,1024]{1,0:T(8,128)(2,1)}, bf16[80,1024]{1,0:T(8,128)(2,1)S(1)}, u32[]{:S(2)}, u32[]{:S(2)}) collective-permute-start(bf16[80,1024]{1,0:T(8,128)(2,1)} %get-tuple-element.41), channel_id=1, source_target_pairs={{0,3},{1,2},{2,1},{3,0},{4,19},{5,18},{6,17},{7,16},{16,7},{17,6},... | collective-permute-start | bytes 491528 | tf_op jit(solution)/shard_map/ppermute | solution.py:194
  102.9 15.9 %collective-permute-start.22 = (bf16[80,1024]{1,0:T(8,128)(2,1)S(1)}, bf16[80,1024]{1,0:T(8,128)(2,1)S(1)}, u32[]{:S(2)}, u32[]{:S(2)}) collective-permute-start(bf16[80,1024]{1,0:T(8,128)(2,1)S(1)} %get-tuple-element.77), channel_id=1, source_target_pairs={{0,1},{1,0},{2,3},{3,2},{4,17},{5,16},{6,19},{7,18},{16,5},{17,4},... | collective-permute-start | bytes 491528 | tf_op jit(solution)/shard_map/ppermute | solution.py:194
  104.1 16.9 %collective-permute-start.23 = (bf16[80,1024]{1,0:T(8,128)(2,1)S(1)}, bf16[80,1024]{1,0:T(8,128)(2,1)S(1)}, u32[]{:S(2)}, u32[]{:S(2)}) collective-permute-start(bf16[80,1024]{1,0:T(8,128)(2,1)S(1)} %get-tuple-element.76), channel_id=1, source_target_pairs={{0,2},{1,3},{2,0},{3,1},{4,18},{5,19},{6,16},{7,17},{16,6},{17,7},... | collective-permute-start | bytes 491528 | tf_op jit(solution)/shard_map/ppermute | solution.py:194
  104.1 17.2 %collective-permute-start.24 = (bf16[80,1024]{1,0:T(8,128)(2,1)S(1)}, bf16[80,1024]{1,0:T(8,128)(2,1)S(1)}, u32[]{:S(2)}, u32[]{:S(2)}) collective-permute-start(bf16[80,1024]{1,0:T(8,128)(2,1)S(1)} %get-tuple-element.75), channel_id=1, source_target_pairs={{0,3},{1,2},{2,1},{3,0},{4,19},{5,18},{6,17},{7,16},{16,7},{17,6},... | collective-permute-start | bytes 491528 | tf_op jit(solution)/shard_map/ppermute | solution.py:194
  106.5 14.8 %collective-permute-start.21 = (bf16[80,1024]{1,0:T(8,128)(2,1)S(1)}, bf16[80,1024]{1,0:T(8,128)(2,1)S(1)}, u32[]{:S(2)}, u32[]{:S(2)}) collective-permute-start(bf16[80,1024]{1,0:T(8,128)(2,1)S(1)} %get-tuple-element.54), channel_id=1, source_target_pairs={{0,0},{1,1},{2,2},{3,3},{4,16},{5,17},{6,18},{7,19},{16,4},{17,5},... | collective-permute-start | bytes 491528 | tf_op jit(solution)/shard_map/ppermute | solution.py:194
  117.8 16.6 %collective-permute-start.16 = (bf16[80,2560]{1,0:T(8,128)(2,1)S(1)}, bf16[80,2560]{1,0:T(8,128)(2,1)S(1)}, u32[]{:S(2)}, u32[]{:S(2)}) collective-permute-start(bf16[80,2560]{1,0:T(8,128)(2,1)S(1)} %get-tuple-element.51), channel_id=1, source_target_pairs={{0,1},{1,0},{2,3},{3,2},{4,5},{5,4},{6,7},{7,6},{8,9},{9,8},{10,11... | collective-permute-start | bytes 1228808 | tf_op jit(solution)/shard_map/ppermute | solution.py:261
  118.9 15.9 %collective-permute-start.17 = (bf16[80,2560]{1,0:T(8,128)(2,1)S(1)}, bf16[80,2560]{1,0:T(8,128)(2,1)S(1)}, u32[]{:S(2)}, u32[]{:S(2)}) collective-permute-start(bf16[80,2560]{1,0:T(8,128)(2,1)S(1)} %get-tuple-element.52), channel_id=1, source_target_pairs={{0,2},{1,3},{2,0},{3,1},{4,6},{5,7},{6,4},{7,5},{8,10},{9,11},{10,... | collective-permute-start | bytes 1228808 | tf_op jit(solution)/shard_map/ppermute | solution.py:261
  120.9 17.6 %collective-permute-start.18 = (bf16[80,2560]{1,0:T(8,128)(2,1)S(1)}, bf16[80,2560]{1,0:T(8,128)(2,1)S(1)}, u32[]{:S(2)}, u32[]{:S(2)}) collective-permute-start(bf16[80,2560]{1,0:T(8,128)(2,1)S(1)} %get-tuple-element.53), channel_id=1, source_target_pairs={{0,3},{1,2},{2,1},{3,0},{4,7},{5,6},{6,5},{7,4},{8,11},{9,10},{10,... | collective-permute-start | bytes 1228808 | tf_op jit(solution)/shard_map/ppermute | solution.py:261
  131.2 17.6 %collective-permute-start.25 = (bf16[80,2560]{1,0:T(8,128)(2,1)S(1)}, bf16[80,2560]{1,0:T(8,128)(2,1)S(1)}, u32[]{:S(2)}, u32[]{:S(2)}) collective-permute-start(bf16[80,2560]{1,0:T(8,128)(2,1)S(1)} %get-tuple-element.56), channel_id=1, source_target_pairs={{0,1},{1,0},{2,3},{3,2},{4,5},{5,4},{6,7},{7,6},{8,9},{9,8},{10,11... | collective-permute-start | bytes 1228808 | tf_op jit(solution)/shard_map/ppermute | solution.py:261
  132.4 16.4 %collective-permute-start.26 = (bf16[80,2560]{1,0:T(8,128)(2,1)S(1)}, bf16[80,2560]{1,0:T(8,128)(2,1)S(1)}, u32[]{:S(2)}, u32[]{:S(2)}) collective-permute-start(bf16[80,2560]{1,0:T(8,128)(2,1)S(1)} %get-tuple-element.57), channel_id=1, source_target_pairs={{0,2},{1,3},{2,0},{3,1},{4,6},{5,7},{6,4},{7,5},{8,10},{9,11},{10,... | collective-permute-start | bytes 1228808 | tf_op jit(solution)/shard_map/ppermute | solution.py:261
  134.4 26.1 %collective-permute-start.27 = (bf16[80,2560]{1,0:T(8,128)(2,1)S(1)}, bf16[80,2560]{1,0:T(8,128)(2,1)S(1)}, u32[]{:S(2)}, u32[]{:S(2)}) collective-permute-start(bf16[80,2560]{1,0:T(8,128)(2,1)S(1)} %get-tuple-element.58), channel_id=1, source_target_pairs={{0,3},{1,2},{2,1},{3,0},{4,7},{5,6},{6,5},{7,4},{8,11},{9,10},{10,... | collective-permute-start | bytes 1228808 | tf_op jit(solution)/shard_map/ppermute | solution.py:261
  138.7 23.6 %collective-permute-start.19 = (bf16[80,2560]{1,0:T(8,128)(2,1)S(1)}, bf16[80,2560]{1,0:T(8,128)(2,1)S(1)}, u32[]{:S(2)}, u32[]{:S(2)}) collective-permute-start(bf16[80,2560]{1,0:T(8,128)(2,1)S(1)} %add_convert_fusion.3), channel_id=1, source_target_pairs={{0,0},{1,1},{2,2},{3,3},{4,16},{5,17},{6,18},{7,19},{16,4},{17,5},... | collective-permute-start | bytes 1228808 | tf_op jit(solution)/shard_map/ppermute | solution.py:194
  162.3 18.2 %collective-permute-start.20 = (bf16[80,2560]{1,0:T(8,128)(2,1)S(1)}, bf16[80,2560]{1,0:T(8,128)(2,1)S(1)}, u32[]{:S(2)}, u32[]{:S(2)}) collective-permute-start(bf16[80,2560]{1,0:T(8,128)(2,1)S(1)} %collective-permute-done.19), channel_id=1, source_target_pairs={{0,16},{1,17},{2,18},{3,19},{4,20},{5,21},{6,22},{7,23},{8,24},{9,... | collective-permute-start | bytes 1228808 | tf_op jit(solution)/shard_map/ppermute | solution.py:263
  169.8 11.9 %collective-permute-start.29 = (bf16[80,2560]{1,0:T(8,128)(2,1)S(1)}, bf16[80,2560]{1,0:T(8,128)(2,1)S(1)}, u32[]{:S(2)}, u32[]{:S(2)}) collective-permute-start(bf16[80,2560]{1,0:T(8,128)(2,1)S(1)} %collective-permute-done.28), channel_id=1, source_target_pairs={{0,16},{1,17},{2,18},{3,19},{4,20},{5,21},{6,22},{7,23},{8,24},{9,... | collective-permute-start | bytes 1228808 | tf_op jit(solution)/shard_map/ppermute | solution.py:263
  (13 other events, 148.3 us)

commit v4 on v3

--- a/solution.py
+++ b/solution.py
@@ -8,16 +8,18 @@
 from jax.sharding import PartitionSpec as P
 
 HEADS = 32
-CHUNKS = (1, 1)
+CHUNKS = (4, 6)
+ROWS_SENT = ((1,), (3, 3))
 JOINED = 4
 
 
 def attend_project(
-    query_parts, context, weight_blocks, where, head_size
+    query_parts, marks, context, weight_blocks, where, head_size
 ):
     homes, home_rows, features = context[0].shape
     home_rows = home_rows // 2
     chunk_rows = query_parts[0].shape[0]
+    groups = len(marks) - 1
     joined = math.gcd(features // head_size, JOINED)
     steps = features // head_size // joined
     key_rows = homes * home_rows
@@ -31,7 +33,7 @@
     def body(where, *refs):
         q_refs, refs = refs[:homes], refs[homes:]
         context_refs, weight_refs, refs = refs[:2], refs[2:6], refs[6:]
-        out_refs, (attended, w_held, w_sem) = refs[:homes], refs[homes:]
+        out_refs, (attended, w_held, w_sem) = refs[: homes * groups], refs[homes * groups :]
         step = pl.program_id(0)
         side, mine, spot = where[0], where[1], where[2]
 
@@ -113,8 +115,11 @@
                     contract,
                     preferred_element_type=jnp.float32,
                 )
-                for at, ref in enumerate(out_refs[first : first + together]):
-                    ref[...] = product[at * chunk_rows : (at + 1) * chunk_rows].astype(ref.dtype)
+                for at in range(together):
+                    for some in range(groups):
+                        ref = out_refs[some * homes + first + at]
+                        begin, end = (at * chunk_rows + mark for mark in marks[some : some + 2])
+                        ref[...] = product[begin:end].astype(ref.dtype)
 
     width = joined * head_size
     stacked = pl.BlockSpec((homes, 2 * home_rows, width), lambda step, _: (0, 0, step))
@@ -128,7 +133,11 @@
                 *[stacked] * 2,
                 *[pl.BlockSpec(memory_space=pl.ANY)] * 4,
             ],
-            out_specs=[pl.BlockSpec((chunk_rows, columns), lambda step, _: (0, 0))] * homes,
+            out_specs=[
+                pl.BlockSpec((last - first, columns), lambda step, _: (0, 0))
+                for first, last in zip(marks, marks[1:])
+                for home in range(homes)
+            ],
             scratch_shapes=[
                 pltpu.VMEM((homes * chunk_rows, features), jnp.bfloat16),
                 pltpu.VMEM((columns, features), jnp.bfloat16),
@@ -136,19 +145,20 @@
             ],
         ),
         out_shape=[
-            jax.ShapeDtypeStruct((chunk_rows, columns), jnp.float32 if home == 0 else jnp.bfloat16)
+            jax.ShapeDtypeStruct((last - first, columns), jnp.float32 if home == 0 else jnp.bfloat16)
+            for first, last in zip(marks, marks[1:])
             for home in range(homes)
         ],
         compiler_params=pltpu.CompilerParams(vmem_limit_bytes=(28 if homes <= 4 else 56) * 1024 * 1024),
         cost_estimate=pl.CostEstimate(
-            flops=homes * chunk_rows * features * (8 * key_rows + 2 * columns) + 0,
+            flops=homes * chunk_rows * features * (8 * key_rows + 2 * columns),
             bytes_accessed=2 * features * (4 * key_rows + columns),
             transcendentals=homes * chunk_rows * 2 * key_rows * (features // head_size),
         ),
     )(where, *query_parts, *context, *weight_blocks)
 
 
-def gathered(parts, rows, hidden):
+def gathered(parts, rows):
     homes, width = len(parts), parts[0].shape[1]
 
     def body(*refs):
@@ -160,7 +170,7 @@
         body,
         out_shape=jax.ShapeDtypeStruct((homes, rows, width), parts[0].dtype),
         compiler_params=pltpu.CompilerParams(vmem_limit_bytes=16 * 1024 * 1024),
-        cost_estimate=pl.CostEstimate(flops=hidden, bytes_accessed=8 * homes * rows * width, transcendentals=0),
+        cost_estimate=pl.CostEstimate(flops=0, bytes_accessed=8 * homes * rows * width, transcendentals=0),
     )(*parts)
 
 
@@ -218,6 +228,8 @@
         part = jnp.concatenate([mine(key, step), mine(value, step)], axis=0)
         if step > 0:
             part, weight_parts[step - 1] = after(part, weight_parts[step - 1])
+        if step == half - 1:
+            part, weight_parts[step] = after(part, weight_parts[step])
         pair_parts.append(send(part, step))
     own, pair_parts[0] = after(own, pair_parts[0])
     own_far, other_far = sibling(own), sibling(other)
@@ -227,25 +239,25 @@
         queries[0][step], pair_parts[at] = after(queries[0][step], pair_parts[at])
     queries[0][2], own_far = after(queries[0][2], own_far)
     query_parts = [send(part, step) for step, part in enumerate(queries[0])]
-    near = gathered(pair_parts, 2 * rows, 0)
+    near = gathered(pair_parts, 2 * rows)
     far = sibling(near)
-    queries[1][0], other_far = after(queries[1][0], other_far)
-    queries[1][0], far = after(queries[1][0], far)
+    queries[1][3], other_far = after(queries[1][3], other_far)
+    queries[1][3], far = after(queries[1][3], far)
     query_parts = [query_parts] + [
         [send(part, step) for step, part in enumerate(parts)] for parts in queries[1:]
     ]
     weight_blocks = (own, other, own_far, other_far)
 
-    partials = [
-        attend_project(
-            parts,
-            (near, far),
-            weight_blocks,
-            where,
-            head_size,
-        )
-        for parts in query_parts
-    ]
+    partials, done_rows = [], []
+    for parts, piece, sizes in zip(query_parts, pieces, ROWS_SENT):
+        length = piece.stop - piece.start
+        marks = [length * sum(sizes[:at]) // sum(sizes) for at in range(len(sizes) + 1)]
+        if partials:
+            parts[0], partials[-1][0] = after(parts[0], partials[-1][0])
+        sums = attend_project(parts, marks, (near, far), weight_blocks, where, head_size)
+        for at in range(len(sizes)):
+            partials.append(list(sums[at * half : (at + 1) * half]))
+            done_rows.append(slice(piece.start + marks[at], piece.start + marks[at + 1]))
 
     step_ids = lax.broadcasted_iota(jnp.int32, (step_gates.shape[0], 1), 0)
     gate_row = jnp.sum(
@@ -254,11 +266,20 @@
     is_main = branch == 1
     wanted = control_mask[:, None] == 1
     result = jnp.zeros_like(residual)
-    for piece, partial in zip(pieces, partials):
+    arrived = []
+    for piece, partial in zip(done_rows, partials):
+        parts = []
+        for step in range(1, half):
+            part = partial[step]
+            if len(arrived) >= 2:
+                part, arrived[0][step - 1] = after(part, arrived[0][step - 1])
+            swap = [(s, s ^ step) for s in range(count)]
+            parts.append(lax.ppermute(part, "seq", swap))
+        arrived.append(parts)
+    for piece, partial, parts in zip(done_rows, partials, arrived):
         summed = partial[0]
-        for step in range(1, half):
-            swap = [(s, s ^ step) for s in range(count)]
-            summed = summed + lax.ppermute(partial[step], "seq", swap).astype(jnp.float32)
+        for part in parts:
+            summed = summed + part.astype(jnp.float32)
         projected = send(summed.astype(jnp.bfloat16), 0)
         context_rows = jnp.where(is_main, lax.ppermute(projected, "branch", [(0, 1)]), projected)
         hint = jnp.where(wanted[piece], context_rows, jnp.zeros_like(projected))

time: 184 us -> 179 us (0.973)
  waiting for transfers between devices: 64.2 us -> 50.1 us
  starting transfers between devices: 89.9 us -> 98.6 us
    ppermute x3, starting transfers between devices: 25.2 us -> 36.1 us  [sibling(): return lax.ppermute(array, 'branch', [(0, 1), (1, 0)])]
    ppermute x18 -> x19, waiting for transfers between devices: 38.3 us -> 28.7 us  [send(): return lax.ppermute(array, pair, crossing(step))]
    ppermute x6 -> x9, waiting for transfers between devices: 24.6 us -> 20.8 us  [per_device(): parts.append(lax.ppermute(part, 'seq', swap))]
    ppermute x2 -> x3, starting transfers between devices: 18.1 us -> 16.6 us  [per_device(): lax.ppermute(projected, 'branch', [(0, 1)])]
    ppermute x18 -> x19, starting transfers between devices: 37.6 us -> 36.7 us  [send(): return lax.ppermute(array, pair, crossing(step))]
    ppermute x6 -> x9, starting transfers between devices: 7.11 us -> 7.66 us  [per_device(): parts.append(lax.ppermute(part, 'seq', swap))]
  transfers between devices with their start and end apart: 30 -> 35, of which waited for: 9 -> 9; matrix products, arithmetic and copies ran while one was open for 2% -> 3% of each run, Pallas kernels for 11% -> 11%
where the time goes in v4:
time: 179 us; the launch traced here: 178 us
  starting transfers between devices  98.6 us (55%)
  waiting for transfers between devices  50.1 us (28%)
  Pallas kernels  19.9 us (11%)
  other arithmetic  4.48 us (3%)
  local copies, waits for them, and re-layouts  3.9 us (2%)
    ppermute x19, starting transfers between devices, send(): return lax.ppermute(array, pair, crossing(step))  36.7 us
    ppermute x3, starting transfers between devices, sibling(): return lax.ppermute(array, 'branch', [(0, 1), (1, 0)])  36.1 us
    ppermute x19, waiting for transfers between devices, send(): return lax.ppermute(array, pair, crossing(step))  28.7 us
    ppermute x9, waiting for transfers between devices, per_device(): parts.append(lax.ppermute(part, 'seq', swap))  20.8 us
    pallas_call x2, Pallas kernels, attend_project(): pl.pallas_call(body, grid_spec=pltpu.PrefetchScalarGridSpec(num_scalar_pr...  19.8 us
    ppermute x3, starting transfers between devices, per_device(): lax.ppermute(projected, 'branch', [(0, 1)])  16.6 us
    ppermute x9, starting transfers between devices, per_device(): parts.append(lax.ppermute(part, 'seq', swap))  7.66 us
  transfers between devices with their start and end apart: 35, of which 9 were waited for; matrix products, arithmetic and copies ran while one was open for 3% of the time, Pallas kernels for 11%

profile of v4, /device:TPU:0, one launch (start us, length us, event | category | flops | bytes accessed | tf_op | source)
XLA Modules:
  0.0 178.0 jit_solution(4079135081831395959)
XLA Ops:
  0.0 2.4 %dynamic-slice_bitcast_fusion.11 = (bf16[320,512]{1,0:T(8,128)(2,1)}, bf16[320,512]{1,0:T(8,128)(2,1)}, bf16[320,512]{1,0:T(8,128)(2,1)S(1)}, bf16[320,512]{1,0:T(8,128)(2,1)}) fusion(bf16[1,4096,320]{1,2,0:T(8,128)(2,1)} %param.15, s32[]{:T(128)S(6)} %select_n.94, s32[]{:T(128)S(6)} %select_n.95, s32[]{:T(128)S(6)} %select_n.97, s32[]{:T(128)S(6)} %select_n.96), kind=kLoop, calls=%fused_computation.27 | loop fusion | bytes 2621456 | tf_op jit(solution)/shard_map/dynamic_slice | solution.py:220
  2.4 2.9 %collective-permute-start.2 = (bf16[320,512]{1,0:T(8,128)(2,1)}, bf16[320,512]{1,0:T(8,128)(2,1)S(1)}, u32[]{:S(2)}, u32[]{:S(2)}) collective-permute-start(bf16[320,512]{1,0:T(8,128)(2,1)} %get-tuple-element.86), channel_id=1, source_target_pairs={{0,1},{1,0},{2,3},{3,2},{4,17},{5,16},{6,19},{7,18},{16,5},{17,4},... | collective-permute-start | bytes 983048 | tf_op jit(solution)/shard_map/ppermute | solution.py:204
  5.4 1.6 collective-permute-start.3
  6.9 3.9 %collective-permute-start.1 = (bf16[320,512]{1,0:T(8,128)(2,1)}, bf16[320,512]{1,0:T(8,128)(2,1)}, u32[]{:S(2)}, u32[]{:S(2)}) collective-permute-start(bf16[320,512]{1,0:T(8,128)(2,1)} %get-tuple-element.85), channel_id=1, source_target_pairs={{0,0},{1,1},{2,2},{3,3},{4,16},{5,17},{6,18},{7,19},{16,4},{17,5},... | collective-permute-start | bytes 983048 | tf_op jit(solution)/shard_map/ppermute | solution.py:204
  16.5 5.8 %collective-permute-done.4 = bf16[320,512]{1,0:T(8,128)(2,1)} collective-permute-done((bf16[320,512]{1,0:T(8,128)(2,1)S(1)}, bf16[320,512]{1,0:T(8,128)(2,1)}, u32[]{:S(2)}, u32[]{:S(2)}) %collective-permute-start.4) | collective-permute-done | bytes 327712 | tf_op jit(solution)/shard_map/ppermute | solution.py:204
  22.3 3.6 %collective-permute-start.13 = (bf16[320,1024]{1,0:T(8,128)(2,1)S(1)}, bf16[320,1024]{1,0:T(8,128)(2,1)S(1)}, u32[]{:S(2)}, u32[]{:S(2)}) collective-permute-start(bf16[320,1024]{1,0:T(8,128)(2,1)S(1)} %pad_maximum_fusion.4), channel_id=1, source_target_pairs={{0,3},{1,2},{2,1},{3,0},{4,19},{5,18},{6,17},{7,16},{16,7},{17,6},... | collective-permute-start | bytes 1966088 | tf_op jit(solution)/shard_map/ppermute | solution.py:204
  25.9 2.5 %pad_maximum_fusion.refs_6_ = bf16[4,320,512]{2,1,0:T(8,128)(2,1)} fusion(bf16[1,320,512]{2,1,0:T(8,128)(2,1)} %bitcast.17, bf16[1,320,512]{2,1,0:T(8,128)(2,1)} %bitcast.14, bf16[1,320,512]{2,1,0:T(8,128)(2,1)S(1)} %bitcast.68, bf16[1,320,512]{2,1,0:T(8,128)(2,1)} %bitcast.8), kind=kLoop, calls=%fused_computation | loop fusion | flops 1966080 | bytes 2621440 | tf_op jit(solution)/shard_map/stack | solution.py:223
  30.6 7.3 %collective-permute-done.9.refs_2_ = bf16[320,1024]{1,0:T(8,128)(2,1)S(1)} collective-permute-done((bf16[320,1024]{1,0:T(8,128)(2,1)S(1)}, bf16[320,1024]{1,0:T(8,128)(2,1)S(1)}, u32[]{:S(2)}, u32[]{:S(2)}) %collective-permute-start.9) | collective-permute-done | bytes 655392 | tf_op jit(solution)/shard_map/ppermute | solution.py:204
  37.9 12.9 %collective-permute-done.13.refs_3_ = bf16[320,1024]{1,0:T(8,128)(2,1)S(1)} collective-permute-done((bf16[320,1024]{1,0:T(8,128)(2,1)S(1)}, bf16[320,1024]{1,0:T(8,128)(2,1)S(1)}, u32[]{:S(2)}, u32[]{:S(2)}) %collective-permute-start.13) | collective-permute-done | bytes 655392 | tf_op jit(solution)/shard_map/ppermute | solution.py:204
  51.0 35.6 %collective-permute-start.16 = (bf16[4,320,1024]{2,1,0:T(8,128)(2,1)S(1)}, bf16[4,320,1024]{2,1,0:T(8,128)(2,1)}, u32[]{:S(2)}, u32[]{:S(2)}) collective-permute-start(bf16[4,320,1024]{2,1,0:T(8,128)(2,1)S(1)} %shard_map.82.refs_4_), channel_id=1, source_target_pairs={{0,16},{16,0},{1,17},{17,1},{2,18},{18,2},{3,19},{19,3},{4,20},{20... | collective-permute-start | bytes 7864328 | tf_op jit(solution)/shard_map/ppermute | solution.py:207
  87.8 1.6 collective-permute-start.6
  89.4 8.2 %collective-permute-start.12 = (bf16[64,1024]{1,0:T(8,128)(2,1)}, bf16[64,1024]{1,0:T(8,128)(2,1)S(1)}, u32[]{:S(2)}, u32[]{:S(2)}) collective-permute-start(bf16[64,1024]{1,0:T(8,128)(2,1)} %get-tuple-element.54), channel_id=1, source_target_pairs={{0,3},{1,2},{2,1},{3,0},{4,19},{5,18},{6,17},{7,16},{16,7},{17,6},... | collective-permute-start | bytes 393224 | tf_op jit(solution)/shard_map/ppermute | solution.py:204
  98.5 4.3 %collective-permute-start.11 = (bf16[64,1024]{1,0:T(8,128)(2,1)S(1)}, bf16[64,1024]{1,0:T(8,128)(2,1)S(1)}, u32[]{:S(2)}, u32[]{:S(2)}) collective-permute-start(bf16[64,1024]{1,0:T(8,128)(2,1)S(1)} %get-tuple-element.52), channel_id=1, source_target_pairs={{0,2},{1,3},{2,0},{3,1},{4,18},{5,19},{6,16},{7,17},{16,6},{17,7},... | collective-permute-start | bytes 393224 | tf_op jit(solution)/shard_map/ppermute | solution.py:204
  105.0 3.0 %collective-permute-start.19 = (bf16[96,1024]{1,0:T(8,128)(2,1)S(1)}, bf16[96,1024]{1,0:T(8,128)(2,1)S(1)}, u32[]{:S(2)}, u32[]{:S(2)}) collective-permute-start(bf16[96,1024]{1,0:T(8,128)(2,1)S(1)} %get-tuple-element.67), channel_id=1, source_target_pairs={{0,3},{1,2},{2,1},{3,0},{4,19},{5,18},{6,17},{7,16},{16,7},{17,6},... | collective-permute-start | bytes 589832 | tf_op jit(solution)/shard_map/ppermute | solution.py:204
  108.0 8.6 %shard_map.83 = (f32[64,2560]{1,0:T(8,128)S(1)}, bf16[64,2560]{1,0:T(8,128)(2,1)S(1)}, bf16[64,2560]{1,0:T(8,128)(2,1)S(1)}, bf16[64,2560]{1,0:T(8,128)(2,1)S(1)}) custom-call(s32[3]{0:T(128)S(1)} %pad_add_fusion.where, bf16[64,1024]{1,0:T(8,128)(2,1)S(1)} %collective-permute-done.6.refs_0_, bf16[64,1024]{1,0:T(8,128)(2,1)S(1)} %collective-permute-done.8.refs_1_, ...), custom_call_target="tpu_custom_call" | custom-call | flops 2684354560 | bytes 10485760 | tf_op jit(solution)/shard_map/pallas_call | solution.py:126
  117.2 1.8 %collective-permute-start.21 = (bf16[64,2560]{1,0:T(8,128)(2,1)S(1)}, bf16[64,2560]{1,0:T(8,128)(2,1)S(1)}, u32[]{:S(2)}, u32[]{:S(2)}) collective-permute-start(bf16[64,2560]{1,0:T(8,128)(2,1)S(1)} %get-tuple-element.72), channel_id=1, source_target_pairs={{0,2},{1,3},{2,0},{3,1},{4,6},{5,7},{6,4},{7,5},{8,10},{9,11},{10,... | collective-permute-start | bytes 983048 | tf_op jit(solution)/shard_map/ppermute | solution.py:277
  120.2 11.1 %shard_map.84 = (f32[48,2560]{1,0:T(8,128)S(1)}, bf16[48,2560]{1,0:T(8,128)(2,1)S(1)}, bf16[48,2560]{1,0:T(8,128)(2,1)S(1)}, bf16[48,2560]{1,0:T(8,128)(2,1)S(1)...) custom-call(s32[3]{0:T(128)S(1)} %pad_add_fusion.where, ...), custom_call_target="tpu_custom_call" | custom-call | flops 4026531840 | bytes 10485760 | tf_op jit(solution)/shard_map/pallas_call | solution.py:126
  131.9 1.8 %collective-permute-start.26 = (bf16[48,2560]{1,0:T(8,128)(2,1)S(1)}, bf16[48,2560]{1,0:T(8,128)(2,1)S(1)}, u32[]{:S(2)}, u32[]{:S(2)}) collective-permute-start(bf16[48,2560]{1,0:T(8,128)(2,1)S(1)} %get-tuple-element.79), channel_id=1, source_target_pairs={{0,2},{1,3},{2,0},{3,1},{4,6},{5,7},{6,4},{7,5},{8,10},{9,11},{10,... | collective-permute-start | bytes 737288 | tf_op jit(solution)/shard_map/ppermute | solution.py:277
  135.4 4.3 %collective-permute-done.22 = bf16[64,2560]{1,0:T(8,128)(2,1)S(1)} collective-permute-done((bf16[64,2560]{1,0:T(8,128)(2,1)S(1)}, bf16[64,2560]{1,0:T(8,128)(2,1)S(1)}, u32[]{:S(2)}, u32[]{:S(2)}) %collective-permute-start.22) | collective-permute-done | bytes 327712 | tf_op jit(solution)/shard_map/ppermute | solution.py:277
  139.9 7.7 %collective-permute-done.25 = bf16[48,2560]{1,0:T(8,128)(2,1)S(1)} collective-permute-done((bf16[48,2560]{1,0:T(8,128)(2,1)S(1)}, bf16[48,2560]{1,0:T(8,128)(2,1)S(1)}, u32[]{:S(2)}, u32[]{:S(2)}) %collective-permute-start.25) | collective-permute-done | bytes 245792 | tf_op jit(solution)/shard_map/ppermute | solution.py:277
  149.2 8.9 %collective-permute-done.30 = bf16[48,2560]{1,0:T(8,128)(2,1)S(1)} collective-permute-done((bf16[48,2560]{1,0:T(8,128)(2,1)S(1)}, bf16[48,2560]{1,0:T(8,128)(2,1)S(1)}, u32[]{:S(2)}, u32[]{:S(2)}) %collective-permute-start.30) | collective-permute-done | bytes 245792 | tf_op jit(solution)/shard_map/ppermute | solution.py:277
  158.9 9.0 %collective-permute-start.24 = (bf16[64,2560]{1,0:T(8,128)(2,1)S(1)}, bf16[64,2560]{1,0:T(8,128)(2,1)S(1)}, u32[]{:S(2)}, u32[]{:S(2)}) collective-permute-start(bf16[64,2560]{1,0:T(8,128)(2,1)S(1)} %collective-permute-done.23), channel_id=1, source_target_pairs={{0,16},{1,17},{2,18},{3,19},{4,20},{5,21},{6,22},{7,23},{8,24},{9,... | collective-permute-start | bytes 983048 | tf_op jit(solution)/shard_map/ppermute | solution.py:284
  168.1 5.0 %collective-permute-start.29 = (bf16[48,2560]{1,0:T(8,128)(2,1)S(1)}, bf16[48,2560]{1,0:T(8,128)(2,1)S(1)}, u32[]{:S(2)}, u32[]{:S(2)}) collective-permute-start(bf16[48,2560]{1,0:T(8,128)(2,1)S(1)} %collective-permute-done.28), channel_id=1, source_target_pairs={{0,16},{1,17},{2,18},{3,19},{4,20},{5,21},{6,22},{7,23},{8,24},{9,... | collective-permute-start | bytes 737288 | tf_op jit(solution)/shard_map/ppermute | solution.py:284
  173.2 2.6 %collective-permute-start.34 = (bf16[48,2560]{1,0:T(8,128)(2,1)S(1)}, bf16[48,2560]{1,0:T(8,128)(2,1)S(1)}, u32[]{:S(2)}, u32[]{:S(2)}) collective-permute-start(bf16[48,2560]{1,0:T(8,128)(2,1)S(1)} %collective-permute-done.33), channel_id=1, source_target_pairs={{0,16},{1,17},{2,18},{3,19},{4,20},{5,21},{6,22},{7,23},{8,24},{9,... | collective-permute-start | bytes 737288 | tf_op jit(solution)/shard_map/ppermute | solution.py:284
  (86 shorter events, 20.8 us)
Async XLA Ops:
  6.9 15.3 %collective-permute-start.4 = (bf16[320,512]{1,0:T(8,128)(2,1)S(1)}, bf16[320,512]{1,0:T(8,128)(2,1)}, u32[]{:S(2)}, u32[]{:S(2)}) collective-permute-start(bf16[320,512]{1,0:T(8,128)(2,1)S(1)} %get-tuple-element.87), channel_id=1, source_target_pairs={{0,3},{1,2},{2,1},{3,0},{4,19},{5,18},{6,17},{7,16},{16,7},{17,6},... | collective-permute-start | bytes 983048 | tf_op jit(solution)/shard_map/ppermute | solution.py:204
  11.1 19.5 %collective-permute-start.5 = (bf16[320,1024]{1,0:T(8,128)(2,1)S(1)}, bf16[320,1024]{1,0:T(8,128)(2,1)S(1)}, u32[]{:S(2)}, u32[]{:S(2)}) collective-permute-start(bf16[320,1024]{1,0:T(8,128)(2,1)S(1)} %pad_maximum_fusion.1), channel_id=1, source_target_pairs={{0,0},{1,1},{2,2},{3,3},{4,16},{5,17},{6,18},{7,19},{16,4},{17,5},... | collective-permute-start | bytes 1966088 | tf_op jit(solution)/shard_map/ppermute | solution.py:204
  13.4 24.5 %collective-permute-start.9 = (bf16[320,1024]{1,0:T(8,128)(2,1)S(1)}, bf16[320,1024]{1,0:T(8,128)(2,1)S(1)}, u32[]{:S(2)}, u32[]{:S(2)}) collective-permute-start(bf16[320,1024]{1,0:T(8,128)(2,1)S(1)} %pad_maximum_fusion.3), channel_id=1, source_target_pairs={{0,2},{1,3},{2,0},{3,1},{4,18},{5,19},{6,16},{7,17},{16,6},{17,7},... | collective-permute-start | bytes 1966088 | tf_op jit(solution)/shard_map/ppermute | solution.py:204
  16.0 21.9 %collective-permute-start.7 = (bf16[320,1024]{1,0:T(8,128)(2,1)S(1)}, bf16[320,1024]{1,0:T(8,128)(2,1)S(1)}, u32[]{:S(2)}, u32[]{:S(2)}) collective-permute-start(bf16[320,1024]{1,0:T(8,128)(2,1)S(1)} %pad_maximum_fusion.2), channel_id=1, source_target_pairs={{0,1},{1,0},{2,3},{3,2},{4,17},{5,16},{6,19},{7,18},{16,5},{17,4},... | collective-permute-start | bytes 1966088 | tf_op jit(solution)/shard_map/ppermute | solution.py:204
  22.3 28.5 %collective-permute-start.13 = (bf16[320,1024]{1,0:T(8,128)(2,1)S(1)}, bf16[320,1024]{1,0:T(8,128)(2,1)S(1)}, u32[]{:S(2)}, u32[]{:S(2)}) collective-permute-start(bf16[320,1024]{1,0:T(8,128)(2,1)S(1)} %pad_maximum_fusion.4), channel_id=1, source_target_pairs={{0,3},{1,2},{2,1},{3,0},{4,19},{5,18},{6,17},{7,16},{16,7},{17,6},... | collective-permute-start | bytes 1966088 | tf_op jit(solution)/shard_map/ppermute | solution.py:204
  28.3 58.3 %collective-permute-start.14 = (bf16[4,320,512]{2,1,0:T(8,128)(2,1)}, bf16[4,320,512]{2,1,0:T(8,128)(2,1)}, u32[]{:S(2)}, u32[]{:S(2)}) collective-permute-start(bf16[4,320,512]{2,1,0:T(8,128)(2,1)} %pad_maximum_fusion.refs_6_), channel_id=1, source_target_pairs={{0,8},{8,0},{1,9},{9,1},{2,10},{10,2},{3,11},{11,3},{4,12},{12,4},... | collective-permute-start | bytes 3932168 | tf_op jit(solution)/shard_map/ppermute | solution.py:224
  51.0 51.9 %collective-permute-start.16 = (bf16[4,320,1024]{2,1,0:T(8,128)(2,1)S(1)}, bf16[4,320,1024]{2,1,0:T(8,128)(2,1)}, u32[]{:S(2)}, u32[]{:S(2)}) collective-permute-start(bf16[4,320,1024]{2,1,0:T(8,128)(2,1)S(1)} %shard_map.82.refs_4_), channel_id=1, source_target_pairs={{0,16},{16,0},{1,17},{17,1},{2,18},{18,2},{3,19},{19,3},{4,20},{20... | collective-permute-start | bytes 7864328 | tf_op jit(solution)/shard_map/ppermute | solution.py:207
  87.8 16.0 %collective-permute-start.6 = (bf16[64,1024]{1,0:T(8,128)(2,1)}, bf16[64,1024]{1,0:T(8,128)(2,1)S(1)}, u32[]{:S(2)}, u32[]{:S(2)}) collective-permute-start(bf16[64,1024]{1,0:T(8,128)(2,1)} %get-tuple-element.46), channel_id=1, source_target_pairs={{0,0},{1,1},{2,2},{3,3},{4,16},{5,17},{6,18},{7,19},{16,4},{17,5},... | collective-permute-start | bytes 393224 | tf_op jit(solution)/shard_map/ppermute | solution.py:204
  89.4 15.6 %collective-permute-start.12 = (bf16[64,1024]{1,0:T(8,128)(2,1)}, bf16[64,1024]{1,0:T(8,128)(2,1)S(1)}, u32[]{:S(2)}, u32[]{:S(2)}) collective-permute-start(bf16[64,1024]{1,0:T(8,128)(2,1)} %get-tuple-element.54), channel_id=1, source_target_pairs={{0,3},{1,2},{2,1},{3,0},{4,19},{5,18},{6,17},{7,16},{16,7},{17,6},... | collective-permute-start | bytes 393224 | tf_op jit(solution)/shard_map/ppermute | solution.py:204
  102.9 13.7 %collective-permute-start = (bf16[96,1024]{1,0:T(8,128)(2,1)S(1)}, bf16[96,1024]{1,0:T(8,128)(2,1)S(1)}, u32[]{:S(2)}, u32[]{:S(2)}) collective-permute-start(bf16[96,1024]{1,0:T(8,128)(2,1)S(1)} %get-tuple-element.100), channel_id=1, source_target_pairs={{0,0},{1,1},{2,2},{3,3},{4,16},{5,17},{6,18},{7,19},{16,4},{17,5},... | collective-permute-start | bytes 589832 | tf_op jit(solution)/shard_map/ppermute | solution.py:204
  103.8 15.3 %collective-permute-start.17 = (bf16[96,1024]{1,0:T(8,128)(2,1)S(1)}, bf16[96,1024]{1,0:T(8,128)(2,1)S(1)}, u32[]{:S(2)}, u32[]{:S(2)}) collective-permute-start(bf16[96,1024]{1,0:T(8,128)(2,1)S(1)} %get-tuple-element.98), channel_id=1, source_target_pairs={{0,1},{1,0},{2,3},{3,2},{4,17},{5,16},{6,19},{7,18},{16,5},{17,4},... | collective-permute-start | bytes 589832 | tf_op jit(solution)/shard_map/ppermute | solution.py:204
  105.0 15.2 %collective-permute-start.18 = (bf16[96,1024]{1,0:T(8,128)(2,1)S(1)}, bf16[96,1024]{1,0:T(8,128)(2,1)S(1)}, u32[]{:S(2)}, u32[]{:S(2)}) collective-permute-start(bf16[96,1024]{1,0:T(8,128)(2,1)S(1)} %get-tuple-element.97), channel_id=1, source_target_pairs={{0,2},{1,3},{2,0},{3,1},{4,18},{5,19},{6,16},{7,17},{16,6},{17,7},... | collective-permute-start | bytes 589832 | tf_op jit(solution)/shard_map/ppermute | solution.py:204
  105.0 15.2 %collective-permute-start.19 = (bf16[96,1024]{1,0:T(8,128)(2,1)S(1)}, bf16[96,1024]{1,0:T(8,128)(2,1)S(1)}, u32[]{:S(2)}, u32[]{:S(2)}) collective-permute-start(bf16[96,1024]{1,0:T(8,128)(2,1)S(1)} %get-tuple-element.67), channel_id=1, source_target_pairs={{0,3},{1,2},{2,1},{3,0},{4,19},{5,18},{6,17},{7,16},{16,7},{17,6},... | collective-permute-start | bytes 589832 | tf_op jit(solution)/shard_map/ppermute | solution.py:204
  116.6 17.1 %collective-permute-start.20 = (bf16[64,2560]{1,0:T(8,128)(2,1)S(1)}, bf16[64,2560]{1,0:T(8,128)(2,1)S(1)}, u32[]{:S(2)}, u32[]{:S(2)}) collective-permute-start(bf16[64,2560]{1,0:T(8,128)(2,1)S(1)} %get-tuple-element.69), channel_id=1, source_target_pairs={{0,1},{1,0},{2,3},{3,2},{4,5},{5,4},{6,7},{7,6},{8,9},{9,8},{10,11... | collective-permute-start | bytes 983048 | tf_op jit(solution)/shard_map/ppermute | solution.py:277
  117.2 17.7 %collective-permute-start.21 = (bf16[64,2560]{1,0:T(8,128)(2,1)S(1)}, bf16[64,2560]{1,0:T(8,128)(2,1)S(1)}, u32[]{:S(2)}, u32[]{:S(2)}) collective-permute-start(bf16[64,2560]{1,0:T(8,128)(2,1)S(1)} %get-tuple-element.72), channel_id=1, source_target_pairs={{0,2},{1,3},{2,0},{3,1},{4,6},{5,7},{6,4},{7,5},{8,10},{9,11},{10,... | collective-permute-start | bytes 983048 | tf_op jit(solution)/shard_map/ppermute | solution.py:277
  119.0 20.7 %collective-permute-start.22 = (bf16[64,2560]{1,0:T(8,128)(2,1)S(1)}, bf16[64,2560]{1,0:T(8,128)(2,1)S(1)}, u32[]{:S(2)}, u32[]{:S(2)}) collective-permute-start(bf16[64,2560]{1,0:T(8,128)(2,1)S(1)} %get-tuple-element.75), channel_id=1, source_target_pairs={{0,3},{1,2},{2,1},{3,0},{4,7},{5,6},{6,5},{7,4},{8,11},{9,10},{10,... | collective-permute-start | bytes 983048 | tf_op jit(solution)/shard_map/ppermute | solution.py:277
  131.3 16.2 %collective-permute-start.25 = (bf16[48,2560]{1,0:T(8,128)(2,1)S(1)}, bf16[48,2560]{1,0:T(8,128)(2,1)S(1)}, u32[]{:S(2)}, u32[]{:S(2)}) collective-permute-start(bf16[48,2560]{1,0:T(8,128)(2,1)S(1)} %get-tuple-element.78), channel_id=1, source_target_pairs={{0,1},{1,0},{2,3},{3,2},{4,5},{5,4},{6,7},{7,6},{8,9},{9,8},{10,11... | collective-permute-start | bytes 737288 | tf_op jit(solution)/shard_map/ppermute | solution.py:277
  131.9 15.6 %collective-permute-start.26 = (bf16[48,2560]{1,0:T(8,128)(2,1)S(1)}, bf16[48,2560]{1,0:T(8,128)(2,1)S(1)}, u32[]{:S(2)}, u32[]{:S(2)}) collective-permute-start(bf16[48,2560]{1,0:T(8,128)(2,1)S(1)} %get-tuple-element.79), channel_id=1, source_target_pairs={{0,2},{1,3},{2,0},{3,1},{4,6},{5,7},{6,4},{7,5},{8,10},{9,11},{10,... | collective-permute-start | bytes 737288 | tf_op jit(solution)/shard_map/ppermute | solution.py:277
  133.8 14.5 %collective-permute-start.27 = (bf16[48,2560]{1,0:T(8,128)(2,1)S(1)}, bf16[48,2560]{1,0:T(8,128)(2,1)S(1)}, u32[]{:S(2)}, u32[]{:S(2)}) collective-permute-start(bf16[48,2560]{1,0:T(8,128)(2,1)S(1)} %get-tuple-element.80), channel_id=1, source_target_pairs={{0,3},{1,2},{2,1},{3,0},{4,7},{5,6},{6,5},{7,4},{8,11},{9,10},{10,... | collective-permute-start | bytes 737288 | tf_op jit(solution)/shard_map/ppermute | solution.py:277
  134.9 23.2 %collective-permute-start.30 = (bf16[48,2560]{1,0:T(8,128)(2,1)S(1)}, bf16[48,2560]{1,0:T(8,128)(2,1)S(1)}, u32[]{:S(2)}, u32[]{:S(2)}) collective-permute-start(bf16[48,2560]{1,0:T(8,128)(2,1)S(1)} %get-tuple-element.82), channel_id=1, source_target_pairs={{0,1},{1,0},{2,3},{3,2},{4,5},{5,4},{6,7},{7,6},{8,9},{9,8},{10,11... | collective-permute-start | bytes 737288 | tf_op jit(solution)/shard_map/ppermute | solution.py:277
  139.7 18.4 %collective-permute-start.31 = (bf16[48,2560]{1,0:T(8,128)(2,1)S(1)}, bf16[48,2560]{1,0:T(8,128)(2,1)S(1)}, u32[]{:S(2)}, u32[]{:S(2)}) collective-permute-start(bf16[48,2560]{1,0:T(8,128)(2,1)S(1)} %get-tuple-element.83), channel_id=1, source_target_pairs={{0,2},{1,3},{2,0},{3,1},{4,6},{5,7},{6,4},{7,5},{8,10},{9,11},{10,... | collective-permute-start | bytes 737288 | tf_op jit(solution)/shard_map/ppermute | solution.py:277
  148.4 19.7 %collective-permute-start.28 = (bf16[48,2560]{1,0:T(8,128)(2,1)S(1)}, bf16[48,2560]{1,0:T(8,128)(2,1)S(1)}, u32[]{:S(2)}, u32[]{:S(2)}) collective-permute-start(bf16[48,2560]{1,0:T(8,128)(2,1)S(1)} %add_convert_fusion.5), channel_id=1, source_target_pairs={{0,0},{1,1},{2,2},{3,3},{4,16},{5,17},{6,18},{7,19},{16,4},{17,5},... | collective-permute-start | bytes 737288 | tf_op jit(solution)/shard_map/ppermute | solution.py:204
  158.2 15.0 %collective-permute-start.33 = (bf16[48,2560]{1,0:T(8,128)(2,1)S(1)}, bf16[48,2560]{1,0:T(8,128)(2,1)S(1)}, u32[]{:S(2)}, u32[]{:S(2)}) collective-permute-start(bf16[48,2560]{1,0:T(8,128)(2,1)S(1)} %add_convert_fusion.3), channel_id=1, source_target_pairs={{0,0},{1,1},{2,2},{3,3},{4,16},{5,17},{6,18},{7,19},{16,4},{17,5},... | collective-permute-start | bytes 737288 | tf_op jit(solution)/shard_map/ppermute | solution.py:204
  158.9 16.9 %collective-permute-start.24 = (bf16[64,2560]{1,0:T(8,128)(2,1)S(1)}, bf16[64,2560]{1,0:T(8,128)(2,1)S(1)}, u32[]{:S(2)}, u32[]{:S(2)}) collective-permute-start(bf16[64,2560]{1,0:T(8,128)(2,1)S(1)} %collective-permute-done.23), channel_id=1, source_target_pairs={{0,16},{1,17},{2,18},{3,19},{4,20},{5,21},{6,22},{7,23},{8,24},{9,... | collective-permute-start | bytes 983048 | tf_op jit(solution)/shard_map/ppermute | solution.py:284
  (19 other events, 266.4 us)

commit v5 on v4

--- a/solution.py
+++ b/solution.py
@@ -228,8 +228,8 @@
         part = jnp.concatenate([mine(key, step), mine(value, step)], axis=0)
         if step > 0:
             part, weight_parts[step - 1] = after(part, weight_parts[step - 1])
-        if step == half - 1:
-            part, weight_parts[step] = after(part, weight_parts[step])
+        if step == half - 2:
+            part, weight_parts[step + 1] = after(part, weight_parts[step + 1])
         pair_parts.append(send(part, step))
     own, pair_parts[0] = after(own, pair_parts[0])
     own_far, other_far = sibling(own), sibling(other)

time: 179 us -> 179 us (level)
  starting transfers between devices: 98.6 us -> 89.6 us
  waiting for transfers between devices: 50.1 us -> 59.1 us
    ppermute x3, starting transfers between devices: 36.1 us -> 27 us  [sibling(): return lax.ppermute(array, 'branch', [(0, 1), (1, 0)])]
    ppermute x19, waiting for transfers between devices: 28.7 us -> 36 us  [send(): return lax.ppermute(array, pair, crossing(step))]
    ppermute x3, starting transfers between devices: 16.6 us -> 14.6 us  [per_device(): lax.ppermute(projected, 'branch', [(0, 1)])]
  transfers between devices with their start and end apart: 35 -> 35, of which waited for: 9 -> 8; matrix products, arithmetic and copies ran while one was open for 3% -> 3% of each run, Pallas kernels for 11% -> 11%
where the time goes in v5:
time: 179 us; the launch traced here: 178 us
  starting transfers between devices  89.6 us (50%)
  waiting for transfers between devices  59.1 us (33%)
  Pallas kernels  19.9 us (11%)
  other arithmetic  4.48 us (3%)
  local copies, waits for them, and re-layouts  3.9 us (2%)
    ppermute x19, starting transfers between devices, send(): return lax.ppermute(array, pair, crossing(step))  38.5 us
    ppermute x19, waiting for transfers between devices, send(): return lax.ppermute(array, pair, crossing(step))  36 us
    ppermute x3, starting transfers between devices, sibling(): return lax.ppermute(array, 'branch', [(0, 1), (1, 0)])  27 us
    ppermute x9, waiting for transfers between devices, per_device(): parts.append(lax.ppermute(part, 'seq', swap))  22.5 us
    pallas_call x2, Pallas kernels, attend_project(): pl.pallas_call(body, grid_spec=pltpu.PrefetchScalarGridSpec(num_scalar_pr...  19.8 us
    ppermute x3, starting transfers between devices, per_device(): lax.ppermute(projected, 'branch', [(0, 1)])  14.6 us
    ppermute x9, starting transfers between devices, per_device(): parts.append(lax.ppermute(part, 'seq', swap))  7.86 us
  transfers between devices with their start and end apart: 35, of which 8 were waited for; matrix products, arithmetic and copies ran while one was open for 3% of the time, Pallas kernels for 11%

profile of v5, /device:TPU:0, one launch (start us, length us, event | category | flops | bytes accessed | tf_op | source)
XLA Modules:
  0.0 178.0 jit_solution(7619165547700737704)
XLA Ops:
  0.0 2.4 %dynamic-slice_bitcast_fusion.11 = (bf16[320,512]{1,0:T(8,128)(2,1)}, bf16[320,512]{1,0:T(8,128)(2,1)}, bf16[320,512]{1,0:T(8,128)(2,1)}, bf16[320,512]{1,0:T(8,128)(2,1)S(1)}) fusion(bf16[1,4096,320]{1,2,0:T(8,128)(2,1)} %param.15, s32[]{:T(128)S(6)} %select_n.94, s32[]{:T(128)S(6)} %select_n.95, s32[]{:T(128)S(6)} %select_n.97, s32[]{:T(128)S(6)} %select_n.96), kind=kLoop, calls=%fused_computation.27 | loop fusion | bytes 2621456 | tf_op jit(solution)/shard_map/dynamic_slice | solution.py:220
  2.4 2.9 %collective-permute-start.2 = (bf16[320,512]{1,0:T(8,128)(2,1)}, bf16[320,512]{1,0:T(8,128)(2,1)S(1)}, u32[]{:S(2)}, u32[]{:S(2)}) collective-permute-start(bf16[320,512]{1,0:T(8,128)(2,1)} %get-tuple-element.86), channel_id=1, source_target_pairs={{0,1},{1,0},{2,3},{3,2},{4,17},{5,16},{6,19},{7,18},{16,5},{17,4},... | collective-permute-start | bytes 983048 | tf_op jit(solution)/shard_map/ppermute | solution.py:204
  6.9 3.9 %collective-permute-start.1 = (bf16[320,512]{1,0:T(8,128)(2,1)}, bf16[320,512]{1,0:T(8,128)(2,1)}, u32[]{:S(2)}, u32[]{:S(2)}) collective-permute-start(bf16[320,512]{1,0:T(8,128)(2,1)} %get-tuple-element.85), channel_id=1, source_target_pairs={{0,0},{1,1},{2,2},{3,3},{4,16},{5,17},{6,18},{7,19},{16,4},{17,5},... | collective-permute-start | bytes 983048 | tf_op jit(solution)/shard_map/ppermute | solution.py:204
  11.9 6.6 %collective-permute-done.2 = bf16[320,512]{1,0:T(8,128)(2,1)S(1)} collective-permute-done((bf16[320,512]{1,0:T(8,128)(2,1)}, bf16[320,512]{1,0:T(8,128)(2,1)S(1)}, u32[]{:S(2)}, u32[]{:S(2)}) %collective-permute-start.2) | collective-permute-done | bytes 327712 | tf_op jit(solution)/shard_map/ppermute | solution.py:204
  18.5 4.7 %collective-permute-start.9 = (bf16[320,1024]{1,0:T(8,128)(2,1)S(1)}, bf16[320,1024]{1,0:T(8,128)(2,1)S(1)}, u32[]{:S(2)}, u32[]{:S(2)}) collective-permute-start(bf16[320,1024]{1,0:T(8,128)(2,1)S(1)} %pad_maximum_fusion.3), channel_id=1, source_target_pairs={{0,2},{1,3},{2,0},{3,1},{4,18},{5,19},{6,16},{7,17},{16,6},{17,7},... | collective-permute-start | bytes 1966088 | tf_op jit(solution)/shard_map/ppermute | solution.py:204
  23.3 1.6 collective-permute-start.7
  25.8 2.5 %pad_maximum_fusion.refs_6_ = bf16[4,320,512]{2,1,0:T(8,128)(2,1)} fusion(bf16[1,320,512]{2,1,0:T(8,128)(2,1)} %bitcast.17, bf16[1,320,512]{2,1,0:T(8,128)(2,1)} %bitcast.14, bf16[1,320,512]{2,1,0:T(8,128)(2,1)S(1)} %bitcast.68, bf16[1,320,512]{2,1,0:T(8,128)(2,1)} %bitcast.8), kind=kLoop, calls=%fused_computation | loop fusion | flops 1966080 | bytes 2621440 | tf_op jit(solution)/shard_map/stack | solution.py:223
  30.5 8.4 %collective-permute-done.9.refs_2_ = bf16[320,1024]{1,0:T(8,128)(2,1)S(1)} collective-permute-done((bf16[320,1024]{1,0:T(8,128)(2,1)S(1)}, bf16[320,1024]{1,0:T(8,128)(2,1)S(1)}, u32[]{:S(2)}, u32[]{:S(2)}) %collective-permute-start.9) | collective-permute-done | bytes 655392 | tf_op jit(solution)/shard_map/ppermute | solution.py:204
  38.9 20.9 %collective-permute-done.13.refs_3_ = bf16[320,1024]{1,0:T(8,128)(2,1)S(1)} collective-permute-done((bf16[320,1024]{1,0:T(8,128)(2,1)S(1)}, bf16[320,1024]{1,0:T(8,128)(2,1)S(1)}, u32[]{:S(2)}, u32[]{:S(2)}) %collective-permute-start.13) | collective-permute-done | bytes 655392 | tf_op jit(solution)/shard_map/ppermute | solution.py:204
  60.1 26.5 %collective-permute-start.16 = (bf16[4,320,1024]{2,1,0:T(8,128)(2,1)S(1)}, bf16[4,320,1024]{2,1,0:T(8,128)(2,1)}, u32[]{:S(2)}, u32[]{:S(2)}) collective-permute-start(bf16[4,320,1024]{2,1,0:T(8,128)(2,1)S(1)} %shard_map.82.refs_4_), channel_id=1, source_target_pairs={{0,16},{16,0},{1,17},{17,1},{2,18},{18,2},{3,19},{19,3},{4,20},{20... | collective-permute-start | bytes 7864328 | tf_op jit(solution)/shard_map/ppermute | solution.py:207
  89.4 8.5 %collective-permute-start.12 = (bf16[64,1024]{1,0:T(8,128)(2,1)}, bf16[64,1024]{1,0:T(8,128)(2,1)S(1)}, u32[]{:S(2)}, u32[]{:S(2)}) collective-permute-start(bf16[64,1024]{1,0:T(8,128)(2,1)} %get-tuple-element.55), channel_id=1, source_target_pairs={{0,3},{1,2},{2,1},{3,0},{4,19},{5,18},{6,17},{7,16},{16,7},{17,6},... | collective-permute-start | bytes 393224 | tf_op jit(solution)/shard_map/ppermute | solution.py:204
  98.5 4.3 %collective-permute-start.11 = (bf16[64,1024]{1,0:T(8,128)(2,1)S(1)}, bf16[64,1024]{1,0:T(8,128)(2,1)S(1)}, u32[]{:S(2)}, u32[]{:S(2)}) collective-permute-start(bf16[64,1024]{1,0:T(8,128)(2,1)S(1)} %get-tuple-element.53), channel_id=1, source_target_pairs={{0,2},{1,3},{2,0},{3,1},{4,18},{5,19},{6,16},{7,17},{16,6},{17,7},... | collective-permute-start | bytes 393224 | tf_op jit(solution)/shard_map/ppermute | solution.py:204
  105.3 2.7 %collective-permute-start.19 = (bf16[96,1024]{1,0:T(8,128)(2,1)S(1)}, bf16[96,1024]{1,0:T(8,128)(2,1)S(1)}, u32[]{:S(2)}, u32[]{:S(2)}) collective-permute-start(bf16[96,1024]{1,0:T(8,128)(2,1)S(1)} %get-tuple-element.67), channel_id=1, source_target_pairs={{0,3},{1,2},{2,1},{3,0},{4,19},{5,18},{6,17},{7,16},{16,7},{17,6},... | collective-permute-start | bytes 589832 | tf_op jit(solution)/shard_map/ppermute | solution.py:204
  108.1 8.6 %shard_map.83 = (f32[64,2560]{1,0:T(8,128)S(1)}, bf16[64,2560]{1,0:T(8,128)(2,1)S(1)}, bf16[64,2560]{1,0:T(8,128)(2,1)S(1)}, bf16[64,2560]{1,0:T(8,128)(2,1)S(1)}) custom-call(s32[3]{0:T(128)S(1)} %pad_add_fusion.where, bf16[64,1024]{1,0:T(8,128)(2,1)S(1)} %collective-permute-done.6.refs_0_, bf16[64,1024]{1,0:T(8,128)(2,1)S(1)} %collective-permute-done.8.refs_1_, ...), custom_call_target="tpu_custom_call" | custom-call | flops 2684354560 | bytes 10485760 | tf_op jit(solution)/shard_map/pallas_call | solution.py:126
  117.5 1.8 collective-permute-start.21
  120.3 11.1 %shard_map.84 = (f32[48,2560]{1,0:T(8,128)S(1)}, bf16[48,2560]{1,0:T(8,128)(2,1)S(1)}, bf16[48,2560]{1,0:T(8,128)(2,1)S(1)}, bf16[48,2560]{1,0:T(8,128)(2,1)S(1)...) custom-call(s32[3]{0:T(128)S(1)} %pad_add_fusion.where, ...), custom_call_target="tpu_custom_call" | custom-call | flops 4026531840 | bytes 10485760 | tf_op jit(solution)/shard_map/pallas_call | solution.py:126
  132.2 1.8 collective-permute-start.26
  135.7 4.2 %collective-permute-done.22 = bf16[64,2560]{1,0:T(8,128)(2,1)S(1)} collective-permute-done((bf16[64,2560]{1,0:T(8,128)(2,1)S(1)}, bf16[64,2560]{1,0:T(8,128)(2,1)S(1)}, u32[]{:S(2)}, u32[]{:S(2)}) %collective-permute-start.22) | collective-permute-done | bytes 327712 | tf_op jit(solution)/shard_map/ppermute | solution.py:277
  140.1 7.6 %collective-permute-done.25 = bf16[48,2560]{1,0:T(8,128)(2,1)S(1)} collective-permute-done((bf16[48,2560]{1,0:T(8,128)(2,1)S(1)}, bf16[48,2560]{1,0:T(8,128)(2,1)S(1)}, u32[]{:S(2)}, u32[]{:S(2)}) %collective-permute-start.25) | collective-permute-done | bytes 245792 | tf_op jit(solution)/shard_map/ppermute | solution.py:277
  149.4 8.5 %collective-permute-done.30 = bf16[48,2560]{1,0:T(8,128)(2,1)S(1)} collective-permute-done((bf16[48,2560]{1,0:T(8,128)(2,1)S(1)}, bf16[48,2560]{1,0:T(8,128)(2,1)S(1)}, u32[]{:S(2)}, u32[]{:S(2)}) %collective-permute-start.30) | collective-permute-done | bytes 245792 | tf_op jit(solution)/shard_map/ppermute | solution.py:277
  157.9 2.2 %collective-permute-done.32 = bf16[48,2560]{1,0:T(8,128)(2,1)S(1)} collective-permute-done((bf16[48,2560]{1,0:T(8,128)(2,1)S(1)}, bf16[48,2560]{1,0:T(8,128)(2,1)S(1)}, u32[]{:S(2)}, u32[]{:S(2)}) %collective-permute-start.32) | collective-permute-done | bytes 245792 | tf_op jit(solution)/shard_map/ppermute | solution.py:277
  160.9 7.0 %collective-permute-start.24 = (bf16[64,2560]{1,0:T(8,128)(2,1)S(1)}, bf16[64,2560]{1,0:T(8,128)(2,1)S(1)}, u32[]{:S(2)}, u32[]{:S(2)}) collective-permute-start(bf16[64,2560]{1,0:T(8,128)(2,1)S(1)} %collective-permute-done.23), channel_id=1, source_target_pairs={{0,16},{1,17},{2,18},{3,19},{4,20},{5,21},{6,22},{7,23},{8,24},{9,... | collective-permute-start | bytes 983048 | tf_op jit(solution)/shard_map/ppermute | solution.py:284
  168.1 5.0 %collective-permute-start.29 = (bf16[48,2560]{1,0:T(8,128)(2,1)S(1)}, bf16[48,2560]{1,0:T(8,128)(2,1)S(1)}, u32[]{:S(2)}, u32[]{:S(2)}) collective-permute-start(bf16[48,2560]{1,0:T(8,128)(2,1)S(1)} %collective-permute-done.28), channel_id=1, source_target_pairs={{0,16},{1,17},{2,18},{3,19},{4,20},{5,21},{6,22},{7,23},{8,24},{9,... | collective-permute-start | bytes 737288 | tf_op jit(solution)/shard_map/ppermute | solution.py:284
  173.2 2.6 %collective-permute-start.34 = (bf16[48,2560]{1,0:T(8,128)(2,1)S(1)}, bf16[48,2560]{1,0:T(8,128)(2,1)S(1)}, u32[]{:S(2)}, u32[]{:S(2)}) collective-permute-start(bf16[48,2560]{1,0:T(8,128)(2,1)S(1)} %collective-permute-done.33), channel_id=1, source_target_pairs={{0,16},{1,17},{2,18},{3,19},{4,20},{5,21},{6,22},{7,23},{8,24},{9,... | collective-permute-start | bytes 737288 | tf_op jit(solution)/shard_map/ppermute | solution.py:284
  (86 shorter events, 20.6 us)
Async XLA Ops:
  2.4 16.1 %collective-permute-start.2 = (bf16[320,512]{1,0:T(8,128)(2,1)}, bf16[320,512]{1,0:T(8,128)(2,1)S(1)}, u32[]{:S(2)}, u32[]{:S(2)}) collective-permute-start(bf16[320,512]{1,0:T(8,128)(2,1)} %get-tuple-element.86), channel_id=1, source_target_pairs={{0,1},{1,0},{2,3},{3,2},{4,17},{5,16},{6,19},{7,18},{16,5},{17,4},... | collective-permute-start | bytes 983048 | tf_op jit(solution)/shard_map/ppermute | solution.py:204
  6.9 18.0 %collective-permute-start.3 = (bf16[320,512]{1,0:T(8,128)(2,1)S(1)}, bf16[320,512]{1,0:T(8,128)(2,1)}, u32[]{:S(2)}, u32[]{:S(2)}) collective-permute-start(bf16[320,512]{1,0:T(8,128)(2,1)S(1)} %get-tuple-element.88), channel_id=1, source_target_pairs={{0,2},{1,3},{2,0},{3,1},{4,18},{5,19},{6,16},{7,17},{16,6},{17,7},... | collective-permute-start | bytes 983048 | tf_op jit(solution)/shard_map/ppermute | solution.py:204
  6.9 16.3 %collective-permute-start.1 = (bf16[320,512]{1,0:T(8,128)(2,1)}, bf16[320,512]{1,0:T(8,128)(2,1)}, u32[]{:S(2)}, u32[]{:S(2)}) collective-permute-start(bf16[320,512]{1,0:T(8,128)(2,1)} %get-tuple-element.85), channel_id=1, source_target_pairs={{0,0},{1,1},{2,2},{3,3},{4,16},{5,17},{6,18},{7,19},{16,4},{17,5},... | collective-permute-start | bytes 983048 | tf_op jit(solution)/shard_map/ppermute | solution.py:204
  11.1 19.4 %collective-permute-start.5 = (bf16[320,1024]{1,0:T(8,128)(2,1)S(1)}, bf16[320,1024]{1,0:T(8,128)(2,1)S(1)}, u32[]{:S(2)}, u32[]{:S(2)}) collective-permute-start(bf16[320,1024]{1,0:T(8,128)(2,1)S(1)} %pad_maximum_fusion.1), channel_id=1, source_target_pairs={{0,0},{1,1},{2,2},{3,3},{4,16},{5,17},{6,18},{7,19},{16,4},{17,5},... | collective-permute-start | bytes 1966088 | tf_op jit(solution)/shard_map/ppermute | solution.py:204
  18.5 20.4 %collective-permute-start.9 = (bf16[320,1024]{1,0:T(8,128)(2,1)S(1)}, bf16[320,1024]{1,0:T(8,128)(2,1)S(1)}, u32[]{:S(2)}, u32[]{:S(2)}) collective-permute-start(bf16[320,1024]{1,0:T(8,128)(2,1)S(1)} %pad_maximum_fusion.3), channel_id=1, source_target_pairs={{0,2},{1,3},{2,0},{3,1},{4,18},{5,19},{6,16},{7,17},{16,6},{17,7},... | collective-permute-start | bytes 1966088 | tf_op jit(solution)/shard_map/ppermute | solution.py:204
  23.3 15.7 %collective-permute-start.7 = (bf16[320,1024]{1,0:T(8,128)(2,1)S(1)}, bf16[320,1024]{1,0:T(8,128)(2,1)S(1)}, u32[]{:S(2)}, u32[]{:S(2)}) collective-permute-start(bf16[320,1024]{1,0:T(8,128)(2,1)S(1)} %pad_maximum_fusion.2), channel_id=1, source_target_pairs={{0,1},{1,0},{2,3},{3,2},{4,17},{5,16},{6,19},{7,18},{16,5},{17,4},... | collective-permute-start | bytes 1966088 | tf_op jit(solution)/shard_map/ppermute | solution.py:204
  24.9 35.0 %collective-permute-start.13 = (bf16[320,1024]{1,0:T(8,128)(2,1)S(1)}, bf16[320,1024]{1,0:T(8,128)(2,1)S(1)}, u32[]{:S(2)}, u32[]{:S(2)}) collective-permute-start(bf16[320,1024]{1,0:T(8,128)(2,1)S(1)} %pad_maximum_fusion.4), channel_id=1, source_target_pairs={{0,3},{1,2},{2,1},{3,0},{4,19},{5,18},{6,17},{7,16},{16,7},{17,6},... | collective-permute-start | bytes 1966088 | tf_op jit(solution)/shard_map/ppermute | solution.py:204
  28.2 58.4 %collective-permute-start.14 = (bf16[4,320,512]{2,1,0:T(8,128)(2,1)}, bf16[4,320,512]{2,1,0:T(8,128)(2,1)}, u32[]{:S(2)}, u32[]{:S(2)}) collective-permute-start(bf16[4,320,512]{2,1,0:T(8,128)(2,1)} %pad_maximum_fusion.refs_6_), channel_id=1, source_target_pairs={{0,8},{8,0},{1,9},{9,1},{2,10},{10,2},{3,11},{11,3},{4,12},{12,4},... | collective-permute-start | bytes 3932168 | tf_op jit(solution)/shard_map/ppermute | solution.py:224
  60.1 42.9 %collective-permute-start.16 = (bf16[4,320,1024]{2,1,0:T(8,128)(2,1)S(1)}, bf16[4,320,1024]{2,1,0:T(8,128)(2,1)}, u32[]{:S(2)}, u32[]{:S(2)}) collective-permute-start(bf16[4,320,1024]{2,1,0:T(8,128)(2,1)S(1)} %shard_map.82.refs_4_), channel_id=1, source_target_pairs={{0,16},{16,0},{1,17},{17,1},{2,18},{18,2},{3,19},{19,3},{4,20},{20... | collective-permute-start | bytes 7864328 | tf_op jit(solution)/shard_map/ppermute | solution.py:207
  87.8 15.9 %collective-permute-start.6 = (bf16[64,1024]{1,0:T(8,128)(2,1)}, bf16[64,1024]{1,0:T(8,128)(2,1)S(1)}, u32[]{:S(2)}, u32[]{:S(2)}) collective-permute-start(bf16[64,1024]{1,0:T(8,128)(2,1)} %get-tuple-element.46), channel_id=1, source_target_pairs={{0,0},{1,1},{2,2},{3,3},{4,16},{5,17},{6,18},{7,19},{16,4},{17,5},... | collective-permute-start | bytes 393224 | tf_op jit(solution)/shard_map/ppermute | solution.py:204
  89.4 15.9 %collective-permute-start.12 = (bf16[64,1024]{1,0:T(8,128)(2,1)}, bf16[64,1024]{1,0:T(8,128)(2,1)S(1)}, u32[]{:S(2)}, u32[]{:S(2)}) collective-permute-start(bf16[64,1024]{1,0:T(8,128)(2,1)} %get-tuple-element.55), channel_id=1, source_target_pairs={{0,3},{1,2},{2,1},{3,0},{4,19},{5,18},{6,17},{7,16},{16,7},{17,6},... | collective-permute-start | bytes 393224 | tf_op jit(solution)/shard_map/ppermute | solution.py:204
  103.8 15.5 %collective-permute-start.17 = (bf16[96,1024]{1,0:T(8,128)(2,1)S(1)}, bf16[96,1024]{1,0:T(8,128)(2,1)S(1)}, u32[]{:S(2)}, u32[]{:S(2)}) collective-permute-start(bf16[96,1024]{1,0:T(8,128)(2,1)S(1)} %get-tuple-element.98), channel_id=1, source_target_pairs={{0,1},{1,0},{2,3},{3,2},{4,17},{5,16},{6,19},{7,18},{16,5},{17,4},... | collective-permute-start | bytes 589832 | tf_op jit(solution)/shard_map/ppermute | solution.py:204
  105.3 14.9 %collective-permute-start.18 = (bf16[96,1024]{1,0:T(8,128)(2,1)S(1)}, bf16[96,1024]{1,0:T(8,128)(2,1)S(1)}, u32[]{:S(2)}, u32[]{:S(2)}) collective-permute-start(bf16[96,1024]{1,0:T(8,128)(2,1)S(1)} %get-tuple-element.97), channel_id=1, source_target_pairs={{0,2},{1,3},{2,0},{3,1},{4,18},{5,19},{6,16},{7,17},{16,6},{17,7},... | collective-permute-start | bytes 589832 | tf_op jit(solution)/shard_map/ppermute | solution.py:204
  105.3 14.9 %collective-permute-start.19 = (bf16[96,1024]{1,0:T(8,128)(2,1)S(1)}, bf16[96,1024]{1,0:T(8,128)(2,1)S(1)}, u32[]{:S(2)}, u32[]{:S(2)}) collective-permute-start(bf16[96,1024]{1,0:T(8,128)(2,1)S(1)} %get-tuple-element.67), channel_id=1, source_target_pairs={{0,3},{1,2},{2,1},{3,0},{4,19},{5,18},{6,17},{7,16},{16,7},{17,6},... | collective-permute-start | bytes 589832 | tf_op jit(solution)/shard_map/ppermute | solution.py:204
  116.7 17.3 %collective-permute-start.20 = (bf16[64,2560]{1,0:T(8,128)(2,1)S(1)}, bf16[64,2560]{1,0:T(8,128)(2,1)S(1)}, u32[]{:S(2)}, u32[]{:S(2)}) collective-permute-start(bf16[64,2560]{1,0:T(8,128)(2,1)S(1)} %get-tuple-element.69), channel_id=1, source_target_pairs={{0,1},{1,0},{2,3},{3,2},{4,5},{5,4},{6,7},{7,6},{8,9},{9,8},{10,11... | collective-permute-start | bytes 983048 | tf_op jit(solution)/shard_map/ppermute | solution.py:277
  117.5 17.5 %collective-permute-start.21 = (bf16[64,2560]{1,0:T(8,128)(2,1)S(1)}, bf16[64,2560]{1,0:T(8,128)(2,1)S(1)}, u32[]{:S(2)}, u32[]{:S(2)}) collective-permute-start(bf16[64,2560]{1,0:T(8,128)(2,1)S(1)} %get-tuple-element.72), channel_id=1, source_target_pairs={{0,2},{1,3},{2,0},{3,1},{4,6},{5,7},{6,4},{7,5},{8,10},{9,11},{10,... | collective-permute-start | bytes 983048 | tf_op jit(solution)/shard_map/ppermute | solution.py:277
  119.3 20.6 %collective-permute-start.22 = (bf16[64,2560]{1,0:T(8,128)(2,1)S(1)}, bf16[64,2560]{1,0:T(8,128)(2,1)S(1)}, u32[]{:S(2)}, u32[]{:S(2)}) collective-permute-start(bf16[64,2560]{1,0:T(8,128)(2,1)S(1)} %get-tuple-element.75), channel_id=1, source_target_pairs={{0,3},{1,2},{2,1},{3,0},{4,7},{5,6},{6,5},{7,4},{8,11},{9,10},{10,... | collective-permute-start | bytes 983048 | tf_op jit(solution)/shard_map/ppermute | solution.py:277
  131.4 16.3 %collective-permute-start.25 = (bf16[48,2560]{1,0:T(8,128)(2,1)S(1)}, bf16[48,2560]{1,0:T(8,128)(2,1)S(1)}, u32[]{:S(2)}, u32[]{:S(2)}) collective-permute-start(bf16[48,2560]{1,0:T(8,128)(2,1)S(1)} %get-tuple-element.78), channel_id=1, source_target_pairs={{0,1},{1,0},{2,3},{3,2},{4,5},{5,4},{6,7},{7,6},{8,9},{9,8},{10,11... | collective-permute-start | bytes 737288 | tf_op jit(solution)/shard_map/ppermute | solution.py:277
  132.2 15.5 %collective-permute-start.26 = (bf16[48,2560]{1,0:T(8,128)(2,1)S(1)}, bf16[48,2560]{1,0:T(8,128)(2,1)S(1)}, u32[]{:S(2)}, u32[]{:S(2)}) collective-permute-start(bf16[48,2560]{1,0:T(8,128)(2,1)S(1)} %get-tuple-element.79), channel_id=1, source_target_pairs={{0,2},{1,3},{2,0},{3,1},{4,6},{5,7},{6,4},{7,5},{8,10},{9,11},{10,... | collective-permute-start | bytes 737288 | tf_op jit(solution)/shard_map/ppermute | solution.py:277
  134.0 14.4 %collective-permute-start.27 = (bf16[48,2560]{1,0:T(8,128)(2,1)S(1)}, bf16[48,2560]{1,0:T(8,128)(2,1)S(1)}, u32[]{:S(2)}, u32[]{:S(2)}) collective-permute-start(bf16[48,2560]{1,0:T(8,128)(2,1)S(1)} %get-tuple-element.80), channel_id=1, source_target_pairs={{0,3},{1,2},{2,1},{3,0},{4,7},{5,6},{6,5},{7,4},{8,11},{9,10},{10,... | collective-permute-start | bytes 737288 | tf_op jit(solution)/shard_map/ppermute | solution.py:277
  135.0 22.9 %collective-permute-start.30 = (bf16[48,2560]{1,0:T(8,128)(2,1)S(1)}, bf16[48,2560]{1,0:T(8,128)(2,1)S(1)}, u32[]{:S(2)}, u32[]{:S(2)}) collective-permute-start(bf16[48,2560]{1,0:T(8,128)(2,1)S(1)} %get-tuple-element.82), channel_id=1, source_target_pairs={{0,1},{1,0},{2,3},{3,2},{4,5},{5,4},{6,7},{7,6},{8,9},{9,8},{10,11... | collective-permute-start | bytes 737288 | tf_op jit(solution)/shard_map/ppermute | solution.py:277
  139.9 17.9 %collective-permute-start.31 = (bf16[48,2560]{1,0:T(8,128)(2,1)S(1)}, bf16[48,2560]{1,0:T(8,128)(2,1)S(1)}, u32[]{:S(2)}, u32[]{:S(2)}) collective-permute-start(bf16[48,2560]{1,0:T(8,128)(2,1)S(1)} %get-tuple-element.83), channel_id=1, source_target_pairs={{0,2},{1,3},{2,0},{3,1},{4,6},{5,7},{6,4},{7,5},{8,10},{9,11},{10,... | collective-permute-start | bytes 737288 | tf_op jit(solution)/shard_map/ppermute | solution.py:277
  148.6 19.5 %collective-permute-start.28 = (bf16[48,2560]{1,0:T(8,128)(2,1)S(1)}, bf16[48,2560]{1,0:T(8,128)(2,1)S(1)}, u32[]{:S(2)}, u32[]{:S(2)}) collective-permute-start(bf16[48,2560]{1,0:T(8,128)(2,1)S(1)} %add_convert_fusion.5), channel_id=1, source_target_pairs={{0,0},{1,1},{2,2},{3,3},{4,16},{5,17},{6,18},{7,19},{16,4},{17,5},... | collective-permute-start | bytes 737288 | tf_op jit(solution)/shard_map/ppermute | solution.py:204
  160.9 14.9 %collective-permute-start.24 = (bf16[64,2560]{1,0:T(8,128)(2,1)S(1)}, bf16[64,2560]{1,0:T(8,128)(2,1)S(1)}, u32[]{:S(2)}, u32[]{:S(2)}) collective-permute-start(bf16[64,2560]{1,0:T(8,128)(2,1)S(1)} %collective-permute-done.23), channel_id=1, source_target_pairs={{0,16},{1,17},{2,18},{3,19},{4,20},{5,21},{6,22},{7,23},{8,24},{9,... | collective-permute-start | bytes 983048 | tf_op jit(solution)/shard_map/ppermute | solution.py:284
  (19 other events, 261.0 us)
